TPU v7x, 128 devices: a whole 4x4x4 slice. The times are simulated.
128 devices in a mesh: ctx: 32 (over x_hi, y, z), fsdp: 4 (over x_lo, core).
Axes of the slice: x: 4 (x_hi: 2, x_lo: 2; x = x_hi * 2 + x_lo), y: 4, z: 4, core: 2. Of those that a mesh axis runs over, the one named last changes fastest.
Arguments:
- hidden_in: bfloat16 [4, 4096, 1024], P('fsdp', 'ctx'), may hold values from -6 to 6
- segment_ids: int32 [4, 4096], P('fsdp', 'ctx'), may hold values from 0 to 514, as said below
- block_order: int32 [4, 64], P('fsdp'), may hold values from 0 to 63, as said below
- expert_ids: int32 [4, 4096, 8], P('fsdp', 'ctx'), may hold values from 0 to 31, all different within a row
- pair_order: int32 [4, 32, 1024], P('fsdp', 'ctx'), may hold values from 0 to 1023, each once within a row
- attn_norm: bfloat16 [1024], P(('ctx', 'fsdp')), may hold values from 0.5 to 1.5
- w_query: bfloat16 [1024, 1024], P(('ctx', 'fsdp')), may hold values from -0.1875 to 0.1875
- w_key: bfloat16 [1024, 512], P(('ctx', 'fsdp')), may hold values from -0.1875 to 0.1875
- w_value: bfloat16 [1024, 512], P(('ctx', 'fsdp')), may hold values from -0.1875 to 0.1875
- query_norm: bfloat16 [1024], P(('ctx', 'fsdp')), may hold values from 0.5 to 1.5
- key_norm: bfloat16 [512], P(('ctx', 'fsdp')), may hold values from 0.5 to 1.5
- w_out: bfloat16 [1024, 1024], P(('ctx', 'fsdp')), may hold values from -0.75 to 0.75
- ffn_norm: bfloat16 [1024], P(('ctx', 'fsdp')), may hold values from 0.5 to 1.5
- w_router: bfloat16 [1024, 32], P(('ctx', 'fsdp')), may hold values from -0.09375 to 0.09375
- w_gate: bfloat16 [32, 1024, 512], P('ctx', 'fsdp'), may hold values from -0.1875 to 0.1875
- w_up: bfloat16 [32, 1024, 512], P('ctx', 'fsdp'), may hold values from -0.1875 to 0.1875
- w_down: bfloat16 [32, 512, 1024], P('ctx', 'fsdp'), may hold values from -0.75 to 0.75
- cotangent: bfloat16 [4, 4096, 1024], P('fsdp', 'ctx'), may hold values from -6 to 6
Outputs:
- layer_out: bfloat16 [4, 4096, 1024], P('fsdp', 'ctx')
- input_grad: float32 [4, 4096, 1024], P('fsdp', 'ctx')
- grad_attn_norm: float32 [1024], P(('ctx', 'fsdp'))
- grad_query: float32 [1024, 1024], P(('ctx', 'fsdp'))
- grad_key: float32 [1024, 512], P(('ctx', 'fsdp'))
- grad_value: float32 [1024, 512], P(('ctx', 'fsdp'))
- grad_query_norm: float32 [1024], P(('ctx', 'fsdp'))
- grad_key_norm: float32 [512], P(('ctx', 'fsdp'))
- grad_out: float32 [1024, 1024], P(('ctx', 'fsdp'))
- grad_ffn_norm: float32 [1024], P(('ctx', 'fsdp'))
- grad_router: float32 [1024, 32], P(('ctx', 'fsdp'))
- grad_gate: float32 [32, 1024, 512], P('ctx', 'fsdp')
- grad_up: float32 [32, 1024, 512], P('ctx', 'fsdp')
- grad_down: float32 [32, 512, 1024], P('ctx', 'fsdp')
Inputs may be any that keep to these rules, and one draw needn't show every extreme that they name: `block_order`: for each sequence, entries 2 c and 2 c + 1 are a half-block b of the first half and 2 * 32 - 1 - b; each half-block appears once. `segment_ids`: in sequence-position order the ids of a sequence never fall; document 0 holds more than the first half of the sequence; the last document of each sequence has the largest id. `expert_ids`: each token names 8 different experts. `pair_order`: in each routing group the 1024 pairs, token-major, hold each priority once.
All inputs are finite; a program needn't handle non-finite values.
Results may differ from a plain program's by a relative error of at most 0.04.
Values may be sent and summed in bfloat16 or wider, within the bound.
No kernel may reach another device: no remote copies, remote signals or barrier semaphores. Data moves between devices by JAX's collectives and lax.ppermute only.
A program may use at most 192 MiB of HBM per device.

v0:
```python
import jax
import jax.numpy as jnp
from jax import lax
from jax.experimental import pallas as pl
from jax.experimental.pallas import tpu as pltpu
from jax.sharding import PartitionSpec as P

D = 1024
HEADS = 16
KVH = 8
HD = 64
EXPERTS = 32
TOPK = 8
TOK = 128
CAP = 32
N_CTX = 32
EPSILON = 1e-05
THETA = 10000.0
BF = jnp.bfloat16
F32 = jnp.float32

PARTS = 2
PART_HEADS = KVH // PARTS
COLS = PART_HEADS * 256
FEATURES = PART_HEADS * 128
ROWS = PARTS * TOK
QUARTERS = 4
PACK = TOK + TOK // QUARTERS
KEYS = N_CTX * TOK
QUERIES = KEYS // QUARTERS
KEY_TILE = 512
TOK_TILE = 128
TILES = QUERIES // TOK_TILE


def dot(a, b, dims=((1,), (0,))):
    return lax.dot_general(a, b, (dims, ((), ())), preferred_element_type=F32)


def swap(array, j):
    return lax.ppermute(array, "fsdp", [(i, i ^ j) for i in range(4)]) if j else array


def swapped(pieces):
    return [swap(piece, j) for j, piece in enumerate(pieces)]


def sum_parts(value):
    step = 1
    while step < PARTS:
        value = value + swap(jnp.stack([value[:, j ^ step] for j in range(PARTS)], 1), step)
        step *= 2
    return value


def exchange(array, axis):
    return lax.all_to_all(array, axis, split_axis=0, concat_axis=0, tiled=True)


def lanes(shape):
    return lax.broadcasted_iota(jnp.int32, shape, len(shape) - 1)


def swap_halves(value):
    first = lanes(value.shape) % HD < HD // 2
    up = pltpu.roll(value, value.shape[1] - HD // 2, 1)
    down = pltpu.roll(value, HD // 2, 1)
    return jnp.where(first, up, down)


def call(kernel, inputs, outputs, name, micros=2, mib=12):
    vmem = pl.BlockSpec(memory_space=pltpu.VMEM)
    return pl.pallas_call(
        kernel,
        in_specs=[vmem] * len(inputs),
        out_specs=[pl.BlockSpec() if sent else vmem for _, _, sent in outputs],
        out_shape=[jax.ShapeDtypeStruct(shape, dtype) for shape, dtype, _ in outputs],
        compiler_params=pltpu.CompilerParams(vmem_limit_bytes=mib << 20),
        cost_estimate=estimate(micros),
        name=name,
    )(*inputs)


def estimate(micros):
    return pl.CostEstimate(flops=int(micros * 1.1e9), bytes_accessed=1 << 16, transcendentals=0)


def weights_kernel(w_query, w_key, w_value, w_router, gains, segments, out):
    row = lax.broadcasted_iota(jnp.int32, (8, 128), 0)
    lane = lanes((8, 128))
    middle = (lane >= 32) & (lane < 96)
    seg = segments[...]
    low, high = (seg & 255).astype(F32), (seg >> 8).astype(F32)
    small = jnp.zeros((8, 128), F32)
    lines = (
        pltpu.roll(low, 32, 1),
        pltpu.roll(low, 96, 1),
        pltpu.roll(high, 32, 1),
        pltpu.roll(high, 96, 1),
    )
    for r, line in enumerate(lines):
        small = jnp.where((row == r + 1) & middle, line, small)
    small = jnp.where((row == 0) & (lane >= 32), pltpu.roll(gains[...], 32, 1), small)
    router = jnp.concatenate([w_router[...].astype(F32), jnp.zeros((8, 96), F32)], axis=1)
    small = jnp.where(lane < 32, router, small)
    parts = []
    for p in range(PARTS):
        columns = []
        for h in range(PART_HEADS):
            at = p * PART_HEADS + h
            columns.append(w_query[:, at * 128 : at * 128 + 128].astype(F32))
            columns.append(w_key[:, at * HD : at * HD + HD].astype(F32))
            columns.append(w_value[:, at * HD : at * HD + HD].astype(F32))
        parts.append(jnp.concatenate(columns + [small], axis=1).astype(BF))
    for to in range(4 * N_CTX):
        out[to] = parts[to % PARTS]


def pack_kernel(qkv, scale_q, scale_k, gain, cosine, sine, out):
    for j in range(PARTS):
        rows = slice(j * TOK, (j + 1) * TOK)
        turn_c, turn_s = cosine[rows], sine[rows]
        cq, ck = scale_q[rows], scale_k[rows]
        for h in range(PART_HEADS):
            at = h * 256
            q = qkv[rows, at : at + 128] * cq * gain[:, at : at + 128]
            q = (q * turn_c + swap_halves(q) * turn_s).astype(BF)
            kv = qkv[rows, at + 128 : at + 256]
            k = kv * ck * gain[:, at + 128 : at + 256]
            k = k * turn_c + swap_halves(k) * turn_s
            kv = jnp.where(lanes(kv.shape) < HD, k, kv).astype(BF)
            for qd in range(QUARTERS):
                to = (j * PART_HEADS + h) * QUARTERS + qd
                out[to, 0:TOK, :] = kv
                out[to, TOK : TOK + 16, :] = q[qd * 16 : qd * 16 + 16]
                out[to, TOK + 16 : TOK + 32, :] = q[64 + qd * 16 : 64 + qd * 16 + 16]


def unpack_kernel(grads_q, qkv, scale_q, scale_k, gain, cosine, sine, out, sums, gain_grad):
    grads = grads_q
    for j in range(PARTS):
        rows = slice(j * TOK, (j + 1) * TOK)
        turn_c, turn_s = cosine[rows], sine[rows]
        cq, ck = scale_q[rows], scale_k[rows]
        sum_q = jnp.zeros((TOK, 128), F32)
        sum_k = jnp.zeros((TOK, 128), F32)
        for h in range(PART_HEADS):
            at = h * 256
            base = (j * PART_HEADS + h) * QUARTERS
            pieces = [
                grads[base + qd, TOK + 16 * half : TOK + 16 * half + 16, :]
                for half in range(2)
                for qd in range(QUARTERS)
            ]
            dq = jnp.concatenate(pieces, axis=0).astype(F32)
            dq = dq * turn_c - swap_halves(dq) * turn_s
            dkv = sum(grads[base + qd, 0:TOK, :].astype(F32) for qd in range(QUARTERS))
            dk = dkv * turn_c - swap_halves(dkv) * turn_s
            is_k = lanes(dkv.shape) < HD
            dkv = jnp.where(is_k, dk, dkv)
            a_q = qkv[rows, at : at + 128] * cq
            a_k = qkv[rows, at + 128 : at + 256] * ck
            through_q = dq * a_q
            through_k = jnp.where(is_k, dkv * a_k, 0.0)
            g_q = gain[:, at : at + 128]
            g_k = gain[:, at + 128 : at + 256]
            out[rows, at : at + 128] = dq * g_q
            out[rows, at + 128 : at + 256] = dkv * g_k
            sum_q = sum_q + through_q * g_q
            sum_k = sum_k + through_k * g_k
            line_q = jnp.sum(through_q, axis=0, keepdims=True)
            line_k = jnp.sum(through_k, axis=0, keepdims=True)
            if j == 0:
                gain_grad[:, at : at + 128] = line_q
                gain_grad[:, at + 128 : at + 256] = line_k
            else:
                gain_grad[:, at : at + 128] += line_q
                gain_grad[:, at + 128 : at + 256] += line_k
        total_q = jnp.sum(sum_q, axis=1, keepdims=True)
        total_k = jnp.sum(sum_k, axis=1, keepdims=True)
        sums[rows, :] = jnp.where(lanes((TOK, 128)) == 0, total_q, total_k)


def heads_in_kernel(received, out):
    for j in range(PARTS):
        for h in range(PART_HEADS):
            for qd in range(QUARTERS):
                block = received[(j * PART_HEADS + h) * QUARTERS + qd]
                columns = slice(h * 128, h * 128 + 128)
                out[j, qd * 16 : qd * 16 + 16, columns] = block[:16]
                out[j, 64 + qd * 16 : 80 + qd * 16, columns] = block[16:]


def heads_out_kernel(*refs):
    out = refs[-1]
    for j in range(PARTS):
        for h in range(PART_HEADS):
            for qd in range(QUARTERS):
                to = (j * PART_HEADS + h) * QUARTERS + qd
                columns = slice(h * 128, h * 128 + 128)
                out[to, :16] = refs[j][qd * 16 : qd * 16 + 16, columns]
                out[to, 16:] = refs[j][64 + qd * 16 : 80 + qd * 16, columns]


def finish_kernel(through, qkv, scale_q, scale_k, sum_q, sum_k, normed, proj, scaled_in, small, last, grad_normed):
    lane = lanes((TOK, COLS)) % 256
    is_q, is_k = lane < 128, (lane >= 128) & (lane < 192)
    grads = []
    for j in range(PARTS):
        rows = slice(j * TOK, (j + 1) * TOK)
        scale = jnp.where(is_q, scale_q[rows], jnp.where(is_k, scale_k[rows], 1.0))
        mean = jnp.where(is_q, sum_q[rows] / 1024, jnp.where(is_k, sum_k[rows] / 512, 0.0))
        grads.append((scale * (through[rows, :] - qkv[rows, :] * scale * mean)).astype(BF))
    grad = jnp.concatenate(grads, axis=0)
    normed_grad = dot(grad, proj[...], ((1,), (1,)))
    grad_normed[...] = normed_grad
    products = (normed_grad * scaled_in[...]).astype(BF)
    ones = jnp.where(lanes((ROWS, 128)) == 64, 1.0, 0.0).astype(BF)
    last[:, :COLS] = dot(normed[...], grad, ((0,), (0,))).astype(BF)
    last[:, COLS:] = (small[...].astype(F32) + dot(products, ones, ((0,), (0,)))).astype(BF)


def finish_out_kernel(attended, branch, routed, logits, products, out):
    out[:, :512] = dot(attended[...], branch[...], ((0,), (0,))).astype(BF)
    ones = jnp.where(lanes((TOK, 128)) == 64, 1.0, 0.0).astype(BF)
    small = dot(routed[...], logits[...], ((0,), (0,))) + dot(products[...], ones, ((0,), (0,)))
    out[:, 512:] = small.astype(BF)


def pick(first, rows_out):
    i = lax.broadcasted_iota(jnp.int32, (128, 128), 1 if rows_out else 0)
    j = lax.broadcasted_iota(jnp.int32, (128, 128), 0 if rows_out else 1)
    return (i == j % HD + first).astype(BF)


def head_rows(block):
    low_half = lanes(block.shape) < HD
    zero = jnp.zeros_like(block)
    return jnp.concatenate([jnp.where(low_half, block, zero), jnp.where(low_half, zero, block)], 0)


def query_rows(block):
    low_half = lanes(block.shape) < HD
    block = block.astype(F32) * HD**-0.5
    return jnp.concatenate(
        [
            jnp.where(low_half, block, 0.0),
            jnp.where(low_half, pltpu.roll(block, HD, 1), 0.0),
        ],
        axis=0,
    ).astype(BF)


def key_segments(seg_key, columns):
    for src in range(N_CTX):
        line = jnp.broadcast_to(seg_key[src : src + 1, :], (TOK, TOK))
        columns[src * TOK : (src + 1) * TOK, :] = line.T


def forward_kernel(packed, seg_key, seg_query, mixed, mixed_low, lse, kv, kv_t, columns, limits):
    src = TOK_TILE // 32
    kv[...] = packed[:, 0:TOK, :].reshape(KEYS, 128)
    i = lax.broadcasted_iota(jnp.int32, (128, 128), 0)
    kv_t[...] = dot((i == lanes((128, 128))).astype(BF), kv[...], ((1,), (1,))).astype(BF)
    key_segments(seg_key, columns)
    limits[...] = jnp.ones_like(limits)

    def tile_rows(tile):
        q = packed[pl.ds(tile * src, src), TOK:PACK, :].reshape(TOK_TILE, 128)
        return query_rows(q), jnp.concatenate([seg_query[tile], seg_query[tile]], axis=1)

    def scores(rows, seg_q, keys):
        s = dot(kv[keys, :], rows, ((1,), (1,)))
        seg_k = jnp.concatenate([columns[keys, :]] * (2 * TOK_TILE // 128), axis=1)
        return jnp.where(seg_k == seg_q, s, -1e30)

    def sums(p):
        return jnp.sum(p.reshape(KEY_TILE // 8, 8, 2 * TOK_TILE), axis=0)

    def store(tile, accum, total, top):
        out = (accum / total).T
        out = jnp.where(
            lanes((TOK_TILE, 128)) < HD, pltpu.roll(out[:TOK_TILE], HD, 1), out[TOK_TILE:]
        )
        mixed[pl.ds(tile * TOK_TILE, TOK_TILE), :] = out
        mixed_low[pl.ds(tile * src, src)] = out.astype(BF).reshape(src, 32, 128)
        lse[tile] = top + jnp.log(total)

    for tile in range(TILES):
        rows, seg_q = tile_rows(tile)
        total = jnp.zeros((8, 2 * TOK_TILE), F32)
        accum = jnp.zeros((128, 2 * TOK_TILE), F32)
        for t in range(KEYS // KEY_TILE):
            keys = slice(t * KEY_TILE, (t + 1) * KEY_TILE)
            p = jnp.exp(scores(rows, seg_q, keys))
            total = total + sums(p)
            accum = accum + dot(kv_t[:, keys], p.astype(BF))
        total = jnp.sum(total, axis=0, keepdims=True)
        store(tile, accum, total, jnp.zeros_like(total))
        limits[...] = jnp.maximum(limits[...], jnp.maximum(total, 1.0 / total))

    @pl.when(jnp.logical_not(jnp.max(limits[...]) < 1e25))
    def _():
        @pl.loop(0, TILES)
        def _(tile):
            rows, seg_q = tile_rows(tile)
            top = jnp.full((1, 2 * TOK_TILE), -1e30, F32)
            total = jnp.zeros((8, 2 * TOK_TILE), F32)
            accum = jnp.zeros((128, 2 * TOK_TILE), F32)
            for t in range(KEYS // KEY_TILE):
                keys = slice(t * KEY_TILE, (t + 1) * KEY_TILE)
                s = scores(rows, seg_q, keys)
                newest = jnp.maximum(top, jnp.max(s, axis=0, keepdims=True))
                fade = jnp.exp(top - newest)
                p = jnp.exp(s - newest)
                p = jnp.where(s > -1e29, p, 0.0)
                top = newest
                total = total * fade + sums(p)
                accum = accum * fade + dot(kv_t[:, keys], p.astype(BF))
            store(tile, accum, jnp.sum(total, axis=0, keepdims=True), top)


def backward_kernel(packed, seg_key, seg_query, upper, mixed, lse, out, k2, k2t, v2, dk, dv, columns):
    @pl.when(pl.program_id(0) == 0)
    def _():
        kv = packed[:, 0:TOK, :].reshape(KEYS, 128)
        k2[...] = dot(kv, pick(0, False)).astype(BF)
        k2t[...] = dot(pick(0, True), kv, ((1,), (1,))).astype(BF)
        v2[...] = dot(kv, pick(HD, False)).astype(BF)
        dk[...] = jnp.zeros_like(dk)
        dv[...] = jnp.zeros_like(dv)
        key_segments(seg_key, columns)

    tile = pl.program_id(0)
    src = TOK_TILE // 32
    q = packed[pl.ds(tile * src, src), TOK:PACK, :].reshape(TOK_TILE, 128)
    rows = head_rows(q * BF(HD**-0.5))
    upper_now = upper[...].reshape(TOK_TILE, 128)
    up = head_rows(upper_now)
    along = (upper_now.astype(F32) * mixed[...]).T
    delta = jnp.concatenate(
        [
            jnp.sum(along[:HD], axis=0, keepdims=True),
            jnp.sum(along[HD:], axis=0, keepdims=True),
        ],
        axis=1,
    )
    seg_q = jnp.concatenate([seg_query[tile], seg_query[tile]], axis=1)
    dq = jnp.zeros((128, 2 * TOK_TILE), F32)
    for t in range(KEYS // KEY_TILE):
        at = t * KEY_TILE
        keys = slice(at, at + KEY_TILE)
        s = dot(k2[keys, :], rows, ((1,), (1,)))
        seg_k = jnp.concatenate([columns[keys, :]] * (2 * TOK_TILE // 128), axis=1)
        p = jnp.where(seg_k == seg_q, jnp.exp(s - lse[0]), 0.0)
        dp = dot(v2[keys, :], up, ((1,), (1,)))
        ds = (p * (dp - delta)).astype(BF)
        dv[keys, :] += dot(p.astype(BF), up)
        dk[keys, :] += dot(ds, rows)
        dq = dq + dot(k2t[:, keys], ds)
    dq = (dq * HD**-0.5).T
    dq = jnp.where(lanes((TOK_TILE, 128)) < HD, dq[:TOK_TILE], dq[TOK_TILE:])
    out[pl.ds(tile * src, src), TOK:PACK, :] = dq.astype(BF).reshape(src, 32, 128)

    @pl.when(tile == pl.num_programs(0) - 1)
    def _():
        for t in range(KEYS // KEY_TILE):
            keys = slice(t * KEY_TILE, (t + 1) * KEY_TILE)
            low_half = lanes((KEY_TILE, 128)) < HD
            both_k = dk[keys, :] + pltpu.roll(dk[keys, :], HD, 1)
            both_v = dv[keys, :] + pltpu.roll(dv[keys, :], HD, 1)
            both = jnp.where(low_half, both_k, both_v).astype(BF).reshape(-1, TOK, 128)
            out[t * KEY_TILE // TOK : (t + 1) * KEY_TILE // TOK, 0:TOK, :] = both


def whole(shape):
    return pl.BlockSpec(shape, lambda i: (0,) * len(shape))


def attend(packed, seg_key, seg_query):
    vmem = pl.BlockSpec(memory_space=pltpu.VMEM)
    return pl.pallas_call(
        forward_kernel,
        in_specs=[vmem] * 3,
        out_specs=[vmem, pl.BlockSpec(), vmem],
        out_shape=[
            jax.ShapeDtypeStruct((QUERIES, 128), F32),
            jax.ShapeDtypeStruct((N_CTX, 32, 128), BF),
            jax.ShapeDtypeStruct((TILES, 1, 2 * TOK_TILE), F32),
        ],
        scratch_shapes=[
            pltpu.VMEM((KEYS, 128), BF),
            pltpu.VMEM((128, KEYS), BF),
            pltpu.VMEM((KEYS, 128), jnp.int32),
            pltpu.VMEM((1, 2 * TOK_TILE), F32),
        ],
        compiler_params=pltpu.CompilerParams(vmem_limit_bytes=24 << 20),
        cost_estimate=estimate(12),
        name="attend",
    )(packed, seg_key, seg_query)


def attend_back(packed, seg_key, seg_query, upper, mixed, lse):
    src = TOK_TILE // 32
    return pl.pallas_call(
        backward_kernel,
        grid=(TILES,),
        in_specs=[
            whole((N_CTX, PACK, 128)),
            whole((N_CTX, TOK)),
            whole((TILES, 1, TOK_TILE)),
            pl.BlockSpec((src, 32, 128), lambda i: (i, 0, 0)),
            pl.BlockSpec((TOK_TILE, 128), lambda i: (i, 0)),
            pl.BlockSpec((1, 1, 2 * TOK_TILE), lambda i: (i, 0, 0)),
        ],
        out_specs=whole((N_CTX, PACK, 128)),
        out_shape=jax.ShapeDtypeStruct((N_CTX, PACK, 128), BF),
        scratch_shapes=[
            pltpu.VMEM((KEYS, 128), BF),
            pltpu.VMEM((128, KEYS), BF),
            pltpu.VMEM((KEYS, 128), BF),
            pltpu.VMEM((KEYS, 128), F32),
            pltpu.VMEM((KEYS, 128), F32),
            pltpu.VMEM((KEYS, 128), jnp.int32),
        ],
        compiler_params=pltpu.CompilerParams(vmem_limit_bytes=32 << 20),
        cost_estimate=estimate(25),
        name="attend_back",
    )(packed, seg_key, seg_query, upper, mixed, lse)


def in_order(pieces, fsdp):
    pieces = jnp.stack(pieces)
    return jnp.concatenate(
        [lax.dynamic_index_in_dim(pieces, fsdp ^ p, keepdims=False) for p in range(4)], axis=0
    )


def inverse_rms(value):
    return lax.rsqrt(jnp.mean(value * value, axis=-1, keepdims=True) + EPSILON)


def after(value, *others):
    return lax.optimization_barrier((value, *others))[0]


def shards(
    hidden_in,
    segment_ids,
    block_order,
    expert_ids,
    pair_order,
    attn_norm,
    w_query,
    w_key,
    w_value,
    query_norm,
    key_norm,
    w_out,
    ffn_norm,
    w_router,
    w_gate,
    w_up,
    w_down,
    cotangent,
):
    place = lax.axis_index("ctx")
    fsdp = lax.axis_index("fsdp")
    core = fsdp % 2
    part = fsdp % PARTS
    both_axes = ("ctx", "fsdp")

    gains = jnp.concatenate([attn_norm, query_norm, ffn_norm, key_norm, jnp.zeros((100,), BF)])
    outgoing_w = call(
        weights_kernel,
        (w_query, w_key, w_value, w_router, gains.astype(F32)[None], segment_ids),
        [((4 * N_CTX, 8, COLS + 128), BF, True)],
        "weights",
    )[0]
    out_rows, outgoing_w = lax.optimization_barrier(
        ([swap(w_out, j) for j in range(4)], outgoing_w)
    )
    gathered = exchange(outgoing_w, both_axes)
    small = gathered[:, :, COLS:]

    tokens = hidden_in[0]
    order = block_order[0]
    blocks = lax.dynamic_slice_in_dim(order, place * 2, 2)
    if PARTS == 2:
        tokens_all = [tokens, swap(tokens, 1)]
        blocks_all = [blocks, swap(blocks, 1)]
    else:
        far, far_blocks = swap(tokens, 2), swap(blocks, 2)
        tokens_all = [tokens, swap(tokens, 1), far, swap(far, 1)]
        blocks_all = [blocks, swap(blocks, 1), far_blocks, swap(far_blocks, 1)]
    tokens_all = jnp.concatenate(tokens_all, axis=0)

    proj_out = lax.all_gather(in_order(out_rows, fsdp), "ctx", axis=0, tiled=True)

    ids = expert_ids[0]
    experts = jnp.arange(EXPERTS, dtype=jnp.int32)
    named = ids.T[None, :, :] == experts[:, None, None]
    chosen = jnp.any(named, axis=1)
    ranks = pair_order[0, 0].reshape(TOK, TOPK).T
    rank = jnp.sum(jnp.where(named, ranks[None], 0), axis=1)
    earlier = chosen[:, :, None] & (rank[:, :, None] < rank[:, None, :])
    slot = jnp.sum(earlier.astype(jnp.int32), axis=1)
    kept = chosen & (slot < CAP)
    slot = jnp.where(kept, slot, -1)
    places = slot[:, None, :] == jnp.arange(CAP, dtype=jnp.int32)[None, :, None]
    one_hot = places.astype(BF).reshape(EXPERTS * CAP, TOK)

    lay = jnp.arange(TOK, dtype=jnp.int32)
    half = TOK // 2
    positions = (jnp.repeat(jnp.stack(blocks_all), half, axis=1) * half + lay % half).reshape(ROWS)
    freq = THETA ** (-jnp.arange(0, HD, 2).astype(F32) / HD)
    turned = positions.astype(F32)[:, None] * freq[None, :]
    cosine = jnp.tile(jnp.cos(turned), (1, 4))
    sine = jnp.sin(turned)
    sine = jnp.concatenate([-sine, sine, -sine, sine], axis=1)

    lines = small[:, 0, 32:60].astype(F32)
    gain_attn = lines[:, 0:8].reshape(1, D)
    gain_query = lines[:, 8:16].reshape(D)
    gain_ffn = lines[:, 16:24].reshape(1, D)
    gain_key = lines[:, 24:28].reshape(512)
    gain_heads = jnp.concatenate(
        [
            lax.dynamic_slice_in_dim(gain_query, part * FEATURES, FEATURES).reshape(PART_HEADS, 128),
            lax.dynamic_slice_in_dim(gain_key, part * FEATURES // 2, FEATURES // 2).reshape(
                PART_HEADS, HD
            ),
            jnp.ones((PART_HEADS, HD), F32),
        ],
        axis=1,
    ).reshape(1, COLS)
    proj = gathered[:, :, :COLS].reshape(D, COLS)
    proj_router = small[:, :, :EXPERTS].reshape(D, EXPERTS)

    inputs_all = tokens_all.astype(F32)
    scale_in = inverse_rms(inputs_all)
    scaled_in = inputs_all * scale_in
    normed_low = (scaled_in * gain_attn).astype(BF)
    qkv = dot(normed_low, proj)
    lane = jnp.arange(COLS)[None] % 256
    is_q, is_k = lane < 128, (lane >= 128) & (lane < 192)
    squares = qkv * qkv
    square_sums = jnp.stack(
        [
            jnp.sum(jnp.where(is_q, squares, 0.0), axis=1),
            jnp.sum(jnp.where(is_k, squares, 0.0), axis=1),
        ]
    )
    square_sums = sum_parts(square_sums.reshape(2, PARTS, TOK)).reshape(2, ROWS)
    scale_q = lax.rsqrt(square_sums[0] / 1024 + EPSILON)[:, None]
    scale_k = lax.rsqrt(square_sums[1] / 512 + EPSILON)[:, None]
    packed = call(
        pack_kernel,
        (qkv, scale_q, scale_k, gain_heads, cosine, sine),
        [((N_CTX, PACK, 128), BF, True)],
        "pack",
    )[0]
    packed = exchange(packed, "ctx")

    sequence = fsdp ^ (place // (N_CTX // PARTS))
    seg_small = lax.dynamic_index_in_dim(
        small.reshape(N_CTX, 4, 8, 128), sequence, axis=1, keepdims=False
    )[:, 1:5, 32:96].astype(jnp.int32)
    seg_all = (seg_small[:, 0:2] + 256 * seg_small[:, 2:4]).reshape(N_CTX, TOK)
    seg_query = lax.dynamic_index_in_dim(
        seg_all.reshape(N_CTX, 2, QUARTERS, 16), place % QUARTERS, axis=2, keepdims=False
    ).reshape(TILES, 1, TOK_TILE)

    packed, shard_gate, shard_up, shard_down = lax.optimization_barrier(
        (packed, w_gate[0], w_up[0], w_down[0])
    )
    shards_far = [swap(shard, 2) for shard in (shard_gate, shard_up, shard_down)]
    gate_w, up_w, down_w = [
        in_order([own, swap(own, 1), far, swap(far, 1)], fsdp)
        for own, far in zip((shard_gate, shard_up, shard_down), shards_far)
    ]

    mixed, mixed_low, lse = attend(packed, seg_all, seg_query)
    returned = exchange(mixed_low, "ctx")
    returned = call(heads_in_kernel, (returned,), [((PARTS, TOK, FEATURES), BF, False)], "heads_in", 1)[0]
    pieces = swapped([returned[j] for j in range(PARTS)])
    out_parts = proj_out.reshape(PARTS, FEATURES, D)
    out_parts = [
        lax.dynamic_index_in_dim(out_parts, part ^ j, keepdims=False) for j in range(PARTS)
    ]
    inputs = tokens.astype(F32)
    middle = inputs
    for piece, out_part in zip(pieces, out_parts):
        middle = middle + dot(piece, out_part)
    scale_mid = inverse_rms(middle)
    scaled_mid = middle * scale_mid
    routed_in = (scaled_mid * gain_ffn).astype(BF)
    logits = dot(proj_router, routed_in, ((0,), (1,)))
    logits = jnp.where(chosen, logits, -1e30)
    raised = jnp.where(chosen, jnp.exp(logits - jnp.max(logits, axis=0, keepdims=True)), 0.0)
    gates = raised / jnp.sum(raised, axis=0, keepdims=True)

    upstream_low = cotangent[0]
    upstream = upstream_low.astype(F32)
    rows_out = dot(one_hot, routed_in).astype(BF).reshape(EXPERTS, CAP, D)
    arrived = exchange(rows_out, "ctx").reshape(N_CTX * CAP, D)
    share = jnp.where(places, gates[:, None, :], 0.0)
    row_share = jnp.sum(share, axis=2).reshape(EXPERTS * CAP, 1)
    grads_out = (dot(one_hot, upstream_low) * row_share).astype(BF).reshape(EXPERTS, CAP, D)
    arrived, grads_out, gate_w, up_w, down_w = lax.optimization_barrier(
        (arrived, grads_out, gate_w, up_w, down_w)
    )
    arrived_grad = exchange(grads_out, "ctx").reshape(N_CTX * CAP, D)

    gate_act = dot(arrived, gate_w)
    up_act = dot(arrived, up_w)
    sigma = jax.nn.sigmoid(gate_act)
    silu_gate = gate_act * sigma
    inner = (silu_gate * up_act).astype(BF)
    produced = dot(inner, down_w).astype(BF).reshape(N_CTX, CAP, D)
    produced, arrived_grad = lax.optimization_barrier((produced, arrived_grad))
    produced_home = exchange(produced, "ctx").reshape(EXPERTS * CAP, D)

    grad_inner = dot(arrived_grad, down_w, ((1,), (1,)))
    grad_gate_act = (grad_inner * up_act * sigma * (1.0 + gate_act * (1.0 - sigma))).astype(BF)
    grad_up_act = (grad_inner * silu_gate).astype(BF)
    grad_rows = dot(grad_gate_act, gate_w, ((1,), (1,))) + dot(grad_up_act, up_w, ((1,), (1,)))
    grad_rows = grad_rows.astype(BF).reshape(N_CTX, CAP, D)
    produced_home, grad_rows = lax.optimization_barrier((produced_home, grad_rows))
    grad_home = exchange(grad_rows, "ctx").reshape(EXPERTS * CAP, D)

    share = share.reshape(EXPERTS * CAP, TOK)
    share_high = share.astype(BF)
    share_low = (share - share_high.astype(F32)).astype(BF)
    combined = dot(share_high, produced_home, ((0,), (0,)))
    combined = combined + dot(share_low, produced_home, ((0,), (0,)))
    layer_out = (middle + combined).astype(BF)[None]
    along = dot(produced_home, upstream_low, ((1,), (1,))).reshape(EXPERTS, CAP, TOK)
    grad_gates = jnp.sum(jnp.where(places, along, 0.0), axis=1)
    grad_chosen = gates * (grad_gates - jnp.sum(gates * grad_gates, axis=0, keepdims=True))
    grad_logits = grad_chosen.astype(BF)
    grad_routed = dot(grad_logits, proj_router, ((0,), (1,)))
    grad_routed = grad_routed + dot(one_hot, grad_home, ((0,), (0,)))
    through = grad_routed * gain_ffn
    grad_middle = upstream + scale_mid * (
        through - scaled_mid * jnp.mean(through * scaled_mid, axis=1, keepdims=True)
    )
    grad_branch = grad_middle.astype(BF)
    grad_mixed = [dot(grad_branch, out_part, ((1,), (1,))).astype(BF) for out_part in out_parts]
    upper = call(
        heads_out_kernel, tuple(swapped(grad_mixed)), [((N_CTX, 32, 128), BF, True)], "heads_out", 1
    )[0]
    upper, arrived, arrived_grad = lax.optimization_barrier((upper, arrived, arrived_grad))
    upper = exchange(upper, "ctx")

    grad_gate_w = dot(arrived, grad_gate_act, ((0,), (0,))).astype(BF)
    grad_up_w = dot(arrived, grad_up_act, ((0,), (0,))).astype(BF)
    grad_down_w = dot(inner, arrived_grad, ((0,), (0,))).astype(BF)
    grad_gate_up = lax.psum_scatter(
        jnp.stack([grad_gate_w, grad_up_w]), "fsdp", scatter_dimension=1, tiled=True
    ).astype(F32)
    grad_down = lax.psum_scatter(
        grad_down_w[None], "fsdp", scatter_dimension=1, tiled=True
    ).astype(F32)

    sorted_pieces = jnp.stack(pieces)
    attended = jnp.concatenate(
        [
            lax.dynamic_index_in_dim(sorted_pieces, part ^ p, keepdims=False)
            for p in range(PARTS)
        ],
        axis=1,
    )
    attended_2 = jnp.concatenate([attended, swap(attended, 1)], axis=0)
    branch_halves = jnp.stack([grad_branch[:, :512], grad_branch[:, 512:]])
    own_half = lax.dynamic_index_in_dim(branch_halves, core, keepdims=False)
    other_half = lax.dynamic_index_in_dim(branch_halves, 1 - core, keepdims=False)
    branch_2 = jnp.concatenate([own_half, swap(other_half, 1)], axis=0)
    late = call(
        finish_out_kernel,
        (
            attended_2,
            branch_2,
            routed_in,
            jnp.pad(grad_logits.T, ((0, 0), (0, 128 - EXPERTS))),
            (grad_routed * scaled_mid).astype(BF),
        ),
        [((D, 640), BF, True)],
        "finish_out",
    )[0]
    late, upper = lax.optimization_barrier((late, upper))
    first_sums = exchange(late.reshape(4 * N_CTX, 8, 640), both_axes)

    grads_home = attend_back(packed, seg_all, seg_query, upper, mixed, lse)
    grads_home, first_sums = lax.optimization_barrier((grads_home, first_sums))
    grads_home = exchange(grads_home, "ctx")

    through_heads, sums, grad_gain_heads = call(
        unpack_kernel,
        (grads_home, qkv, scale_q, scale_k, gain_heads, cosine, sine),
        [((ROWS, COLS), F32, False), ((ROWS, 128), F32, False), ((1, COLS), F32, False)],
        "unpack",
    )
    sums = sum_parts(sums[:, :2].T.reshape(2, PARTS, TOK)).reshape(2, ROWS)
    gain_lines = grad_gain_heads.reshape(PART_HEADS, 256)
    query_line = gain_lines[:, :128].reshape(FEATURES)
    key_line = gain_lines[:, 128:192].reshape(FEATURES // 2)
    query_line = lax.dynamic_update_slice_in_dim(
        jnp.zeros((1024,), F32), query_line, part * FEATURES, 0
    )
    key_line = lax.dynamic_update_slice_in_dim(
        jnp.zeros((512,), F32), key_line, part * FEATURES // 2, 0
    )
    small_grads = jnp.concatenate([query_line.reshape(128, 8), key_line.reshape(128, 4)], axis=1)
    small_grads = jnp.pad(small_grads.astype(BF)[:, None, :], ((0, 0), (0, 7), (0, 116)))
    last, grad_normed = call(
        finish_kernel,
        (
            through_heads,
            qkv,
            scale_q,
            scale_k,
            sums[0][:, None],
            sums[1][:, None],
            normed_low,
            proj,
            scaled_in,
            small_grads.reshape(D, 128),
        ),
        [((D, COLS + 128), BF, True), ((ROWS, D), F32, False)],
        "finish",
        3,
        24,
    )
    last_sums = exchange(last.reshape(4 * N_CTX, 8, COLS + 128), both_axes)

    grad_normed = grad_normed.reshape(PARTS, TOK, D)
    if PARTS == 4:
        grad_normed = grad_normed.astype(BF)
    grad_normed = sum(
        piece.astype(F32) for piece in swapped([grad_normed[j] for j in range(PARTS)])
    )
    through_in = grad_normed * gain_attn
    scaled_own = scaled_in[:TOK]
    input_grad = grad_middle + scale_in[:TOK] * (
        through_in - scaled_own * jnp.mean(through_in * scaled_own, axis=1, keepdims=True)
    )

    first_sums = jnp.sum(first_sums.reshape(2 * N_CTX, 2, 8, 640).astype(F32), axis=0)
    grad_out = jnp.concatenate([first_sums[0, :, :512], first_sums[1, :, :512]], axis=1)
    first_small = first_sums[0, :, 512:] + first_sums[1, :, 512:]
    last_sums = jnp.sum(
        last_sums.reshape(4 * N_CTX // PARTS, PARTS, 8, COLS + 128).astype(F32), axis=0
    )
    heads_g = last_sums[:, :, :COLS].reshape(PARTS, 8, PART_HEADS, 256)
    heads_g = jnp.transpose(heads_g, (1, 0, 2, 3))
    last_small = jnp.sum(last_sums[:, :, COLS:], axis=0)
    return (
        layer_out,
        input_grad[None],
        last_small[:, 64],
        heads_g[..., :128].reshape(8, 1024),
        heads_g[..., 128:192].reshape(8, 512),
        heads_g[..., 192:].reshape(8, 512),
        last_small[0, 0:8],
        last_small[0, 8:12],
        grad_out,
        first_small[:, 64],
        first_small[:, :EXPERTS],
        grad_gate_up[0][None],
        grad_gate_up[1][None],
        grad_down,
    )


def solution(mesh):
    row = P("fsdp", "ctx", None)
    flat = P(("ctx", "fsdp"))
    dense = P(("ctx", "fsdp"), None)
    expert = P("ctx", "fsdp", None)
    in_specs = (
        row,
        P("fsdp", "ctx"),
        P("fsdp", None),
        row,
        row,
        flat,
        dense,
        dense,
        dense,
        flat,
        flat,
        dense,
        flat,
        dense,
        expert,
        expert,
        expert,
        row,
    )
    out_specs = (
        row,
        row,
        flat,
        dense,
        dense,
        dense,
        flat,
        flat,
        dense,
        flat,
        dense,
        expert,
        expert,
        expert,
    )
    return jax.shard_map(shards, mesh=mesh, in_specs=in_specs, out_specs=out_specs, check_vma=False)
```

profile of v0, /device:TPU:1, one launch (start us, length us, event | category | flops | bytes accessed | tf_op | source)
XLA Modules:
  0.0 434.1 jit_solution(3220581440041709589)
XLA Ops:
  16.4 10.6 %all-to-all-start = ((bf16[128,8,1152]{2,1,0:T(8,128)(2,1)}), bf16[128,8,1152]{2,1,0:T(8,128)(2,1)}, u32[]{:S(2)}, u32[]{:S(2)}) async-start(bf16[128,8,1152]{2,1,0:T(8,128)(2,1)} %weights.1), calls=%async_computation | async-start | bytes 4718592 | tf_op jit(solution)/shard_map/all_to_all | solution.py:57
  31.6 28.8 %all-to-all-done = bf16[128,8,1152]{2,1,0:T(8,128)(2,1)} async-done(((bf16[128,8,1152]{2,1,0:T(8,128)(2,1)}), bf16[128,8,1152]{2,1,0:T(8,128)(2,1)}, u32[]{:S(2)}, u32[]{:S(2)}) %all-to-all-start) | async-done | bytes 2359328 | tf_op jit(solution)/shard_map/all_to_all | solution.py:57
  69.4 4.6 %all-to-all-start.1 = ((bf16[32,160,128]{2,1,0:T(8,128)(2,1)}), bf16[32,160,128]{2,1,0:T(8,128)(2,1)S(1)}, u32[]{:S(2)}, u32[]{:S(2)}) async-start(bf16[32,160,128]{2,1,0:T(8,128)(2,1)} %copy-done.3), calls=%async_computation.1 | async-start | bytes 2621440 | tf_op jit(solution)/shard_map/all_to_all | solution.py:57
  78.4 15.0 %all-to-all-done.1.packed = bf16[32,160,128]{2,1,0:T(8,128)(2,1)S(1)} async-done(((bf16[32,160,128]{2,1,0:T(8,128)(2,1)}), bf16[32,160,128]{2,1,0:T(8,128)(2,1)S(1)}, u32[]{:S(2)}, u32[]{:S(2)}) %all-to-all-start.1) | async-done | bytes 1310752 | tf_op jit(solution)/shard_map/all_to_all | solution.py:57
  93.4 10.1 %attend.1 = (f32[1024,128]{1,0:T(8,128)S(1)}, bf16[32,32,128]{2,1,0:T(8,128)(2,1)}, f32[8,1,256]{2,1,0:T(1,128)S(1)}) custom-call(bf16[32,160,128]{2,1,0:T(8,128)(2,1)S(1)} %all-to-all-done.1.packed, s32[32,128]{1,0:T(8,128)S(1)} %copy.168.seg_key, s32[8,1,128]{2,1,0:T(1,128)S(1)} %bitcast.267), custom_call_target="tpu_custom_call" | custom-call | flops 13200000000 | bytes 65536 | tf_op jit(solution)/shard_map/attend/pallas_call | solution.py:382
  105.0 7.5 %all-to-all-start.2 = ((bf16[32,32,128]{2,1,0:T(8,128)(2,1)}), bf16[32,32,128]{2,1,0:T(8,128)(2,1)S(1)}, u32[]{:S(2)}, u32[]{:S(2)}) async-start(bf16[32,32,128]{2,1,0:T(8,128)(2,1)} %get-tuple-element.49), calls=%async_computation.2 | async-start | bytes 524288 | tf_op jit(solution)/shard_map/all_to_all | solution.py:57
  117.8 4.2 all-to-all-done.2.received
  131.8 8.7 %all-to-all-start.3 = ((bf16[32,32,1024]{2,1,0:T(8,128)(2,1)}), bf16[32,32,1024]{2,1,0:T(8,128)(2,1)}, u32[]{:S(2)}, u32[]{:S(2)}) async-start(bf16[32,32,1024]{2,1,0:T(8,128)(2,1)} %bitcast.275), calls=%async_computation.3 | async-start | bytes 4194304 | tf_op jit(solution)/shard_map/all_to_all | solution.py:57
  145.4 2.9 multiply_convert_fusion
  156.3 11.4 %all-to-all-done.3 = bf16[32,32,1024]{2,1,0:T(8,128)(2,1)} async-done(((bf16[32,32,1024]{2,1,0:T(8,128)(2,1)}), bf16[32,32,1024]{2,1,0:T(8,128)(2,1)}, u32[]{:S(2)}, u32[]{:S(2)}) %all-to-all-start.3) | async-done | bytes 2097184 | tf_op jit(solution)/shard_map/all_to_all | solution.py:57
  167.7 9.0 %all-to-all-start.4 = ((bf16[32,32,1024]{2,1,0:T(8,128)(2,1)}), bf16[32,32,1024]{2,1,0:T(8,128)(2,1)}, u32[]{:S(2)}, u32[]{:S(2)}) async-start(bf16[32,32,1024]{2,1,0:T(8,128)(2,1)} %bitcast.276), calls=%async_computation.4 | async-start | bytes 4194304 | tf_op jit(solution)/shard_map/all_to_all | solution.py:57
  176.7 3.2 fusion.75
  180.0 5.2 %multiply_convert_fusion.3 = (bf16[1024,512]{1,0:T(8,128)(2,1)S(1)}, f32[1024,512]{1,0:T(8,128)}) fusion(f32[1024,512]{1,0:T(8,128)S(1)} %fusion.75, bf16[1024,1024]{1,0:T(8,128)(2,1)} %bitcast.44, bf16[1024,512]{1,0:T(8,128)(2,1)S(1)} %copy-done.38), kind=kOutput, calls=%fused_computation.8 | convolution fusion | flops 1076887552 | bytes 8388608 | tf_op jit(solution)/shard_map/dot_general | solution.py:37
  188.7 14.7 %all-to-all-done.4 = bf16[32,32,1024]{2,1,0:T(8,128)(2,1)} async-done(((bf16[32,32,1024]{2,1,0:T(8,128)(2,1)}), bf16[32,32,1024]{2,1,0:T(8,128)(2,1)}, u32[]{:S(2)}, u32[]{:S(2)}) %all-to-all-start.4) | async-done | bytes 2097184 | tf_op jit(solution)/shard_map/all_to_all | solution.py:57
  203.4 7.9 %all-to-all-start.5 = ((bf16[32,32,1024]{2,1,0:T(8,128)(2,1)}), bf16[32,32,1024]{2,1,0:T(8,128)(2,1)}, u32[]{:S(2)}, u32[]{:S(2)}) async-start(bf16[32,32,1024]{2,1,0:T(8,128)(2,1)} %bitcast.281), calls=%async_computation.5 | async-start | bytes 4194304 | tf_op jit(solution)/shard_map/all_to_all | solution.py:57
  211.3 5.2 %multiply_convert_fusion.1 = (bf16[1024,512]{1,0:T(8,128)(2,1)S(1)}, bf16[1024,512]{1,0:T(8,128)(2,1)S(1)}) fusion(f32[1024,512]{1,0:T(8,128)} %copy-done.82, f32[1024,512]{1,0:T(8,128)} %get-tuple-element.138, bf16[1024,1024]{1,0:T(8,128)(2,1)} %bitcast.73, bf16[512,1024]{1,0:T(8,128)(2,1)} %pad_maximum_fusion.6), kind=kOutput, calls=%fused_computation.6 | convolution fusion | flops 1080557568 | bytes 9437184 | tf_op jit(solution)/shard_map/dot_general | solution.py:37
  221.1 16.9 %all-to-all-done.5 = bf16[32,32,1024]{2,1,0:T(8,128)(2,1)} async-done(((bf16[32,32,1024]{2,1,0:T(8,128)(2,1)}), bf16[32,32,1024]{2,1,0:T(8,128)(2,1)}, u32[]{:S(2)}, u32[]{:S(2)}) %all-to-all-start.5) | async-done | bytes 2097184 | tf_op jit(solution)/shard_map/all_to_all | solution.py:57
  238.0 8.1 %all-to-all-start.6 = ((bf16[32,32,1024]{2,1,0:T(8,128)(2,1)}), bf16[32,32,1024]{2,1,0:T(8,128)(2,1)}, u32[]{:S(2)}, u32[]{:S(2)}) async-start(bf16[32,32,1024]{2,1,0:T(8,128)(2,1)} %bitcast.277), calls=%async_computation.6 | async-start | bytes 4194304 | tf_op jit(solution)/shard_map/all_to_all | solution.py:57
  249.6 2.9 fusion.6
  255.9 17.1 %all-to-all-done.6 = bf16[32,32,1024]{2,1,0:T(8,128)(2,1)} async-done(((bf16[32,32,1024]{2,1,0:T(8,128)(2,1)}), bf16[32,32,1024]{2,1,0:T(8,128)(2,1)}, u32[]{:S(2)}, u32[]{:S(2)}) %all-to-all-start.6) | async-done | bytes 2097184 | tf_op jit(solution)/shard_map/all_to_all | solution.py:57
  283.0 3.9 fusion.3
  286.9 6.6 %all-to-all-start.7 = ((bf16[32,32,128]{2,1,0:T(8,128)(2,1)}), bf16[32,32,128]{2,1,0:T(8,128)(2,1)}, u32[]{:S(2)}, u32[]{:S(2)}) async-start(bf16[32,32,128]{2,1,0:T(8,128)(2,1)} %copy-done.8), calls=%async_computation.7 | async-start | bytes 524288 | tf_op jit(solution)/shard_map/all_to_all | solution.py:57
  297.0 7.0 %all-to-all-done.7.upper = bf16[32,32,128]{2,1,0:T(8,128)(2,1)} async-done(((bf16[32,32,128]{2,1,0:T(8,128)(2,1)}), bf16[32,32,128]{2,1,0:T(8,128)(2,1)}, u32[]{:S(2)}, u32[]{:S(2)}) %all-to-all-start.7) | async-done | bytes 262176 | tf_op jit(solution)/shard_map/all_to_all | solution.py:57
  304.0 8.3 %all-to-all-start.8 = ((bf16[128,8,640]{2,1,0:T(8,128)(2,1)}), bf16[128,8,640]{2,1,0:T(8,128)(2,1)}, u32[]{:S(2)}, u32[]{:S(2)}) async-start(bf16[128,8,640]{2,1,0:T(8,128)(2,1)} %bitcast.265), calls=%async_computation.8 | async-start | bytes 2621440 | tf_op jit(solution)/shard_map/all_to_all | solution.py:57
  312.3 25.1 %attend_back.1 = bf16[32,160,128]{2,1,0:T(8,128)(2,1)S(1)} custom-call(bf16[32,160,128]{2,1,0:T(8,128)(2,1)S(1)} %all-to-all-done.1.packed, s32[32,128]{1,0:T(8,128)S(1)} %copy-done.17, s32[8,1,128]{2,1,0:T(1,128)S(1)} %bitcast.268, bf16[32,32,128]{2,1,0:T(8,128)(2,1)} %all-to-all-done.7.upper, f32[1024,128]{1,0:T(8,128)S(1)} %copy-done.29, ...), custom_call_target="tpu_custom_call" | custom-call | flops 27499999232 | bytes 65536 | tf_op jit(solution)/shard_map/attend_back/pallas_call | solution.py:405
  338.6 9.9 %all-to-all-start.9 = ((bf16[32,160,128]{2,1,0:T(8,128)(2,1)}), bf16[32,160,128]{2,1,0:T(8,128)(2,1)S(1)}, u32[]{:S(2)}, u32[]{:S(2)}) async-start(bf16[32,160,128]{2,1,0:T(8,128)(2,1)} %copy-done.4), calls=%async_computation.9 | async-start | bytes 2621440 | tf_op jit(solution)/shard_map/all_to_all | solution.py:57
  348.8 3.2 fusion.1
  356.5 3.3 slice_bitcast_fusion.proj
  361.6 6.2 %all-to-all-done.9.grads_q = bf16[32,160,128]{2,1,0:T(8,128)(2,1)S(1)} async-done(((bf16[32,160,128]{2,1,0:T(8,128)(2,1)}), bf16[32,160,128]{2,1,0:T(8,128)(2,1)S(1)}, u32[]{:S(2)}, u32[]{:S(2)}) %all-to-all-start.9) | async-done | bytes 1310752 | tf_op jit(solution)/shard_map/all_to_all | solution.py:57
  380.7 3.0 finish.1
  383.7 4.9 %all-to-all-start.10 = ((bf16[128,8,1152]{2,1,0:T(8,128)(2,1)}), bf16[128,8,1152]{2,1,0:T(8,128)(2,1)}, u32[]{:S(2)}, u32[]{:S(2)}) async-start(bf16[128,8,1152]{2,1,0:T(8,128)(2,1)} %bitcast.100), calls=%async_computation.10 | async-start | bytes 4718592 | tf_op jit(solution)/shard_map/all_to_all | solution.py:57
  405.9 15.5 %all-to-all-done.10 = bf16[128,8,1152]{2,1,0:T(8,128)(2,1)} async-done(((bf16[128,8,1152]{2,1,0:T(8,128)(2,1)}), bf16[128,8,1152]{2,1,0:T(8,128)(2,1)}, u32[]{:S(2)}, u32[]{:S(2)}) %all-to-all-start.10) | async-done | bytes 2359328 | tf_op jit(solution)/shard_map/all_to_all | solution.py:57
  (385 shorter events, 127.8 us)
Async XLA Ops:
  7.2 9.2 %collective-permute-start.1 = (bf16[8,1024]{1,0:T(8,128)(2,1)}, bf16[8,1024]{1,0:T(8,128)(2,1)S(1)}, u32[]{:S(2)}, u32[]{:S(2)}) collective-permute-start(bf16[8,1024]{1,0:T(8,128)(2,1)} %param.29), channel_id=1, source_target_pairs={{0,1},{1,0},{2,3},{3,2},{4,5},{5,4},{6,7},{7,6},{8,9},{9,8},{10,11... | collective-permute-start | bytes 49160 | tf_op jit(solution)/shard_map/ppermute | solution.py:41
  8.7 7.7 %collective-permute-start.2 = (bf16[8,1024]{1,0:T(8,128)(2,1)}, bf16[8,1024]{1,0:T(8,128)(2,1)S(1)}, u32[]{:S(2)}, u32[]{:S(2)}) collective-permute-start(bf16[8,1024]{1,0:T(8,128)(2,1)} %param.29), channel_id=1, source_target_pairs={{0,2},{1,3},{2,0},{3,1},{4,6},{5,7},{6,4},{7,5},{8,10},{9,11},{10,... | collective-permute-start | bytes 49160 | tf_op jit(solution)/shard_map/ppermute | solution.py:41
  10.0 6.4 %collective-permute-start.3 = (bf16[8,1024]{1,0:T(8,128)(2,1)}, bf16[8,1024]{1,0:T(8,128)(2,1)S(1)}, u32[]{:S(2)}, u32[]{:S(2)}) collective-permute-start(bf16[8,1024]{1,0:T(8,128)(2,1)} %param.29), channel_id=1, source_target_pairs={{0,3},{1,2},{2,1},{3,0},{4,7},{5,6},{6,5},{7,4},{8,11},{9,10},{10,... | collective-permute-start | bytes 49160 | tf_op jit(solution)/shard_map/ppermute | solution.py:41
  16.4 43.9 %all-to-all-start = ((bf16[128,8,1152]{2,1,0:T(8,128)(2,1)}), bf16[128,8,1152]{2,1,0:T(8,128)(2,1)}, u32[]{:S(2)}, u32[]{:S(2)}) async-start(bf16[128,8,1152]{2,1,0:T(8,128)(2,1)} %weights.1), calls=%async_computation | async-start | bytes 4718592 | tf_op jit(solution)/shard_map/all_to_all | solution.py:57
  27.0 98.2 %all-gather.2.cloned.1.call-start = ((), (), s32[]{:S(2)}) async-start(), calls=%async_computation.13 | async-start | bytes 2162688 | tf_op jit(solution)/shard_map/all_gather | solution.py:498
  27.1 4.2 collective-permute-start
  69.4 24.0 %all-to-all-start.1 = ((bf16[32,160,128]{2,1,0:T(8,128)(2,1)}), bf16[32,160,128]{2,1,0:T(8,128)(2,1)S(1)}, u32[]{:S(2)}, u32[]{:S(2)}) async-start(bf16[32,160,128]{2,1,0:T(8,128)(2,1)} %copy-done.3), calls=%async_computation.1 | async-start | bytes 2621440 | tf_op jit(solution)/shard_map/all_to_all | solution.py:57
  105.0 17.0 %all-to-all-start.2 = ((bf16[32,32,128]{2,1,0:T(8,128)(2,1)}), bf16[32,32,128]{2,1,0:T(8,128)(2,1)S(1)}, u32[]{:S(2)}, u32[]{:S(2)}) async-start(bf16[32,32,128]{2,1,0:T(8,128)(2,1)} %get-tuple-element.49), calls=%async_computation.2 | async-start | bytes 524288 | tf_op jit(solution)/shard_map/all_to_all | solution.py:57
  114.3 12.4 %collective-permute-start.14 = (bf16[128,1024]{1,0:T(8,128)(2,1)}, bf16[128,1024]{1,0:T(8,128)(2,1)}, u32[]{:S(2)}, u32[]{:S(2)}) collective-permute-start(bf16[128,1024]{1,0:T(8,128)(2,1)} %bitcast.294), channel_id=1, source_target_pairs={{0,2},{1,3},{2,0},{3,1},{4,6},{5,7},{6,4},{7,5},{8,10},{9,11},{10,... | collective-permute-start | bytes 786440 | tf_op jit(solution)/shard_map/ppermute | solution.py:41
  115.0 33.3 %collective-permute-start.13 = (bf16[128,1024]{1,0:T(8,128)(2,1)}, bf16[128,1024]{1,0:T(8,128)(2,1)}, u32[]{:S(2)}, u32[]{:S(2)}) collective-permute-start(bf16[128,1024]{1,0:T(8,128)(2,1)} %bitcast.295), channel_id=1, source_target_pairs={{0,1},{1,0},{2,3},{3,2},{4,5},{5,4},{6,7},{7,6},{8,9},{9,8},{10,11... | collective-permute-start | bytes 786440 | tf_op jit(solution)/shard_map/ppermute | solution.py:41
  116.1 32.6 %collective-permute-start.11 = (bf16[256,512]{1,0:T(8,128)(2,1)}, bf16[256,512]{1,0:T(8,128)(2,1)}, u32[]{:S(2)}, u32[]{:S(2)}) collective-permute-start(bf16[256,512]{1,0:T(8,128)(2,1)} %bitcast.296), channel_id=1, source_target_pairs={{0,2},{1,3},{2,0},{3,1},{4,6},{5,7},{6,4},{7,5},{8,10},{9,11},{10,... | collective-permute-start | bytes 786440 | tf_op jit(solution)/shard_map/ppermute | solution.py:41
  117.5 33.1 %collective-permute-start.10 = (bf16[256,512]{1,0:T(8,128)(2,1)}, bf16[256,512]{1,0:T(8,128)(2,1)}, u32[]{:S(2)}, u32[]{:S(2)}) collective-permute-start(bf16[256,512]{1,0:T(8,128)(2,1)} %bitcast.297), channel_id=1, source_target_pairs={{0,1},{1,0},{2,3},{3,2},{4,5},{5,4},{6,7},{7,6},{8,9},{9,8},{10,11... | collective-permute-start | bytes 786440 | tf_op jit(solution)/shard_map/ppermute | solution.py:41
  122.7 4.4 %collective-permute-start.6 = (bf16[128,512]{1,0:T(8,128)(2,1)S(1)}, bf16[128,512]{1,0:T(8,128)(2,1)S(1)}, u32[]{:S(2)}, u32[]{:S(2)}) collective-permute-start(bf16[128,512]{1,0:T(8,128)(2,1)S(1)} %get-tuple-element.109), channel_id=1, source_target_pairs={{0,1},{1,0},{2,3},{3,2},{4,5},{5,4},{6,7},{7,6},{8,9},{9,8},{10,11... | collective-permute-start | bytes 393224 | tf_op jit(solution)/shard_map/ppermute | solution.py:41
  126.8 22.1 %collective-permute-start.8 = (bf16[256,512]{1,0:T(8,128)(2,1)}, bf16[256,512]{1,0:T(8,128)(2,1)}, u32[]{:S(2)}, u32[]{:S(2)}) collective-permute-start(bf16[256,512]{1,0:T(8,128)(2,1)} %bitcast.16), channel_id=1, source_target_pairs={{0,2},{1,3},{2,0},{3,1},{4,6},{5,7},{6,4},{7,5},{8,10},{9,11},{10,... | collective-permute-start | bytes 786440 | tf_op jit(solution)/shard_map/ppermute | solution.py:41
  127.1 22.1 %collective-permute-start.15 = (bf16[128,1024]{1,0:T(8,128)(2,1)}, bf16[128,1024]{1,0:T(8,128)(2,1)}, u32[]{:S(2)}, u32[]{:S(2)}) collective-permute-start(bf16[128,1024]{1,0:T(8,128)(2,1)} %collective-permute-done.14), channel_id=1, source_target_pairs={{0,1},{1,0},{2,3},{3,2},{4,5},{5,4},{6,7},{7,6},{8,9},{9,8},{10,11... | collective-permute-start | bytes 786440 | tf_op jit(solution)/shard_map/ppermute | solution.py:41
  131.8 35.9 %all-to-all-start.3 = ((bf16[32,32,1024]{2,1,0:T(8,128)(2,1)}), bf16[32,32,1024]{2,1,0:T(8,128)(2,1)}, u32[]{:S(2)}, u32[]{:S(2)}) async-start(bf16[32,32,1024]{2,1,0:T(8,128)(2,1)} %bitcast.275), calls=%async_computation.3 | async-start | bytes 4194304 | tf_op jit(solution)/shard_map/all_to_all | solution.py:57
  148.3 3.6 collective-permute-start.7
  148.8 3.1 collective-permute-start.9
  167.7 35.7 %all-to-all-start.4 = ((bf16[32,32,1024]{2,1,0:T(8,128)(2,1)}), bf16[32,32,1024]{2,1,0:T(8,128)(2,1)}, u32[]{:S(2)}, u32[]{:S(2)}) async-start(bf16[32,32,1024]{2,1,0:T(8,128)(2,1)} %bitcast.276), calls=%async_computation.4 | async-start | bytes 4194304 | tf_op jit(solution)/shard_map/all_to_all | solution.py:57
  203.4 34.6 %all-to-all-start.5 = ((bf16[32,32,1024]{2,1,0:T(8,128)(2,1)}), bf16[32,32,1024]{2,1,0:T(8,128)(2,1)}, u32[]{:S(2)}, u32[]{:S(2)}) async-start(bf16[32,32,1024]{2,1,0:T(8,128)(2,1)} %bitcast.281), calls=%async_computation.5 | async-start | bytes 4194304 | tf_op jit(solution)/shard_map/all_to_all | solution.py:57
  238.0 35.0 %all-to-all-start.6 = ((bf16[32,32,1024]{2,1,0:T(8,128)(2,1)}), bf16[32,32,1024]{2,1,0:T(8,128)(2,1)}, u32[]{:S(2)}, u32[]{:S(2)}) async-start(bf16[32,32,1024]{2,1,0:T(8,128)(2,1)} %bitcast.277), calls=%async_computation.6 | async-start | bytes 4194304 | tf_op jit(solution)/shard_map/all_to_all | solution.py:57
  246.1 152.4 %reduce-scatter.5.cloned.1.call-start = ((), (), s32[]{:S(2)}) async-start(), calls=%async_computation.15 | async-start | bytes 1310720 | tf_op jit(solution)/shard_map/reduce_scatter | solution.py:662
  246.4 2.1 collective-permute-start.16
  277.6 4.2 collective-permute-start.18
  280.8 12.7 %collective-permute-start.17 = (bf16[128,512]{1,0:T(8,128)(2,1)}, bf16[128,512]{1,0:T(8,128)(2,1)}, u32[]{:S(2)}, u32[]{:S(2)}) collective-permute-start(bf16[128,512]{1,0:T(8,128)(2,1)} %get-tuple-element.103), channel_id=1, source_target_pairs={{0,1},{1,0},{2,3},{3,2},{4,5},{5,4},{6,7},{7,6},{8,9},{9,8},{10,11... | collective-permute-start | bytes 393224 | tf_op jit(solution)/shard_map/ppermute | solution.py:41
  286.9 17.1 %all-to-all-start.7 = ((bf16[32,32,128]{2,1,0:T(8,128)(2,1)}), bf16[32,32,128]{2,1,0:T(8,128)(2,1)}, u32[]{:S(2)}, u32[]{:S(2)}) async-start(bf16[32,32,128]{2,1,0:T(8,128)(2,1)} %copy-done.8), calls=%async_computation.7 | async-start | bytes 524288 | tf_op jit(solution)/shard_map/all_to_all | solution.py:57
  304.0 34.6 %all-to-all-start.8 = ((bf16[128,8,640]{2,1,0:T(8,128)(2,1)}), bf16[128,8,640]{2,1,0:T(8,128)(2,1)}, u32[]{:S(2)}, u32[]{:S(2)}) async-start(bf16[128,8,640]{2,1,0:T(8,128)(2,1)} %bitcast.265), calls=%async_computation.8 | async-start | bytes 2621440 | tf_op jit(solution)/shard_map/all_to_all | solution.py:57
  338.6 29.1 %all-to-all-start.9 = ((bf16[32,160,128]{2,1,0:T(8,128)(2,1)}), bf16[32,160,128]{2,1,0:T(8,128)(2,1)S(1)}, u32[]{:S(2)}, u32[]{:S(2)}) async-start(bf16[32,160,128]{2,1,0:T(8,128)(2,1)} %copy-done.4), calls=%async_computation.9 | async-start | bytes 2621440 | tf_op jit(solution)/shard_map/all_to_all | solution.py:57
  348.5 55.3 %reduce-scatter.3.cloned.1.call-start = ((), (), s32[]{:S(2)}) async-start(), calls=%async_computation.14 | async-start | bytes 2621440 | tf_op jit(solution)/shard_map/reduce_scatter | solution.py:659
  373.1 3.1 collective-permute-start.19
  383.7 37.8 %all-to-all-start.10 = ((bf16[128,8,1152]{2,1,0:T(8,128)(2,1)}), bf16[128,8,1152]{2,1,0:T(8,128)(2,1)}, u32[]{:S(2)}, u32[]{:S(2)}) async-start(bf16[128,8,1152]{2,1,0:T(8,128)(2,1)} %bitcast.100), calls=%async_computation.10 | async-start | bytes 4718592 | tf_op jit(solution)/shard_map/all_to_all | solution.py:57
  395.9 4.4 %collective-permute-start.20 = (f32[128,1024]{1,0:T(8,128)}, f32[128,1024]{1,0:T(8,128)}, u32[]{:S(2)}, u32[]{:S(2)}) collective-permute-start(f32[128,1024]{1,0:T(8,128)} %slice.175), channel_id=1, source_target_pairs={{0,1},{1,0},{2,3},{3,2},{4,5},{5,4},{6,7},{7,6},{8,9},{9,8},{10,11... | collective-permute-start | bytes 1572872 | tf_op jit(solution)/shard_map/ppermute | solution.py:41
  (87 other events, 537.5 us)
Sparse Core Ops, SparseCore 0:
  31.6 90.3 all-gather.1
  287.1 21.0 reduce-scatter.4
  356.6 29.8 reduce-scatter.2
where the time goes:
time: 442 us; the launch traced here: 434 us
  waiting for transfers between devices  140 us (32%)
  starting transfers between devices  107 us (24%)
  matrix products  54.6 us (12%)
  Pallas kernels  42.5 us (10%)
  local copies, waits for them, and re-layouts  39.9 us (9%)
  other arithmetic  34.4 us (8%)
  between operations  15.5 us (4%)
    all_to_all x11, waiting for transfers between devices, exchange(): return lax.all_to_all(array, axis, split_axis=0, concat_axis=0, tiled=True)  137 us
    all_to_all x11, starting transfers between devices, exchange(): return lax.all_to_all(array, axis, split_axis=0, concat_axis=0, tiled=True)  86.1 us
    dot_general x22, matrix products, dot(): return lax.dot_general(a, b, (dims, ((), ())), preferred_element_type=F32)  54.6 us
    pallas_call x1, Pallas kernels, attend_back(): pl.pallas_call(backward_kernel, grid=(TILES,), in_specs=[whole((N_CTX, PA...  25.1 us
    ppermute x21, starting transfers between devices, swap(): lax.ppermute(array, 'fsdp', [(i, i ^ j) for i in range(4)])  20.5 us
    unnamed x169, local copies, waits for them, and re-layouts  20 us
    pallas_call x1, Pallas kernels, attend(): pl.pallas_call(forward_kernel, in_specs=[vmem] * 3, out_specs=[vmem, pl.B...  10.1 us
  transfers between devices with their start and end apart: 35, of which 14 were waited for; matrix products, arithmetic and copies ran while one was open for 23% of the time, Pallas kernels for 10%

commit v1 on v0

--- a/solution.py
+++ b/solution.py
@@ -29,6 +29,7 @@
 KEYS = N_CTX * TOK
 QUERIES = KEYS // QUARTERS
 KEY_TILE = 512
+VMEM_LIMIT = 62 << 20
 TOK_TILE = 128
 TILES = QUERIES // TOK_TILE
 
@@ -68,7 +69,7 @@
     return jnp.where(first, up, down)
 
 
-def call(kernel, inputs, outputs, name, micros=2, mib=12):
+def call_near(kernel, inputs, outputs, name, micros=2, mib=12):
     vmem = pl.BlockSpec(memory_space=pltpu.VMEM)
     return pl.pallas_call(
         kernel,
@@ -81,14 +82,109 @@
     )(*inputs)
 
 
+class Held:
+    def __init__(self, buffer, copy):
+        self.buffer, self.copy = buffer, copy
+
+    def wait(self):
+        if self.copy is not None:
+            self.copy.wait()
+            self.copy = None
+
+    def __getitem__(self, index):
+        self.wait()
+        return self.buffer[index]
+
+
+class Made:
+    def __init__(self, buffer, target, sems, first):
+        self.buffer, self.target, self.sems, self.first = buffer, target, sems, first
+        self.copies = []
+
+    def __getitem__(self, index):
+        return self.buffer[index]
+
+    def __setitem__(self, index, value):
+        self.buffer[index] = value
+
+    def send(self, rows=None):
+        source, target = self.buffer, self.target
+        if rows is not None:
+            source, target = source.at[rows], target.at[rows]
+        copy = pltpu.make_async_copy(source, target, self.sems.at[self.first + len(self.copies)])
+        copy.start()
+        self.copies.append(copy)
+
+
+SENDS = 4
+
+
+def far(array, rows=None, at=None, cut=None):
+    return (array, rows, at, cut)
+
+
+def call(kernel, inputs, outputs, name, micros=2, ids=None):
+    hbm = pl.BlockSpec(memory_space=pltpu.HBM)
+    inputs = [i if isinstance(i, tuple) else far(i) for i in inputs]
+    scratch = []
+    for array, rows, _, part in inputs:
+        shape = array.shape if rows is None else (rows, *array.shape[1:])
+        if part is not None:
+            shape = tuple(p.stop - p.start for p in part) + array.shape[len(part) :]
+        scratch.append(pltpu.VMEM(shape, array.dtype))
+    scratch += [pltpu.VMEM(shape, dtype) for shape, dtype in outputs]
+    scratch.append(pltpu.SemaphoreType.DMA((len(inputs) + SENDS * len(outputs),)))
+    numbers = [] if ids is None else [ids]
+
+    def body(*refs):
+        refs = list(refs)
+        own_ids = refs.pop(0) if numbers else None
+        ins, outs = refs[: len(inputs)], refs[len(inputs) : len(inputs) + len(outputs)]
+        buffers = refs[len(inputs) + len(outputs) :]
+        sems = buffers[-1]
+        given, results = [], []
+        for k, (ref, (_, rows, at, part)) in enumerate(zip(ins, inputs)):
+            if rows is not None:
+                ref = ref.at[pl.ds(pl.multiple_of(own_ids[at] * rows, rows), rows)]
+            elif part is not None:
+                ref = ref.at[part]
+            copy = pltpu.make_async_copy(ref, buffers[k], sems.at[k])
+            copy.start()
+            given.append(Held(buffers[k], copy))
+        for k, ref in enumerate(outs):
+            results.append(Made(buffers[len(inputs) + k], ref, sems, len(inputs) + SENDS * k))
+        kernel(*([own_ids] if numbers else []), *given, *results)
+        for held in given:
+            held.wait()
+        for made in results:
+            if not made.copies:
+                made.send()
+        for made in results:
+            for copy in made.copies:
+                copy.wait()
+
+    return pl.pallas_call(
+        body,
+        in_specs=[pl.BlockSpec(memory_space=pltpu.SMEM)] * len(numbers) + [hbm] * len(inputs),
+        out_specs=[hbm] * len(outputs),
+        out_shape=[jax.ShapeDtypeStruct(shape, dtype) for shape, dtype in outputs],
+        scratch_shapes=scratch,
+        compiler_params=pltpu.CompilerParams(vmem_limit_bytes=VMEM_LIMIT),
+        cost_estimate=estimate(micros),
+        name=name,
+    )(*numbers, *[i[0] for i in inputs])
+
+
 def estimate(micros):
     return pl.CostEstimate(flops=int(micros * 1.1e9), bytes_accessed=1 << 16, transcendentals=0)
 
 
-def weights_kernel(w_query, w_key, w_value, w_router, gains, segments, out):
+def weights_kernel(w_query, w_key, w_value, w_router, attn, query, ffn, key, segments, out):
     row = lax.broadcasted_iota(jnp.int32, (8, 128), 0)
     lane = lanes((8, 128))
     middle = (lane >= 32) & (lane < 96)
+    gains = [line[...].astype(F32) for line in (attn, query, ffn, key)]
+    gains = jnp.concatenate(gains + [jnp.zeros((1, 100), F32)], axis=1)
     seg = segments[...]
     low, high = (seg & 255).astype(F32), (seg >> 8).astype(F32)
     small = jnp.zeros((8, 128), F32)
@@ -100,7 +196,7 @@
     )
     for r, line in enumerate(lines):
         small = jnp.where((row == r + 1) & middle, line, small)
-    small = jnp.where((row == 0) & (lane >= 32), pltpu.roll(gains[...], 32, 1), small)
+    small = jnp.where((row == 0) & (lane >= 32), pltpu.roll(gains, 32, 1), small)
     router = jnp.concatenate([w_router[...].astype(F32), jnp.zeros((8, 96), F32)], axis=1)
     small = jnp.where(lane < 32, router, small)
     parts = []
@@ -136,12 +232,17 @@
                 out[to, TOK + 16 : TOK + 32, :] = q[64 + qd * 16 : 64 + qd * 16 + 16]
 
 
-def unpack_kernel(grads_q, qkv, scale_q, scale_k, gain, cosine, sine, out, sums, gain_grad):
-    grads = grads_q
+def other_rows(value):
+    return jnp.concatenate([value[TOK:], value[:TOK]], axis=0)
+
+
+def unpack_kernel(grads, qkv, scales, gains, cosine, sine, out, sums, gain_grad):
+    gain = gains[0:1, :]
+    lines = [None] * (2 * PART_HEADS)
     for j in range(PARTS):
         rows = slice(j * TOK, (j + 1) * TOK)
-        turn_c, turn_s = cosine[rows], sine[rows]
-        cq, ck = scale_q[rows], scale_k[rows]
+        turn_c, turn_s = cosine[rows, :], sine[rows, :]
+        cq, ck = scales[rows, 0:1], scales[rows, 1:2]
         sum_q = jnp.zeros((TOK, 128), F32)
         sum_k = jnp.zeros((TOK, 128), F32)
         for h in range(PART_HEADS):
@@ -168,17 +269,48 @@
             out[rows, at + 128 : at + 256] = dkv * g_k
             sum_q = sum_q + through_q * g_q
             sum_k = sum_k + through_k * g_k
-            line_q = jnp.sum(through_q, axis=0, keepdims=True)
-            line_k = jnp.sum(through_k, axis=0, keepdims=True)
-            if j == 0:
-                gain_grad[:, at : at + 128] = line_q
-                gain_grad[:, at + 128 : at + 256] = line_k
-            else:
-                gain_grad[:, at : at + 128] += line_q
-                gain_grad[:, at + 128 : at + 256] += line_k
+            for k, through in enumerate((through_q, through_k)):
+                line = jnp.sum(through, axis=0, keepdims=True)
+                known = lines[2 * h + k]
+                lines[2 * h + k] = line if known is None else known + line
+        out.send(rows)
         total_q = jnp.sum(sum_q, axis=1, keepdims=True)
         total_k = jnp.sum(sum_k, axis=1, keepdims=True)
         sums[rows, :] = jnp.where(lanes((TOK, 128)) == 0, total_q, total_k)
+    gain_grad[...] = jnp.broadcast_to(jnp.concatenate(lines, axis=1), (8, COLS))
+
+
+def finish_kernel(ids, through, qkv, scales, sums, sums_other, normed, weights, tokens, gain_grad, last, grad_normed):
+    total = sums[...] + other_rows(sums_other[...])
+    lane = lanes((TOK, COLS)) % 256
+    is_q, is_k = lane < 128, (lane >= 128) & (lane < 192)
+    grads = []
+    for j in range(PARTS):
+        rows = slice(j * TOK, (j + 1) * TOK)
+        scale = jnp.where(is_q, scales[rows, 0:1], jnp.where(is_k, scales[rows, 1:2], 1.0))
+        mean = jnp.where(is_q, total[rows, 0:1] / 1024, jnp.where(is_k, total[rows, 1:2] / 512, 0.0))
+        grads.append((scale * (through[rows, :] - qkv[rows, :] * scale * mean)).astype(BF))
+    grad = jnp.concatenate(grads, axis=0)
+    normed_grad = dot(grad, weights[:, :COLS], ((1,), (1,)))
+    grad_normed[...] = normed_grad
+    grad_normed.send()
+    value = tokens[...].astype(F32)
+    products = (normed_grad * (value * inverse_rms(value))).astype(BF)
+    ones = jnp.where(lanes((ROWS, 128)) == 64, 1.0, 0.0).astype(BF)
+    last[:, COLS:] = dot(products, ones, ((0,), (0,))).astype(BF)
+    row = lax.broadcasted_iota(jnp.int32, (TOK, TOK), 0) % 8
+    for h in range(PART_HEADS):
+        query, key = [gain_grad[0:1, h * 256 + k : h * 256 + k + 128] for k in (0, 128)]
+        block = jnp.where(row == 0, query, jnp.where(row == 1, key, 0.0))
+        block = jnp.where(row == 2, pltpu.roll(query, HD, 1), block)
+        at = pl.ds(pl.multiple_of(ids[0] * FEATURES + h * TOK, TOK), TOK)
+        known = last[at, COLS:].astype(F32)
+        last[at, COLS:] = jnp.where(lanes((TOK, TOK)) < HD, block, known).astype(BF)
+    tile = D // SENDS
+    for t in range(SENDS):
+        rows = slice(t * tile, (t + 1) * tile)
+        last[rows, :COLS] = dot(normed[:, rows], grad, ((0,), (0,))).astype(BF)
+        last.send(rows)
 
 
 def heads_in_kernel(received, out):
@@ -200,24 +332,6 @@
                 columns = slice(h * 128, h * 128 + 128)
                 out[to, :16] = refs[j][qd * 16 : qd * 16 + 16, columns]
                 out[to, 16:] = refs[j][64 + qd * 16 : 80 + qd * 16, columns]
-
-
-def finish_kernel(through, qkv, scale_q, scale_k, sum_q, sum_k, normed, proj, scaled_in, small, last, grad_normed):
-    lane = lanes((TOK, COLS)) % 256
-    is_q, is_k = lane < 128, (lane >= 128) & (lane < 192)
-    grads = []
-    for j in range(PARTS):
-        rows = slice(j * TOK, (j + 1) * TOK)
-        scale = jnp.where(is_q, scale_q[rows], jnp.where(is_k, scale_k[rows], 1.0))
-        mean = jnp.where(is_q, sum_q[rows] / 1024, jnp.where(is_k, sum_k[rows] / 512, 0.0))
-        grads.append((scale * (through[rows, :] - qkv[rows, :] * scale * mean)).astype(BF))
-    grad = jnp.concatenate(grads, axis=0)
-    normed_grad = dot(grad, proj[...], ((1,), (1,)))
-    grad_normed[...] = normed_grad
-    products = (normed_grad * scaled_in[...]).astype(BF)
-    ones = jnp.where(lanes((ROWS, 128)) == 64, 1.0, 0.0).astype(BF)
-    last[:, :COLS] = dot(normed[...], grad, ((0,), (0,))).astype(BF)
-    last[:, COLS:] = (small[...].astype(F32) + dot(products, ones, ((0,), (0,)))).astype(BF)
 
 
 def finish_out_kernel(attended, branch, routed, logits, products, out):
@@ -470,29 +584,24 @@
     part = fsdp % PARTS
     both_axes = ("ctx", "fsdp")
 
-    gains = jnp.concatenate([attn_norm, query_norm, ffn_norm, key_norm, jnp.zeros((100,), BF)])
+    small_lines = [line[None] for line in (attn_norm, query_norm, ffn_norm, key_norm)]
     outgoing_w = call(
         weights_kernel,
-        (w_query, w_key, w_value, w_router, gains.astype(F32)[None], segment_ids),
-        [((4 * N_CTX, 8, COLS + 128), BF, True)],
+        (w_query, w_key, w_value, w_router, *small_lines, segment_ids),
+        [((4 * N_CTX, 8, COLS + 128), BF)],
         "weights",
     )[0]
     out_rows, outgoing_w = lax.optimization_barrier(
         ([swap(w_out, j) for j in range(4)], outgoing_w)
     )
     gathered = exchange(outgoing_w, both_axes)
-    small = gathered[:, :, COLS:]
+    part_ids = jnp.stack([part ^ j for j in range(PARTS)]).astype(jnp.int32)
 
     tokens = hidden_in[0]
     order = block_order[0]
     blocks = lax.dynamic_slice_in_dim(order, place * 2, 2)
-    if PARTS == 2:
-        tokens_all = [tokens, swap(tokens, 1)]
-        blocks_all = [blocks, swap(blocks, 1)]
-    else:
-        far, far_blocks = swap(tokens, 2), swap(blocks, 2)
-        tokens_all = [tokens, swap(tokens, 1), far, swap(far, 1)]
-        blocks_all = [blocks, swap(blocks, 1), far_blocks, swap(far_blocks, 1)]
+    tokens_all = [tokens, swap(tokens, 1)]
+    blocks_all = [blocks, swap(blocks, 1)]
     tokens_all = jnp.concatenate(tokens_all, axis=0)
 
     proj_out = lax.all_gather(in_order(out_rows, fsdp), "ctx", axis=0, tiled=True)
@@ -519,6 +628,10 @@
     sine = jnp.sin(turned)
     sine = jnp.concatenate([-sine, sine, -sine, sine], axis=1)
 
+    inputs_all = tokens_all.astype(F32)
+    scale_in = inverse_rms(inputs_all)
+    scaled_in = inputs_all * scale_in
+    small = gathered[:, :, COLS:]
     lines = small[:, 0, 32:60].astype(F32)
     gain_attn = lines[:, 0:8].reshape(1, D)
     gain_query = lines[:, 8:16].reshape(D)
@@ -534,12 +647,10 @@
         ],
         axis=1,
     ).reshape(1, COLS)
-    proj = gathered[:, :, :COLS].reshape(D, COLS)
+    weights = gathered.reshape(D, COLS + 128)
+    proj = weights[:, :COLS]
     proj_router = small[:, :, :EXPERTS].reshape(D, EXPERTS)
 
-    inputs_all = tokens_all.astype(F32)
-    scale_in = inverse_rms(inputs_all)
-    scaled_in = inputs_all * scale_in
     normed_low = (scaled_in * gain_attn).astype(BF)
     qkv = dot(normed_low, proj)
     lane = jnp.arange(COLS)[None] % 256
@@ -554,13 +665,15 @@
     square_sums = sum_parts(square_sums.reshape(2, PARTS, TOK)).reshape(2, ROWS)
     scale_q = lax.rsqrt(square_sums[0] / 1024 + EPSILON)[:, None]
     scale_k = lax.rsqrt(square_sums[1] / 512 + EPSILON)[:, None]
-    packed = call(
+    packed = call_near(
         pack_kernel,
         (qkv, scale_q, scale_k, gain_heads, cosine, sine),
         [((N_CTX, PACK, 128), BF, True)],
         "pack",
     )[0]
     packed = exchange(packed, "ctx")
+    scales = jnp.where(jnp.arange(128)[None] == 0, scale_q, scale_k)
+    gains = jnp.broadcast_to(gain_heads, (8, COLS))
 
     sequence = fsdp ^ (place // (N_CTX // PARTS))
     seg_small = lax.dynamic_index_in_dim(
@@ -582,7 +695,7 @@
 
     mixed, mixed_low, lse = attend(packed, seg_all, seg_query)
     returned = exchange(mixed_low, "ctx")
-    returned = call(heads_in_kernel, (returned,), [((PARTS, TOK, FEATURES), BF, False)], "heads_in", 1)[0]
+    returned = call_near(heads_in_kernel, (returned,), [((PARTS, TOK, FEATURES), BF, False)], "heads_in", 1)[0]
     pieces = swapped([returned[j] for j in range(PARTS)])
     out_parts = proj_out.reshape(PARTS, FEATURES, D)
     out_parts = [
@@ -629,6 +742,17 @@
     produced_home, grad_rows = lax.optimization_barrier((produced_home, grad_rows))
     grad_home = exchange(grad_rows, "ctx").reshape(EXPERTS * CAP, D)
 
+    grad_gate_w = dot(arrived, grad_gate_act, ((0,), (0,))).astype(BF)
+    grad_up_w = dot(arrived, grad_up_act, ((0,), (0,))).astype(BF)
+    grad_down_w = dot(inner, arrived_grad, ((0,), (0,))).astype(BF)
+    grad_gate_up = jnp.stack([grad_gate_w, grad_up_w])
+    grad_home, grad_down_w, grad_gate_up = lax.optimization_barrier(
+        (grad_home, grad_down_w, grad_gate_up)
+    )
+    grad_down = lax.psum_scatter(
+        grad_down_w[None], "fsdp", scatter_dimension=1, tiled=True
+    ).astype(F32)
+
     share = share.reshape(EXPERTS * CAP, TOK)
     share_high = share.astype(BF)
     share_low = (share - share_high.astype(F32)).astype(BF)
@@ -647,21 +771,10 @@
     )
     grad_branch = grad_middle.astype(BF)
     grad_mixed = [dot(grad_branch, out_part, ((1,), (1,))).astype(BF) for out_part in out_parts]
-    upper = call(
+    upper = call_near(
         heads_out_kernel, tuple(swapped(grad_mixed)), [((N_CTX, 32, 128), BF, True)], "heads_out", 1
     )[0]
-    upper, arrived, arrived_grad = lax.optimization_barrier((upper, arrived, arrived_grad))
     upper = exchange(upper, "ctx")
-
-    grad_gate_w = dot(arrived, grad_gate_act, ((0,), (0,))).astype(BF)
-    grad_up_w = dot(arrived, grad_up_act, ((0,), (0,))).astype(BF)
-    grad_down_w = dot(inner, arrived_grad, ((0,), (0,))).astype(BF)
-    grad_gate_up = lax.psum_scatter(
-        jnp.stack([grad_gate_w, grad_up_w]), "fsdp", scatter_dimension=1, tiled=True
-    ).astype(F32)
-    grad_down = lax.psum_scatter(
-        grad_down_w[None], "fsdp", scatter_dimension=1, tiled=True
-    ).astype(F32)
 
     sorted_pieces = jnp.stack(pieces)
     attended = jnp.concatenate(
@@ -676,7 +789,7 @@
     own_half = lax.dynamic_index_in_dim(branch_halves, core, keepdims=False)
     other_half = lax.dynamic_index_in_dim(branch_halves, 1 - core, keepdims=False)
     branch_2 = jnp.concatenate([own_half, swap(other_half, 1)], axis=0)
-    late = call(
+    late = call_near(
         finish_out_kernel,
         (
             attended_2,
@@ -692,54 +805,42 @@
     first_sums = exchange(late.reshape(4 * N_CTX, 8, 640), both_axes)
 
     grads_home = attend_back(packed, seg_all, seg_query, upper, mixed, lse)
-    grads_home, first_sums = lax.optimization_barrier((grads_home, first_sums))
+    grads_home, first_sums, grad_gate_up = lax.optimization_barrier(
+        (grads_home, first_sums, grad_gate_up)
+    )
+    grad_gate_up = lax.psum_scatter(
+        grad_gate_up, "fsdp", scatter_dimension=1, tiled=True
+    ).astype(F32)
     grads_home = exchange(grads_home, "ctx")
 
-    through_heads, sums, grad_gain_heads = call(
+    through_heads, sums, gain_grad = call(
         unpack_kernel,
-        (grads_home, qkv, scale_q, scale_k, gain_heads, cosine, sine),
-        [((ROWS, COLS), F32, False), ((ROWS, 128), F32, False), ((1, COLS), F32, False)],
+        (grads_home, qkv, scales, gains, cosine, sine),
+        [((ROWS, COLS), F32), ((ROWS, 128), F32), ((8, COLS), F32)],
         "unpack",
     )
-    sums = sum_parts(sums[:, :2].T.reshape(2, PARTS, TOK)).reshape(2, ROWS)
-    gain_lines = grad_gain_heads.reshape(PART_HEADS, 256)
-    query_line = gain_lines[:, :128].reshape(FEATURES)
-    key_line = gain_lines[:, 128:192].reshape(FEATURES // 2)
-    query_line = lax.dynamic_update_slice_in_dim(
-        jnp.zeros((1024,), F32), query_line, part * FEATURES, 0
-    )
-    key_line = lax.dynamic_update_slice_in_dim(
-        jnp.zeros((512,), F32), key_line, part * FEATURES // 2, 0
-    )
-    small_grads = jnp.concatenate([query_line.reshape(128, 8), key_line.reshape(128, 4)], axis=1)
-    small_grads = jnp.pad(small_grads.astype(BF)[:, None, :], ((0, 0), (0, 7), (0, 116)))
     last, grad_normed = call(
         finish_kernel,
         (
             through_heads,
             qkv,
-            scale_q,
-            scale_k,
-            sums[0][:, None],
-            sums[1][:, None],
+            scales,
+            sums,
+            swap(sums, 1),
             normed_low,
-            proj,
-            scaled_in,
-            small_grads.reshape(D, 128),
+            weights,
+            tokens_all,
+            gain_grad,
         ),
-        [((D, COLS + 128), BF, True), ((ROWS, D), F32, False)],
+        [((D, COLS + 128), BF), ((ROWS, D), F32)],
         "finish",
-        3,
-        24,
+        4,
+        part_ids,
     )
     last_sums = exchange(last.reshape(4 * N_CTX, 8, COLS + 128), both_axes)
 
     grad_normed = grad_normed.reshape(PARTS, TOK, D)
-    if PARTS == 4:
-        grad_normed = grad_normed.astype(BF)
-    grad_normed = sum(
-        piece.astype(F32) for piece in swapped([grad_normed[j] for j in range(PARTS)])
-    )
+    grad_normed = sum(swapped([grad_normed[j] for j in range(PARTS)]))
     through_in = grad_normed * gain_attn
     scaled_own = scaled_in[:TOK]
     input_grad = grad_middle + scale_in[:TOK] * (
@@ -755,6 +856,11 @@
     heads_g = last_sums[:, :, :COLS].reshape(PARTS, 8, PART_HEADS, 256)
     heads_g = jnp.transpose(heads_g, (1, 0, 2, 3))
     last_small = jnp.sum(last_sums[:, :, COLS:], axis=0)
+    index = 4 * place + fsdp
+    query_gain = lax.dynamic_slice(
+        last_small, (index % 16 // 8 * 2, index % 8 * 8), (1, 8)
+    ).reshape(8)
+    key_gain = lax.dynamic_slice(last_small, (1, index % 16 * 4), (1, 4)).reshape(4)
     return (
         layer_out,
         input_grad[None],
@@ -762,8 +868,8 @@
         heads_g[..., :128].reshape(8, 1024),
         heads_g[..., 128:192].reshape(8, 512),
         heads_g[..., 192:].reshape(8, 512),
-        last_small[0, 0:8],
-        last_small[0, 8:12],
+        query_gain,
+        key_gain,
         grad_out,
         first_small[:, 64],
         first_small[:, :EXPERTS],

time: 442 us -> 430 us (0.973)
  local copies, waits for them, and re-layouts: 39.9 us -> 18.5 us
  Pallas kernels: 42.5 us -> 53.2 us
  waiting for transfers between devices: 140 us -> 146 us
    unnamed x169 -> x115, local copies, waits for them, and re-layouts: 20 us -> 4.98 us
    pallas_call x7, Pallas kernels: 7.18 us -> 17.6 us  [the longest x3 13.1 us: call(): pl.pallas_call(body, in_specs=[pl.BlockSpec(memory_space=pltpu.SMEM)] * l...]
    all_to_all x11, waiting for transfers between devices: 137 us -> 143 us  [exchange(): return lax.all_to_all(array, axis, split_axis=0, concat_axis=0, tiled=True)]
  transfers between devices with their start and end apart: 35 -> 35, of which waited for: 14 -> 14; matrix products, arithmetic and copies ran while one was open for 23% -> 22% of each run, Pallas kernels for 10% -> 13%
where the time goes in v1:
time: 430 us; the launch traced here: 424 us
  waiting for transfers between devices  146 us (34%)
  starting transfers between devices  105 us (24%)
  matrix products  54.7 us (13%)
  Pallas kernels  53.2 us (12%)
  other arithmetic  30.8 us (7%)
  local copies, waits for them, and re-layouts  18.5 us (4%)
  between operations  15.4 us (4%)
    all_to_all x11, waiting for transfers between devices, exchange(): return lax.all_to_all(array, axis, split_axis=0, concat_axis=0, tiled=True)  143 us
    all_to_all x11, starting transfers between devices, exchange(): return lax.all_to_all(array, axis, split_axis=0, concat_axis=0, tiled=True)  82.9 us
    dot_general x22, matrix products, dot(): return lax.dot_general(a, b, (dims, ((), ())), preferred_element_type=F32)  54.7 us
    pallas_call x1, Pallas kernels, attend_back(): pl.pallas_call(backward_kernel, grid=(TILES,), in_specs=[whole((N_CTX, PA...  25.4 us
    ppermute x21, starting transfers between devices, swap(): lax.ppermute(array, 'fsdp', [(i, i ^ j) for i in range(4)])  21.5 us
    pallas_call x3, Pallas kernels, call(): pl.pallas_call(body, in_specs=[pl.BlockSpec(memory_space=pltpu.SMEM)] * l...  13.1 us
    pallas_call x1, Pallas kernels, attend(): pl.pallas_call(forward_kernel, in_specs=[vmem] * 3, out_specs=[vmem, pl.B...  10.2 us
  transfers between devices with their start and end apart: 35, of which 14 were waited for; matrix products, arithmetic and copies ran while one was open for 22% of the time, Pallas kernels for 13%

profile of v1, /device:TPU:1, one launch (start us, length us, event | category | flops | bytes accessed | tf_op | source)
XLA Modules:
  0.0 423.5 jit_solution(2223596168539190225)
XLA Ops:
  13.4 10.1 %all-to-all-start = ((bf16[128,8,1152]{2,1,0:T(8,128)(2,1)}), bf16[128,8,1152]{2,1,0:T(8,128)(2,1)S(1)}, u32[]{:S(2)}, u32[]{:S(2)}) async-start(bf16[128,8,1152]{2,1,0:T(8,128)(2,1)} %weights.1), calls=%async_computation | async-start | bytes 4718592 | tf_op jit(solution)/shard_map/all_to_all | solution.py:58
  27.9 29.1 %all-to-all-done = bf16[128,8,1152]{2,1,0:T(8,128)(2,1)S(1)} async-done(((bf16[128,8,1152]{2,1,0:T(8,128)(2,1)}), bf16[128,8,1152]{2,1,0:T(8,128)(2,1)S(1)}, u32[]{:S(2)}, u32[]{:S(2)}) %all-to-all-start) | async-done | bytes 2359328 | tf_op jit(solution)/shard_map/all_to_all | solution.py:58
  66.7 4.3 %all-to-all-start.1 = ((bf16[32,160,128]{2,1,0:T(8,128)(2,1)}), bf16[32,160,128]{2,1,0:T(8,128)(2,1)S(1)}, u32[]{:S(2)}, u32[]{:S(2)}) async-start(bf16[32,160,128]{2,1,0:T(8,128)(2,1)} %pack.1), calls=%async_computation.1 | async-start | bytes 2621440 | tf_op jit(solution)/shard_map/all_to_all | solution.py:58
  75.3 15.0 %all-to-all-done.1.packed = bf16[32,160,128]{2,1,0:T(8,128)(2,1)S(1)} async-done(((bf16[32,160,128]{2,1,0:T(8,128)(2,1)}), bf16[32,160,128]{2,1,0:T(8,128)(2,1)S(1)}, u32[]{:S(2)}, u32[]{:S(2)}) %all-to-all-start.1) | async-done | bytes 1310752 | tf_op jit(solution)/shard_map/all_to_all | solution.py:58
  90.3 10.2 %attend.1 = (f32[1024,128]{1,0:T(8,128)S(1)}, bf16[32,32,128]{2,1,0:T(8,128)(2,1)}, f32[8,1,256]{2,1,0:T(1,128)S(1)}) custom-call(bf16[32,160,128]{2,1,0:T(8,128)(2,1)S(1)} %all-to-all-done.1.packed, s32[32,128]{1,0:T(8,128)S(1)} %copy.119.seg_key, s32[8,1,128]{2,1,0:T(1,128)S(1)} %bitcast.255), custom_call_target="tpu_custom_call" | custom-call | flops 13200000000 | bytes 65536 | tf_op jit(solution)/shard_map/attend/pallas_call | solution.py:496
  100.5 7.5 %all-to-all-start.2 = ((bf16[32,32,128]{2,1,0:T(8,128)(2,1)}), bf16[32,32,128]{2,1,0:T(8,128)(2,1)S(1)}, u32[]{:S(2)}, u32[]{:S(2)}) async-start(bf16[32,32,128]{2,1,0:T(8,128)(2,1)} %get-tuple-element.50), calls=%async_computation.2 | async-start | bytes 524288 | tf_op jit(solution)/shard_map/all_to_all | solution.py:58
  112.7 4.7 %all-to-all-done.2.received = bf16[32,32,128]{2,1,0:T(8,128)(2,1)S(1)} async-done(((bf16[32,32,128]{2,1,0:T(8,128)(2,1)}), bf16[32,32,128]{2,1,0:T(8,128)(2,1)S(1)}, u32[]{:S(2)}, u32[]{:S(2)}) %all-to-all-start.2) | async-done | bytes 262176 | tf_op jit(solution)/shard_map/all_to_all | solution.py:58
  127.3 7.8 %all-to-all-start.3 = ((bf16[32,32,1024]{2,1,0:T(8,128)(2,1)}), bf16[32,32,1024]{2,1,0:T(8,128)(2,1)}, u32[]{:S(2)}, u32[]{:S(2)}) async-start(bf16[32,32,1024]{2,1,0:T(8,128)(2,1)} %bitcast.264), calls=%async_computation.3 | async-start | bytes 4194304 | tf_op jit(solution)/shard_map/all_to_all | solution.py:58
  148.2 14.1 %all-to-all-done.3 = bf16[32,32,1024]{2,1,0:T(8,128)(2,1)} async-done(((bf16[32,32,1024]{2,1,0:T(8,128)(2,1)}), bf16[32,32,1024]{2,1,0:T(8,128)(2,1)}, u32[]{:S(2)}, u32[]{:S(2)}) %all-to-all-start.3) | async-done | bytes 2097184 | tf_op jit(solution)/shard_map/all_to_all | solution.py:58
  162.3 9.3 %all-to-all-start.4 = ((bf16[32,32,1024]{2,1,0:T(8,128)(2,1)}), bf16[32,32,1024]{2,1,0:T(8,128)(2,1)}, u32[]{:S(2)}, u32[]{:S(2)}) async-start(bf16[32,32,1024]{2,1,0:T(8,128)(2,1)} %bitcast.263), calls=%async_computation.4 | async-start | bytes 4194304 | tf_op jit(solution)/shard_map/all_to_all | solution.py:58
  171.9 3.2 fusion.76
  175.1 5.1 %multiply_convert_fusion.3 = (bf16[1024,512]{1,0:T(8,128)(2,1)S(1)}, f32[1024,512]{1,0:T(8,128)}) fusion(f32[1024,512]{1,0:T(8,128)S(1)} %fusion.76, bf16[1024,1024]{1,0:T(8,128)(2,1)} %bitcast.44, bf16[1024,512]{1,0:T(8,128)(2,1)S(1)} %copy-done.14), kind=kOutput, calls=%fused_computation.9 | convolution fusion | flops 1076887552 | bytes 8388608 | tf_op jit(solution)/shard_map/dot_general | solution.py:38
  183.8 14.5 %all-to-all-done.4 = bf16[32,32,1024]{2,1,0:T(8,128)(2,1)} async-done(((bf16[32,32,1024]{2,1,0:T(8,128)(2,1)}), bf16[32,32,1024]{2,1,0:T(8,128)(2,1)}, u32[]{:S(2)}, u32[]{:S(2)}) %all-to-all-start.4) | async-done | bytes 2097184 | tf_op jit(solution)/shard_map/all_to_all | solution.py:58
  198.4 7.9 %all-to-all-start.5 = ((bf16[32,32,1024]{2,1,0:T(8,128)(2,1)}), bf16[32,32,1024]{2,1,0:T(8,128)(2,1)}, u32[]{:S(2)}, u32[]{:S(2)}) async-start(bf16[32,32,1024]{2,1,0:T(8,128)(2,1)} %bitcast.274), calls=%async_computation.5 | async-start | bytes 4194304 | tf_op jit(solution)/shard_map/all_to_all | solution.py:58
  209.7 5.2 %multiply_convert_fusion.1 = (bf16[1024,512]{1,0:T(8,128)(2,1)S(1)}, bf16[1024,512]{1,0:T(8,128)(2,1)S(1)}) fusion(f32[1024,512]{1,0:T(8,128)} %copy-done.55, f32[1024,512]{1,0:T(8,128)} %get-tuple-element.140, bf16[1024,1024]{1,0:T(8,128)(2,1)} %bitcast.73, bf16[512,1024]{1,0:T(8,128)(2,1)} %pad_maximum_fusion.6), kind=kOutput, calls=%fused_computation.7 | convolution fusion | flops 1080557568 | bytes 9437184 | tf_op jit(solution)/shard_map/dot_general | solution.py:38
  219.5 13.4 %all-to-all-done.5 = bf16[32,32,1024]{2,1,0:T(8,128)(2,1)} async-done(((bf16[32,32,1024]{2,1,0:T(8,128)(2,1)}), bf16[32,32,1024]{2,1,0:T(8,128)(2,1)}, u32[]{:S(2)}, u32[]{:S(2)}) %all-to-all-start.5) | async-done | bytes 2097184 | tf_op jit(solution)/shard_map/all_to_all | solution.py:58
  232.9 8.0 %all-to-all-start.6 = ((bf16[32,32,1024]{2,1,0:T(8,128)(2,1)}), bf16[32,32,1024]{2,1,0:T(8,128)(2,1)}, u32[]{:S(2)}, u32[]{:S(2)}) async-start(bf16[32,32,1024]{2,1,0:T(8,128)(2,1)} %bitcast.265), calls=%async_computation.6 | async-start | bytes 4194304 | tf_op jit(solution)/shard_map/all_to_all | solution.py:58
  241.2 3.2 fusion.3
  248.9 4.2 convolution_convert_fusion.4
  253.0 2.9 fusion.7
  259.9 8.0 %all-to-all-done.6 = bf16[32,32,1024]{2,1,0:T(8,128)(2,1)} async-done(((bf16[32,32,1024]{2,1,0:T(8,128)(2,1)}), bf16[32,32,1024]{2,1,0:T(8,128)(2,1)}, u32[]{:S(2)}, u32[]{:S(2)}) %all-to-all-start.6) | async-done | bytes 2097184 | tf_op jit(solution)/shard_map/all_to_all | solution.py:58
  275.7 6.4 %all-to-all-start.7 = ((bf16[32,32,128]{2,1,0:T(8,128)(2,1)}), bf16[32,32,128]{2,1,0:T(8,128)(2,1)S(1)}, u32[]{:S(2)}, u32[]{:S(2)}) async-start(bf16[32,32,128]{2,1,0:T(8,128)(2,1)} %heads_out.1), calls=%async_computation.7 | async-start | bytes 524288 | tf_op jit(solution)/shard_map/all_to_all | solution.py:58
  284.9 9.2 %all-to-all-done.7.upper = bf16[32,32,128]{2,1,0:T(8,128)(2,1)S(1)} async-done(((bf16[32,32,128]{2,1,0:T(8,128)(2,1)}), bf16[32,32,128]{2,1,0:T(8,128)(2,1)S(1)}, u32[]{:S(2)}, u32[]{:S(2)}) %all-to-all-start.7) | async-done | bytes 262176 | tf_op jit(solution)/shard_map/all_to_all | solution.py:58
  294.1 7.1 %all-to-all-start.8 = ((bf16[128,8,640]{2,1,0:T(8,128)(2,1)}), bf16[128,8,640]{2,1,0:T(8,128)(2,1)}, u32[]{:S(2)}, u32[]{:S(2)}) async-start(bf16[128,8,640]{2,1,0:T(8,128)(2,1)} %bitcast.95), calls=%async_computation.8 | async-start | bytes 2621440 | tf_op jit(solution)/shard_map/all_to_all | solution.py:58
  301.2 25.4 %attend_back.1 = bf16[32,160,128]{2,1,0:T(8,128)(2,1)} custom-call(bf16[32,160,128]{2,1,0:T(8,128)(2,1)S(1)} %all-to-all-done.1.packed, s32[32,128]{1,0:T(8,128)S(1)} %copy.119.seg_key, s32[8,1,128]{2,1,0:T(1,128)S(1)} %bitcast.256, bf16[32,32,128]{2,1,0:T(8,128)(2,1)S(1)} %all-to-all-done.7.upper, f32[1024,128]{1,0:T(8,128)S(1)} %get-tuple-element.69.mixed, ...), custom_call_target="tpu_custom_call" | custom-call | flops 27499999232 | bytes 65536 | tf_op jit(solution)/shard_map/attend_back/pallas_call | solution.py:519
  326.6 10.2 %all-to-all-start.9 = ((bf16[32,160,128]{2,1,0:T(8,128)(2,1)}), bf16[32,160,128]{2,1,0:T(8,128)(2,1)S(1)}, u32[]{:S(2)}, u32[]{:S(2)}) async-start(bf16[32,160,128]{2,1,0:T(8,128)(2,1)} %attend_back.1), calls=%async_computation.9 | async-start | bytes 2621440 | tf_op jit(solution)/shard_map/all_to_all | solution.py:58
  338.4 17.7 %all-to-all-done.9.refs_0_ = bf16[32,160,128]{2,1,0:T(8,128)(2,1)S(1)} async-done(((bf16[32,160,128]{2,1,0:T(8,128)(2,1)}), bf16[32,160,128]{2,1,0:T(8,128)(2,1)S(1)}, u32[]{:S(2)}, u32[]{:S(2)}) %all-to-all-start.9) | async-done | bytes 1310752 | tf_op jit(solution)/shard_map/all_to_all | solution.py:58
  357.1 3.6 unpack.1
  360.8 3.0 collective-permute-start.19
  365.9 6.8 %finish.1 = (bf16[1024,1152]{1,0:T(8,128)(2,1)}, f32[256,1024]{1,0:T(8,128)}) custom-call(s32[2]{0:T(128)} %pad_add_fusion.refs_0_, f32[256,1024]{1,0:T(8,128)} %get-tuple-element.74.refs_1_, f32[256,1024]{1,0:T(8,128)} %copy-done.4, f32[256,128]{1,0:T(8,128)} %broadcast_select_fusion.refs_2_.refs_3_, f32[256,128]{1,0:T(8,128)} %get-tuple-element.75.refs_4_, ...), custom_call_target="tpu_custom_call" | custom-call | flops 4400000000 | bytes 65536 | tf_op jit(solution)/shard_map/finish/pallas_call | solution.py:166
  372.7 4.5 %all-to-all-start.10 = ((bf16[128,8,1152]{2,1,0:T(8,128)(2,1)}), bf16[128,8,1152]{2,1,0:T(8,128)(2,1)S(1)}, u32[]{:S(2)}, u32[]{:S(2)}) async-start(bf16[128,8,1152]{2,1,0:T(8,128)(2,1)} %bitcast.273), calls=%async_computation.10 | async-start | bytes 4718592 | tf_op jit(solution)/shard_map/all_to_all | solution.py:58
  393.1 17.2 %all-to-all-done.10 = bf16[128,8,1152]{2,1,0:T(8,128)(2,1)S(1)} async-done(((bf16[128,8,1152]{2,1,0:T(8,128)(2,1)}), bf16[128,8,1152]{2,1,0:T(8,128)(2,1)S(1)}, u32[]{:S(2)}, u32[]{:S(2)}) %all-to-all-start.10) | async-done | bytes 2359328 | tf_op jit(solution)/shard_map/all_to_all | solution.py:58
  (309 shorter events, 109.4 us)
Async XLA Ops:
  7.2 5.9 %collective-permute-start.1 = (bf16[8,1024]{1,0:T(8,128)(2,1)}, bf16[8,1024]{1,0:T(8,128)(2,1)S(1)}, u32[]{:S(2)}, u32[]{:S(2)}) collective-permute-start(bf16[8,1024]{1,0:T(8,128)(2,1)} %param.29), channel_id=1, source_target_pairs={{0,1},{1,0},{2,3},{3,2},{4,5},{5,4},{6,7},{7,6},{8,9},{9,8},{10,11... | collective-permute-start | bytes 49160 | tf_op jit(solution)/shard_map/ppermute | solution.py:42
  8.7 4.4 %collective-permute-start.2 = (bf16[8,1024]{1,0:T(8,128)(2,1)}, bf16[8,1024]{1,0:T(8,128)(2,1)S(1)}, u32[]{:S(2)}, u32[]{:S(2)}) collective-permute-start(bf16[8,1024]{1,0:T(8,128)(2,1)} %param.29), channel_id=1, source_target_pairs={{0,2},{1,3},{2,0},{3,1},{4,6},{5,7},{6,4},{7,5},{8,10},{9,11},{10,... | collective-permute-start | bytes 49160 | tf_op jit(solution)/shard_map/ppermute | solution.py:42
  10.0 3.4 collective-permute-start.3
  13.4 43.6 %all-to-all-start = ((bf16[128,8,1152]{2,1,0:T(8,128)(2,1)}), bf16[128,8,1152]{2,1,0:T(8,128)(2,1)S(1)}, u32[]{:S(2)}, u32[]{:S(2)}) async-start(bf16[128,8,1152]{2,1,0:T(8,128)(2,1)} %weights.1), calls=%async_computation | async-start | bytes 4718592 | tf_op jit(solution)/shard_map/all_to_all | solution.py:58
  23.5 97.6 %all-gather.2.cloned.1.call-start = ((), (), s32[]{:S(2)}) async-start(), calls=%async_computation.13 | async-start | bytes 2162688 | tf_op jit(solution)/shard_map/all_gather | solution.py:607
  23.5 4.2 collective-permute-start
  66.7 23.7 %all-to-all-start.1 = ((bf16[32,160,128]{2,1,0:T(8,128)(2,1)}), bf16[32,160,128]{2,1,0:T(8,128)(2,1)S(1)}, u32[]{:S(2)}, u32[]{:S(2)}) async-start(bf16[32,160,128]{2,1,0:T(8,128)(2,1)} %pack.1), calls=%async_computation.1 | async-start | bytes 2621440 | tf_op jit(solution)/shard_map/all_to_all | solution.py:58
  100.5 17.0 %all-to-all-start.2 = ((bf16[32,32,128]{2,1,0:T(8,128)(2,1)}), bf16[32,32,128]{2,1,0:T(8,128)(2,1)S(1)}, u32[]{:S(2)}, u32[]{:S(2)}) async-start(bf16[32,32,128]{2,1,0:T(8,128)(2,1)} %get-tuple-element.50), calls=%async_computation.2 | async-start | bytes 524288 | tf_op jit(solution)/shard_map/all_to_all | solution.py:58
  109.2 13.5 %collective-permute-start.14 = (bf16[128,1024]{1,0:T(8,128)(2,1)}, bf16[128,1024]{1,0:T(8,128)(2,1)}, u32[]{:S(2)}, u32[]{:S(2)}) collective-permute-start(bf16[128,1024]{1,0:T(8,128)(2,1)} %bitcast.18), channel_id=1, source_target_pairs={{0,2},{1,3},{2,0},{3,1},{4,6},{5,7},{6,4},{7,5},{8,10},{9,11},{10,... | collective-permute-start | bytes 786440 | tf_op jit(solution)/shard_map/ppermute | solution.py:42
  109.8 30.2 %collective-permute-start.13 = (bf16[128,1024]{1,0:T(8,128)(2,1)}, bf16[128,1024]{1,0:T(8,128)(2,1)}, u32[]{:S(2)}, u32[]{:S(2)}) collective-permute-start(bf16[128,1024]{1,0:T(8,128)(2,1)} %bitcast.18), channel_id=1, source_target_pairs={{0,1},{1,0},{2,3},{3,2},{4,5},{5,4},{6,7},{7,6},{8,9},{9,8},{10,11... | collective-permute-start | bytes 786440 | tf_op jit(solution)/shard_map/ppermute | solution.py:42
  111.0 29.4 %collective-permute-start.11 = (bf16[256,512]{1,0:T(8,128)(2,1)}, bf16[256,512]{1,0:T(8,128)(2,1)}, u32[]{:S(2)}, u32[]{:S(2)}) collective-permute-start(bf16[256,512]{1,0:T(8,128)(2,1)} %bitcast.17), channel_id=1, source_target_pairs={{0,2},{1,3},{2,0},{3,1},{4,6},{5,7},{6,4},{7,5},{8,10},{9,11},{10,... | collective-permute-start | bytes 786440 | tf_op jit(solution)/shard_map/ppermute | solution.py:42
  112.5 29.9 %collective-permute-start.10 = (bf16[256,512]{1,0:T(8,128)(2,1)}, bf16[256,512]{1,0:T(8,128)(2,1)}, u32[]{:S(2)}, u32[]{:S(2)}) collective-permute-start(bf16[256,512]{1,0:T(8,128)(2,1)} %bitcast.17), channel_id=1, source_target_pairs={{0,1},{1,0},{2,3},{3,2},{4,5},{5,4},{6,7},{7,6},{8,9},{9,8},{10,11... | collective-permute-start | bytes 786440 | tf_op jit(solution)/shard_map/ppermute | solution.py:42
  118.2 5.0 %collective-permute-start.6 = (bf16[128,512]{1,0:T(8,128)(2,1)S(1)}, bf16[128,512]{1,0:T(8,128)(2,1)S(1)}, u32[]{:S(2)}, u32[]{:S(2)}) collective-permute-start(bf16[128,512]{1,0:T(8,128)(2,1)S(1)} %get-tuple-element.111), channel_id=1, source_target_pairs={{0,1},{1,0},{2,3},{3,2},{4,5},{5,4},{6,7},{7,6},{8,9},{9,8},{10,11... | collective-permute-start | bytes 393224 | tf_op jit(solution)/shard_map/ppermute | solution.py:42
  122.7 17.9 %collective-permute-start.8 = (bf16[256,512]{1,0:T(8,128)(2,1)}, bf16[256,512]{1,0:T(8,128)(2,1)}, u32[]{:S(2)}, u32[]{:S(2)}) collective-permute-start(bf16[256,512]{1,0:T(8,128)(2,1)} %bitcast.16), channel_id=1, source_target_pairs={{0,2},{1,3},{2,0},{3,1},{4,6},{5,7},{6,4},{7,5},{8,10},{9,11},{10,... | collective-permute-start | bytes 786440 | tf_op jit(solution)/shard_map/ppermute | solution.py:42
  123.2 17.7 %collective-permute-start.15 = (bf16[128,1024]{1,0:T(8,128)(2,1)}, bf16[128,1024]{1,0:T(8,128)(2,1)}, u32[]{:S(2)}, u32[]{:S(2)}) collective-permute-start(bf16[128,1024]{1,0:T(8,128)(2,1)} %collective-permute-done.14), channel_id=1, source_target_pairs={{0,1},{1,0},{2,3},{3,2},{4,5},{5,4},{6,7},{7,6},{8,9},{9,8},{10,11... | collective-permute-start | bytes 786440 | tf_op jit(solution)/shard_map/ppermute | solution.py:42
  127.3 35.0 %all-to-all-start.3 = ((bf16[32,32,1024]{2,1,0:T(8,128)(2,1)}), bf16[32,32,1024]{2,1,0:T(8,128)(2,1)}, u32[]{:S(2)}, u32[]{:S(2)}) async-start(bf16[32,32,1024]{2,1,0:T(8,128)(2,1)} %bitcast.264), calls=%async_computation.3 | async-start | bytes 4194304 | tf_op jit(solution)/shard_map/all_to_all | solution.py:58
  140.1 3.6 collective-permute-start.7
  140.6 3.1 collective-permute-start.9
  162.3 36.0 %all-to-all-start.4 = ((bf16[32,32,1024]{2,1,0:T(8,128)(2,1)}), bf16[32,32,1024]{2,1,0:T(8,128)(2,1)}, u32[]{:S(2)}, u32[]{:S(2)}) async-start(bf16[32,32,1024]{2,1,0:T(8,128)(2,1)} %bitcast.263), calls=%async_computation.4 | async-start | bytes 4194304 | tf_op jit(solution)/shard_map/all_to_all | solution.py:58
  198.4 34.6 %all-to-all-start.5 = ((bf16[32,32,1024]{2,1,0:T(8,128)(2,1)}), bf16[32,32,1024]{2,1,0:T(8,128)(2,1)}, u32[]{:S(2)}, u32[]{:S(2)}) async-start(bf16[32,32,1024]{2,1,0:T(8,128)(2,1)} %bitcast.274), calls=%async_computation.5 | async-start | bytes 4194304 | tf_op jit(solution)/shard_map/all_to_all | solution.py:58
  206.3 2.3 collective-permute-start.16
  232.9 34.9 %all-to-all-start.6 = ((bf16[32,32,1024]{2,1,0:T(8,128)(2,1)}), bf16[32,32,1024]{2,1,0:T(8,128)(2,1)}, u32[]{:S(2)}, u32[]{:S(2)}) async-start(bf16[32,32,1024]{2,1,0:T(8,128)(2,1)} %bitcast.265), calls=%async_computation.6 | async-start | bytes 4194304 | tf_op jit(solution)/shard_map/all_to_all | solution.py:58
  240.9 146.5 %reduce-scatter.5.cloned.1.call-start = ((), (), s32[]{:S(2)}) async-start(), calls=%async_computation.15 | async-start | bytes 1310720 | tf_op jit(solution)/shard_map/reduce_scatter | solution.py:752
  271.2 3.8 collective-permute-start.18
  274.4 7.7 %collective-permute-start.17 = (bf16[128,512]{1,0:T(8,128)(2,1)}, bf16[128,512]{1,0:T(8,128)(2,1)}, u32[]{:S(2)}, u32[]{:S(2)}) collective-permute-start(bf16[128,512]{1,0:T(8,128)(2,1)} %get-tuple-element.105), channel_id=1, source_target_pairs={{0,1},{1,0},{2,3},{3,2},{4,5},{5,4},{6,7},{7,6},{8,9},{9,8},{10,11... | collective-permute-start | bytes 393224 | tf_op jit(solution)/shard_map/ppermute | solution.py:42
  275.7 18.4 %all-to-all-start.7 = ((bf16[32,32,128]{2,1,0:T(8,128)(2,1)}), bf16[32,32,128]{2,1,0:T(8,128)(2,1)S(1)}, u32[]{:S(2)}, u32[]{:S(2)}) async-start(bf16[32,32,128]{2,1,0:T(8,128)(2,1)} %heads_out.1), calls=%async_computation.7 | async-start | bytes 524288 | tf_op jit(solution)/shard_map/all_to_all | solution.py:58
  294.1 32.5 %all-to-all-start.8 = ((bf16[128,8,640]{2,1,0:T(8,128)(2,1)}), bf16[128,8,640]{2,1,0:T(8,128)(2,1)}, u32[]{:S(2)}, u32[]{:S(2)}) async-start(bf16[128,8,640]{2,1,0:T(8,128)(2,1)} %bitcast.95), calls=%async_computation.8 | async-start | bytes 2621440 | tf_op jit(solution)/shard_map/all_to_all | solution.py:58
  326.6 29.4 %all-to-all-start.9 = ((bf16[32,160,128]{2,1,0:T(8,128)(2,1)}), bf16[32,160,128]{2,1,0:T(8,128)(2,1)S(1)}, u32[]{:S(2)}, u32[]{:S(2)}) async-start(bf16[32,160,128]{2,1,0:T(8,128)(2,1)} %attend_back.1), calls=%async_computation.9 | async-start | bytes 2621440 | tf_op jit(solution)/shard_map/all_to_all | solution.py:58
  336.8 77.8 %reduce-scatter.3.cloned.1.call-start = ((), (), s32[]{:S(2)}) async-start(), calls=%async_computation.14 | async-start | bytes 2621440 | tf_op jit(solution)/shard_map/reduce_scatter | solution.py:811
  360.8 4.4 %collective-permute-start.19 = (f32[256,128]{1,0:T(8,128)}, f32[256,128]{1,0:T(8,128)S(1)}, u32[]{:S(2)}, u32[]{:S(2)}) collective-permute-start(f32[256,128]{1,0:T(8,128)} %get-tuple-element.75.refs_4_), channel_id=1, source_target_pairs={{0,1},{1,0},{2,3},{3,2},{4,5},{5,4},{6,7},{7,6},{8,9},{9,8},{10,11... | collective-permute-start | bytes 393224 | tf_op jit(solution)/shard_map/ppermute | solution.py:42
  372.7 37.6 %all-to-all-start.10 = ((bf16[128,8,1152]{2,1,0:T(8,128)(2,1)}), bf16[128,8,1152]{2,1,0:T(8,128)(2,1)S(1)}, u32[]{:S(2)}, u32[]{:S(2)}) async-start(bf16[128,8,1152]{2,1,0:T(8,128)(2,1)} %bitcast.273), calls=%async_computation.10 | async-start | bytes 4718592 | tf_op jit(solution)/shard_map/all_to_all | solution.py:58
  385.1 4.3 %collective-permute-start.20 = (f32[128,1024]{1,0:T(8,128)}, f32[128,1024]{1,0:T(8,128)}, u32[]{:S(2)}, u32[]{:S(2)}) collective-permute-start(f32[128,1024]{1,0:T(8,128)} %slice.139), channel_id=1, source_target_pairs={{0,1},{1,0},{2,3},{3,2},{4,5},{5,4},{6,7},{7,6},{8,9},{9,8},{10,11... | collective-permute-start | bytes 1572872 | tf_op jit(solution)/shard_map/ppermute | solution.py:42
  (60 other events, 636.8 us)
Sparse Core Ops, SparseCore 0:
  28.0 90.5 all-gather.1
  275.1 21.4 reduce-scatter.4
  340.2 29.8 reduce-scatter.2

commit v2 on v1

--- a/solution.py
+++ b/solution.py
@@ -97,8 +97,9 @@
 
 
 class Made:
-    def __init__(self, buffer, target, sems, first):
-        self.buffer, self.target, self.sems, self.first = buffer, target, sems, first
+    def __init__(self, buffer, target, columns, sems, first):
+        self.buffer, self.target, self.columns = buffer, target, columns
+        self.sems, self.first = sems, first
         self.copies = []
 
     def __getitem__(self, index):
@@ -110,7 +111,11 @@
     def send(self, rows=None):
         source, target = self.buffer, self.target
         if rows is not None:
-            source, target = source.at[rows], target.at[rows]
+            source = source.at[rows]
+        if self.columns is not None:
+            target = target.at[slice(None) if rows is None else rows, self.columns]
+        elif rows is not None:
+            target = target.at[rows]
         copy = pltpu.make_async_copy(source, target, self.sems.at[self.first + len(self.copies)])
         copy.start()
         self.copies.append(copy)
@@ -124,6 +129,11 @@
 
 
 def call(kernel, inputs, outputs, name, micros=2, ids=None):
+    made = []
+    for k, (shape, dtype, *cuts) in enumerate(outputs):
+        for columns in cuts[0] if cuts else (None,):
+            wide = shape if columns is None else (shape[0], columns.stop - columns.start)
+            made.append((k, wide, dtype, columns))
     hbm = pl.BlockSpec(memory_space=pltpu.HBM)
     inputs = [i if isinstance(i, tuple) else far(i) for i in inputs]
     scratch = []
@@ -132,8 +142,8 @@
         if part is not None:
             shape = tuple(p.stop - p.start for p in part) + array.shape[len(part) :]
         scratch.append(pltpu.VMEM(shape, array.dtype))
-    scratch += [pltpu.VMEM(shape, dtype) for shape, dtype in outputs]
-    scratch.append(pltpu.SemaphoreType.DMA((len(inputs) + SENDS * len(outputs),)))
+    scratch += [pltpu.VMEM(shape, dtype) for _, shape, dtype, _ in made]
+    scratch.append(pltpu.SemaphoreType.DMA((len(inputs) + SENDS * len(made),)))
     numbers = [] if ids is None else [ids]
 
     def body(*refs):
@@ -151,23 +161,26 @@
             copy = pltpu.make_async_copy(ref, buffers[k], sems.at[k])
             copy.start()
             given.append(Held(buffers[k], copy))
-        for k, ref in enumerate(outs):
-            results.append(Made(buffers[len(inputs) + k], ref, sems, len(inputs) + SENDS * k))
+        for k, (number, _, _, columns) in enumerate(made):
+            ref = outs[number]
+            results.append(
+                Made(buffers[len(inputs) + k], ref, columns, sems, len(inputs) + SENDS * k)
+            )
         kernel(*([own_ids] if numbers else []), *given, *results)
         for held in given:
             held.wait()
-        for made in results:
-            if not made.copies:
-                made.send()
-        for made in results:
-            for copy in made.copies:
+        for result in results:
+            if not result.copies:
+                result.send()
+        for result in results:
+            for copy in result.copies:
                 copy.wait()
 
     return pl.pallas_call(
         body,
         in_specs=[pl.BlockSpec(memory_space=pltpu.SMEM)] * len(numbers) + [hbm] * len(inputs),
         out_specs=[hbm] * len(outputs),
-        out_shape=[jax.ShapeDtypeStruct(shape, dtype) for shape, dtype in outputs],
+        out_shape=[jax.ShapeDtypeStruct(shape, dtype) for shape, dtype, *_ in outputs],
         scratch_shapes=scratch,
         compiler_params=pltpu.CompilerParams(vmem_limit_bytes=VMEM_LIMIT),
         cost_estimate=estimate(micros),
@@ -236,8 +249,7 @@
     return jnp.concatenate([value[TOK:], value[:TOK]], axis=0)
 
 
-def unpack_kernel(grads, qkv, scales, gains, cosine, sine, out, sums, gain_grad):
-    gain = gains[0:1, :]
+def unpack_kernel(grads, qkv, scales, gain, cosine, sine, out, sums, gain_grad):
     lines = [None] * (2 * PART_HEADS)
     for j in range(PARTS):
         rows = slice(j * TOK, (j + 1) * TOK)
@@ -280,7 +292,7 @@
     gain_grad[...] = jnp.broadcast_to(jnp.concatenate(lines, axis=1), (8, COLS))
 
 
-def finish_kernel(ids, through, qkv, scales, sums, sums_other, normed, weights, tokens, gain_grad, last, grad_normed):
+def finish_kernel(ids, through, qkv, scales, sums, sums_other, normed, weights, tokens, tokens_other, gain_grad, last, last_small, grad_normed):
     total = sums[...] + other_rows(sums_other[...])
     lane = lanes((TOK, COLS)) % 256
     is_q, is_k = lane < 128, (lane >= 128) & (lane < 192)
@@ -291,26 +303,54 @@
         mean = jnp.where(is_q, total[rows, 0:1] / 1024, jnp.where(is_k, total[rows, 1:2] / 512, 0.0))
         grads.append((scale * (through[rows, :] - qkv[rows, :] * scale * mean)).astype(BF))
     grad = jnp.concatenate(grads, axis=0)
-    normed_grad = dot(grad, weights[:, :COLS], ((1,), (1,)))
+    tile = D // SENDS
+    for t in range(SENDS):
+        rows = slice(t * tile, (t + 1) * tile)
+        last[rows, :] = dot(normed[:, rows], grad, ((0,), (0,))).astype(BF)
+        last.send(rows)
+    normed_grad = dot(grad, weights[...], ((1,), (1,)))
     grad_normed[...] = normed_grad
     grad_normed.send()
-    value = tokens[...].astype(F32)
+    value = jnp.concatenate([tokens[...], tokens_other[...]], axis=0).astype(F32)
     products = (normed_grad * (value * inverse_rms(value))).astype(BF)
     ones = jnp.where(lanes((ROWS, 128)) == 64, 1.0, 0.0).astype(BF)
-    last[:, COLS:] = dot(products, ones, ((0,), (0,))).astype(BF)
+    last_small[...] = dot(products, ones, ((0,), (0,))).astype(BF)
     row = lax.broadcasted_iota(jnp.int32, (TOK, TOK), 0) % 8
     for h in range(PART_HEADS):
         query, key = [gain_grad[0:1, h * 256 + k : h * 256 + k + 128] for k in (0, 128)]
         block = jnp.where(row == 0, query, jnp.where(row == 1, key, 0.0))
         block = jnp.where(row == 2, pltpu.roll(query, HD, 1), block)
         at = pl.ds(pl.multiple_of(ids[0] * FEATURES + h * TOK, TOK), TOK)
-        known = last[at, COLS:].astype(F32)
-        last[at, COLS:] = jnp.where(lanes((TOK, TOK)) < HD, block, known).astype(BF)
-    tile = D // SENDS
-    for t in range(SENDS):
-        rows = slice(t * tile, (t + 1) * tile)
-        last[rows, :COLS] = dot(normed[:, rows], grad, ((0,), (0,))).astype(BF)
-        last.send(rows)
+        known = last_small[at, :].astype(F32)
+        last_small[at, :] = jnp.where(lanes((TOK, TOK)) < HD, block, known).astype(BF)
+
+
+def final_kernel(ids, parts, query, key, value, attn_gain, query_gain, key_gain):
+    def column(t):
+        piece = parts[:, :, t * 128 : t * 128 + 128].astype(F32)
+        return jnp.sum(piece.reshape(4 * N_CTX // PARTS, PARTS, 8, 128), axis=0)
+
+    low_half = lanes((8, 128)) < HD
+    for h in range(0, PART_HEADS, 2):
+        first, second = column(2 * h), column(2 * h + 2)
+        kv_first, kv_second = column(2 * h + 1), column(2 * h + 3)
+        for p in range(PARTS):
+            at = (p * PART_HEADS + h) * 128
+            query[:, at : at + 128] = first[p]
+            query[:, at + 128 : at + 256] = second[p]
+            at = at // 2
+            key[:, at : at + 128] = jnp.where(low_half, kv_first[p], pltpu.roll(kv_second[p], HD, 1))
+            value[:, at : at + 128] = jnp.where(
+                low_half, pltpu.roll(kv_first[p], HD, 1), kv_second[p]
+            )
+    small = jnp.sum(column(2 * PART_HEADS), axis=0)
+    row = lax.broadcasted_iota(jnp.int32, (8, 128), 0)
+    lane = lanes((8, 128))
+    attn = jnp.sum(jnp.where(lane == 64, small, 0.0), axis=1, keepdims=True)
+    attn_gain[...] = jnp.sum(jnp.where(row == lane, attn, 0.0), axis=0, keepdims=True)[:, :8]
+    turned = pltpu.roll(small, ids[1], 1)
+    query_gain[...] = jnp.where(ids[0] == 0, turned[0:1, :8], turned[2:3, :8])
+    key_gain[...] = pltpu.roll(small, ids[2], 1)[1:2, :4]
 
 
 def heads_in_kernel(received, out):
@@ -371,7 +411,7 @@
         columns[src * TOK : (src + 1) * TOK, :] = line.T
 
 
-def forward_kernel(packed, seg_key, seg_query, mixed, mixed_low, lse, kv, kv_t, columns, limits):
+def forward_kernel(packed, seg_key, seg_query, mixed, lse, kv, kv_t, columns, limits):
     src = TOK_TILE // 32
     kv[...] = packed[:, 0:TOK, :].reshape(KEYS, 128)
     i = lax.broadcasted_iota(jnp.int32, (128, 128), 0)
@@ -396,8 +436,7 @@
         out = jnp.where(
             lanes((TOK_TILE, 128)) < HD, pltpu.roll(out[:TOK_TILE], HD, 1), out[TOK_TILE:]
         )
-        mixed[pl.ds(tile * TOK_TILE, TOK_TILE), :] = out
-        mixed_low[pl.ds(tile * src, src)] = out.astype(BF).reshape(src, 32, 128)
+        mixed[pl.ds(tile * src, src)] = out.astype(BF).reshape(src, 32, 128)
         lse[tile] = top + jnp.log(total)
 
     for tile in range(TILES):
@@ -434,24 +473,53 @@
             store(tile, accum, jnp.sum(total, axis=0, keepdims=True), top)
 
 
-def backward_kernel(packed, seg_key, seg_query, upper, mixed, lse, out, k2, k2t, v2, dk, dv, columns):
+def probabilities_kernel(packed, seg_key, seg_query, lse, probs, kv_t, kv, columns):
     @pl.when(pl.program_id(0) == 0)
     def _():
-        kv = packed[:, 0:TOK, :].reshape(KEYS, 128)
-        k2[...] = dot(kv, pick(0, False)).astype(BF)
-        k2t[...] = dot(pick(0, True), kv, ((1,), (1,))).astype(BF)
-        v2[...] = dot(kv, pick(HD, False)).astype(BF)
-        dk[...] = jnp.zeros_like(dk)
-        dv[...] = jnp.zeros_like(dv)
+        kv[...] = packed[:, 0:TOK, :].reshape(KEYS, 128)
+        i = lax.broadcasted_iota(jnp.int32, (128, 128), 0)
+        kv_t[...] = dot((i == lanes((128, 128))).astype(BF), kv[...], ((1,), (1,))).astype(BF)
         key_segments(seg_key, columns)
 
     tile = pl.program_id(0)
     src = TOK_TILE // 32
     q = packed[pl.ds(tile * src, src), TOK:PACK, :].reshape(TOK_TILE, 128)
-    rows = head_rows(q * BF(HD**-0.5))
+    rows = query_rows(q)
+    seg_q = jnp.concatenate([seg_query[tile], seg_query[tile]], axis=1)
+    for t in range(KEYS // KEY_TILE):
+        keys = slice(t * KEY_TILE, (t + 1) * KEY_TILE)
+        s = dot(kv[keys, :], rows, ((1,), (1,)))
+        seg_k = jnp.concatenate([columns[keys, :]] * (2 * TOK_TILE // 128), axis=1)
+        s = jnp.where(seg_k == seg_q, s - lse[0], -1e30)
+        probs[0, keys, :] = jnp.exp(s).astype(BF)
+
+
+def value_rows(block):
+    low_half = lanes(block.shape) < HD
+    block = block.astype(F32)
+    return jnp.concatenate(
+        [
+            jnp.where(low_half, 0.0, pltpu.roll(block, HD, 1)),
+            jnp.where(low_half, 0.0, block),
+        ],
+        axis=0,
+    ).astype(BF)
+
+
+def backward_kernel(packed, probs, kv_t, upper, mixed, out, kv, dkv):
+    tile = pl.program_id(0)
+
+    @pl.when(tile == 0)
+    def _():
+        kv[...] = packed[:, 0:TOK, :].reshape(KEYS, 128)
+        dkv[...] = jnp.zeros_like(dkv)
+
+    src = TOK_TILE // 32
+    q = packed[pl.ds(tile * src, src), TOK:PACK, :].reshape(TOK_TILE, 128)
     upper_now = upper[...].reshape(TOK_TILE, 128)
-    up = head_rows(upper_now)
-    along = (upper_now.astype(F32) * mixed[...]).T
+    up = value_rows(upper_now)
+    both = jnp.concatenate([up, query_rows(q)], axis=0)
+    along = (upper_now.astype(F32) * mixed[...].reshape(TOK_TILE, 128).astype(F32)).T
     delta = jnp.concatenate(
         [
             jnp.sum(along[:HD], axis=0, keepdims=True),
@@ -459,32 +527,21 @@
         ],
         axis=1,
     )
-    seg_q = jnp.concatenate([seg_query[tile], seg_query[tile]], axis=1)
     dq = jnp.zeros((128, 2 * TOK_TILE), F32)
     for t in range(KEYS // KEY_TILE):
-        at = t * KEY_TILE
-        keys = slice(at, at + KEY_TILE)
-        s = dot(k2[keys, :], rows, ((1,), (1,)))
-        seg_k = jnp.concatenate([columns[keys, :]] * (2 * TOK_TILE // 128), axis=1)
-        p = jnp.where(seg_k == seg_q, jnp.exp(s - lse[0]), 0.0)
-        dp = dot(v2[keys, :], up, ((1,), (1,)))
-        ds = (p * (dp - delta)).astype(BF)
-        dv[keys, :] += dot(p.astype(BF), up)
-        dk[keys, :] += dot(ds, rows)
-        dq = dq + dot(k2t[:, keys], ds)
+        keys = slice(t * KEY_TILE, (t + 1) * KEY_TILE)
+        p = probs[0, keys, :]
+        dp = dot(kv[keys, :], up, ((1,), (1,)))
+        ds = (p.astype(F32) * (dp - delta)).astype(BF)
+        dkv[keys, :] += dot(jnp.concatenate([p, ds], axis=1), both)
+        dq = dq + dot(kv_t[:, keys], ds)
     dq = (dq * HD**-0.5).T
-    dq = jnp.where(lanes((TOK_TILE, 128)) < HD, dq[:TOK_TILE], dq[TOK_TILE:])
+    dq = jnp.where(lanes((TOK_TILE, 128)) < HD, dq[:TOK_TILE], pltpu.roll(dq[TOK_TILE:], HD, 1))
     out[pl.ds(tile * src, src), TOK:PACK, :] = dq.astype(BF).reshape(src, 32, 128)
 
     @pl.when(tile == pl.num_programs(0) - 1)
     def _():
-        for t in range(KEYS // KEY_TILE):
-            keys = slice(t * KEY_TILE, (t + 1) * KEY_TILE)
-            low_half = lanes((KEY_TILE, 128)) < HD
-            both_k = dk[keys, :] + pltpu.roll(dk[keys, :], HD, 1)
-            both_v = dv[keys, :] + pltpu.roll(dv[keys, :], HD, 1)
-            both = jnp.where(low_half, both_k, both_v).astype(BF).reshape(-1, TOK, 128)
-            out[t * KEY_TILE // TOK : (t + 1) * KEY_TILE // TOK, 0:TOK, :] = both
+        out[:, 0:TOK, :] = dkv[...].astype(BF).reshape(N_CTX, TOK, 128)
 
 
 def whole(shape):
@@ -496,9 +553,8 @@
     return pl.pallas_call(
         forward_kernel,
         in_specs=[vmem] * 3,
-        out_specs=[vmem, pl.BlockSpec(), vmem],
+        out_specs=[pl.BlockSpec(), vmem],
         out_shape=[
-            jax.ShapeDtypeStruct((QUERIES, 128), F32),
             jax.ShapeDtypeStruct((N_CTX, 32, 128), BF),
             jax.ShapeDtypeStruct((TILES, 1, 2 * TOK_TILE), F32),
         ],
@@ -514,33 +570,49 @@
     )(packed, seg_key, seg_query)
 
 
-def attend_back(packed, seg_key, seg_query, upper, mixed, lse):
+def probabilities(packed, seg_key, seg_query, lse):
+    width = 2 * TOK_TILE
+    return pl.pallas_call(
+        probabilities_kernel,
+        grid=(TILES,),
+        in_specs=[
+            whole((N_CTX, PACK, 128)),
+            whole((N_CTX, TOK)),
+            whole((TILES, 1, TOK_TILE)),
+            pl.BlockSpec((1, 1, width), lambda i: (i, 0, 0)),
+        ],
+        out_specs=[pl.BlockSpec((1, KEYS, width), lambda i: (i, 0, 0)), whole((128, KEYS))],
+        out_shape=[
+            jax.ShapeDtypeStruct((TILES, KEYS, width), BF),
+            jax.ShapeDtypeStruct((128, KEYS), BF),
+        ],
+        scratch_shapes=[pltpu.VMEM((KEYS, 128), BF), pltpu.VMEM((KEYS, 128), jnp.int32)],
+        compiler_params=pltpu.CompilerParams(vmem_limit_bytes=32 << 20),
+        cost_estimate=estimate(11),
+        name="probabilities",
+    )(packed, seg_key, seg_query, lse)
+
+
+def attend_back(packed, probs, kv_t, upper, mixed):
     src = TOK_TILE // 32
+    piece = pl.BlockSpec((src, 32, 128), lambda i: (i, 0, 0))
     return pl.pallas_call(
         backward_kernel,
         grid=(TILES,),
         in_specs=[
             whole((N_CTX, PACK, 128)),
-            whole((N_CTX, TOK)),
-            whole((TILES, 1, TOK_TILE)),
-            pl.BlockSpec((src, 32, 128), lambda i: (i, 0, 0)),
-            pl.BlockSpec((TOK_TILE, 128), lambda i: (i, 0)),
-            pl.BlockSpec((1, 1, 2 * TOK_TILE), lambda i: (i, 0, 0)),
+            pl.BlockSpec((1, KEYS, 2 * TOK_TILE), lambda i: (i, 0, 0)),
+            whole((128, KEYS)),
+            piece,
+            piece,
         ],
         out_specs=whole((N_CTX, PACK, 128)),
         out_shape=jax.ShapeDtypeStruct((N_CTX, PACK, 128), BF),
-        scratch_shapes=[
-            pltpu.VMEM((KEYS, 128), BF),
-            pltpu.VMEM((128, KEYS), BF),
-            pltpu.VMEM((KEYS, 128), BF),
-            pltpu.VMEM((KEYS, 128), F32),
-            pltpu.VMEM((KEYS, 128), F32),
-            pltpu.VMEM((KEYS, 128), jnp.int32),
-        ],
-        compiler_params=pltpu.CompilerParams(vmem_limit_bytes=32 << 20),
-        cost_estimate=estimate(25),
+        scratch_shapes=[pltpu.VMEM((KEYS, 128), BF), pltpu.VMEM((KEYS, 128), F32)],
+        compiler_params=pltpu.CompilerParams(vmem_limit_bytes=40 << 20),
+        cost_estimate=estimate(21),
         name="attend_back",
-    )(packed, seg_key, seg_query, upper, mixed, lse)
+    )(packed, probs, kv_t, upper, mixed)
 
 
 def in_order(pieces, fsdp):
@@ -600,7 +672,8 @@
     tokens = hidden_in[0]
     order = block_order[0]
     blocks = lax.dynamic_slice_in_dim(order, place * 2, 2)
-    tokens_all = [tokens, swap(tokens, 1)]
+    tokens_other = swap(tokens, 1)
+    tokens_all = [tokens, tokens_other]
     blocks_all = [blocks, swap(blocks, 1)]
     tokens_all = jnp.concatenate(tokens_all, axis=0)
 
@@ -673,7 +746,7 @@
     )[0]
     packed = exchange(packed, "ctx")
     scales = jnp.where(jnp.arange(128)[None] == 0, scale_q, scale_k)
-    gains = jnp.broadcast_to(gain_heads, (8, COLS))
+    packed, part_ids = lax.optimization_barrier((packed, part_ids))
 
     sequence = fsdp ^ (place // (N_CTX // PARTS))
     seg_small = lax.dynamic_index_in_dim(
@@ -693,8 +766,8 @@
         for own, far in zip((shard_gate, shard_up, shard_down), shards_far)
     ]
 
-    mixed, mixed_low, lse = attend(packed, seg_all, seg_query)
-    returned = exchange(mixed_low, "ctx")
+    mixed, lse = attend(packed, seg_all, seg_query)
+    returned = exchange(mixed, "ctx")
     returned = call_near(heads_in_kernel, (returned,), [((PARTS, TOK, FEATURES), BF, False)], "heads_in", 1)[0]
     pieces = swapped([returned[j] for j in range(PARTS)])
     out_parts = proj_out.reshape(PARTS, FEATURES, D)
@@ -739,7 +812,10 @@
     grad_up_act = (grad_inner * silu_gate).astype(BF)
     grad_rows = dot(grad_gate_act, gate_w, ((1,), (1,))) + dot(grad_up_act, up_w, ((1,), (1,)))
     grad_rows = grad_rows.astype(BF).reshape(N_CTX, CAP, D)
-    produced_home, grad_rows = lax.optimization_barrier((produced_home, grad_rows))
+    probs, kv_t = probabilities(packed, seg_all, seg_query, lse)
+    produced_home, grad_rows, probs, kv_t = lax.optimization_barrier(
+        (produced_home, grad_rows, probs, kv_t)
+    )
     grad_home = exchange(grad_rows, "ctx").reshape(EXPERTS * CAP, D)
 
     grad_gate_w = dot(arrived, grad_gate_act, ((0,), (0,))).astype(BF)
@@ -749,8 +825,8 @@
     grad_home, grad_down_w, grad_gate_up = lax.optimization_barrier(
         (grad_home, grad_down_w, grad_gate_up)
     )
-    grad_down = lax.psum_scatter(
-        grad_down_w[None], "fsdp", scatter_dimension=1, tiled=True
+    grad_gate_up = lax.psum_scatter(
+        grad_gate_up, "fsdp", scatter_dimension=1, tiled=True
     ).astype(F32)
 
     share = share.reshape(EXPERTS * CAP, TOK)
@@ -804,18 +880,17 @@
     late, upper = lax.optimization_barrier((late, upper))
     first_sums = exchange(late.reshape(4 * N_CTX, 8, 640), both_axes)
 
-    grads_home = attend_back(packed, seg_all, seg_query, upper, mixed, lse)
-    grads_home, first_sums, grad_gate_up = lax.optimization_barrier(
-        (grads_home, first_sums, grad_gate_up)
-    )
-    grad_gate_up = lax.psum_scatter(
-        grad_gate_up, "fsdp", scatter_dimension=1, tiled=True
+    grads_home = attend_back(packed, probs, kv_t, upper, mixed)
+    grads_home, first_sums = lax.optimization_barrier((grads_home, first_sums))
+    grads_home = exchange(grads_home, "ctx")
+    grads_home, grad_down_w = lax.optimization_barrier((grads_home, grad_down_w))
+    grad_down = lax.psum_scatter(
+        grad_down_w[None], "fsdp", scatter_dimension=1, tiled=True
     ).astype(F32)
-    grads_home = exchange(grads_home, "ctx")
 
     through_heads, sums, gain_grad = call(
         unpack_kernel,
-        (grads_home, qkv, scales, gains, cosine, sine),
+        (grads_home, qkv, scales, gain_heads, cosine, sine),
         [((ROWS, COLS), F32), ((ROWS, 128), F32), ((8, COLS), F32)],
         "unpack",
     )
@@ -828,11 +903,15 @@
             sums,
             swap(sums, 1),
             normed_low,
-            weights,
-            tokens_all,
+            far(weights, cut=(slice(0, D), slice(0, COLS))),
+            tokens,
+            tokens_other,
             gain_grad,
         ),
-        [((D, COLS + 128), BF), ((ROWS, D), F32)],
+        [
+            ((D, COLS + 128), BF, (slice(0, COLS), slice(COLS, COLS + 128))),
+            ((ROWS, D), F32),
+        ],
         "finish",
         4,
         part_ids,
@@ -850,32 +929,45 @@
     first_sums = jnp.sum(first_sums.reshape(2 * N_CTX, 2, 8, 640).astype(F32), axis=0)
     grad_out = jnp.concatenate([first_sums[0, :, :512], first_sums[1, :, :512]], axis=1)
     first_small = first_sums[0, :, 512:] + first_sums[1, :, 512:]
-    last_sums = jnp.sum(
-        last_sums.reshape(4 * N_CTX // PARTS, PARTS, 8, COLS + 128).astype(F32), axis=0
-    )
-    heads_g = last_sums[:, :, :COLS].reshape(PARTS, 8, PART_HEADS, 256)
-    heads_g = jnp.transpose(heads_g, (1, 0, 2, 3))
-    last_small = jnp.sum(last_sums[:, :, COLS:], axis=0)
-    index = 4 * place + fsdp
-    query_gain = lax.dynamic_slice(
-        last_small, (index % 16 // 8 * 2, index % 8 * 8), (1, 8)
-    ).reshape(8)
-    key_gain = lax.dynamic_slice(last_small, (1, index % 16 * 4), (1, 4)).reshape(4)
-    return (
-        layer_out,
+    ready = (
         input_grad[None],
-        last_small[:, 64],
-        heads_g[..., :128].reshape(8, 1024),
-        heads_g[..., 128:192].reshape(8, 512),
-        heads_g[..., 192:].reshape(8, 512),
-        query_gain,
-        key_gain,
         grad_out,
         first_small[:, 64],
         first_small[:, :EXPERTS],
         grad_gate_up[0][None],
         grad_gate_up[1][None],
         grad_down,
+    )
+    index = 4 * place + fsdp
+    final_ids = jnp.stack(
+        [index % 16 // 8, (128 - index % 8 * 8) % 128, (128 - index % 16 * 4) % 128]
+    ).astype(jnp.int32)
+    last_sums, ready, final_ids = lax.optimization_barrier((last_sums, ready, final_ids))
+    grad_query, grad_key, grad_value, attn_gain, query_gain, key_gain = call(
+        final_kernel,
+        (last_sums,),
+        [
+            ((8, 1024), F32),
+            ((8, 512), F32),
+            ((8, 512), F32),
+            ((1, 8), F32),
+            ((1, 8), F32),
+            ((1, 4), F32),
+        ],
+        "final",
+        2,
+        final_ids,
+    )
+    return (
+        layer_out,
+        ready[0],
+        attn_gain.reshape(8),
+        grad_query,
+        grad_key,
+        grad_value,
+        query_gain.reshape(8),
+        key_gain.reshape(4),
+        *ready[1:],
     )
 
 

time: 430 us -> 426 us (level)
  Pallas kernels: 53.2 us -> 60.3 us
  local copies, waits for them, and re-layouts: 18.5 us -> 14 us
    pallas_call x1 -> x2, Pallas kernels: 10.2 us -> 18.5 us  [the longest x1 10.1 us: attend(): pl.pallas_call(forward_kernel, in_specs=[vmem] * 3, out_specs=[pl.BlockSp...]
    pallas_call x3 -> x4, Pallas kernels: 13.1 us -> 15.6 us  [call(): pl.pallas_call(body, in_specs=[pl.BlockSpec(memory_space=pltpu.SMEM)] * l...]
  transfers between devices with their start and end apart: 35 -> 35, of which waited for: 14 -> 15; matrix products, arithmetic and copies ran while one was open for 22% -> 21% of each run, Pallas kernels for 13% -> 14%
where the time goes in v2:
time: 426 us; the launch traced here: 419 us
  waiting for transfers between devices  143 us (34%)
  starting transfers between devices  105 us (25%)
  Pallas kernels  60.3 us (14%)
  matrix products  54.8 us (13%)
  other arithmetic  27 us (6%)
  between operations  15.2 us (4%)
  local copies, waits for them, and re-layouts  14 us (3%)
    all_to_all x11, waiting for transfers between devices, exchange(): return lax.all_to_all(array, axis, split_axis=0, concat_axis=0, tiled=True)  141 us
    all_to_all x11, starting transfers between devices, exchange(): return lax.all_to_all(array, axis, split_axis=0, concat_axis=0, tiled=True)  82.9 us
    dot_general x22, matrix products, dot(): return lax.dot_general(a, b, (dims, ((), ())), preferred_element_type=F32)  54.8 us
    pallas_call x1, Pallas kernels, attend_back(): pl.pallas_call(backward_kernel, grid=(TILES,), in_specs=[whole((N_CTX, PA...  21.7 us
    ppermute x21, starting transfers between devices, swap(): lax.ppermute(array, 'fsdp', [(i, i ^ j) for i in range(4)])  21.2 us
    pallas_call x4, Pallas kernels, call(): pl.pallas_call(body, in_specs=[pl.BlockSpec(memory_space=pltpu.SMEM)] * l...  15.6 us
    pallas_call x1, Pallas kernels, attend(): pl.pallas_call(forward_kernel, in_specs=[vmem] * 3, out_specs=[pl.BlockSp...  10.1 us
  transfers between devices with their start and end apart: 35, of which 15 were waited for; matrix products, arithmetic and copies ran while one was open for 21% of the time, Pallas kernels for 14%

profile of v2, /device:TPU:1, one launch (start us, length us, event | category | flops | bytes accessed | tf_op | source)
XLA Modules:
  0.0 418.9 jit_solution(2078619393368805950)
XLA Ops:
  13.4 10.1 %all-to-all-start = ((bf16[128,8,1152]{2,1,0:T(8,128)(2,1)}), bf16[128,8,1152]{2,1,0:T(8,128)(2,1)S(1)}, u32[]{:S(2)}, u32[]{:S(2)}) async-start(bf16[128,8,1152]{2,1,0:T(8,128)(2,1)} %weights.1), calls=%async_computation | async-start | bytes 4718592 | tf_op jit(solution)/shard_map/all_to_all | solution.py:58
  27.9 29.1 %all-to-all-done = bf16[128,8,1152]{2,1,0:T(8,128)(2,1)S(1)} async-done(((bf16[128,8,1152]{2,1,0:T(8,128)(2,1)}), bf16[128,8,1152]{2,1,0:T(8,128)(2,1)S(1)}, u32[]{:S(2)}, u32[]{:S(2)}) %all-to-all-start) | async-done | bytes 2359328 | tf_op jit(solution)/shard_map/all_to_all | solution.py:58
  66.7 4.6 %all-to-all-start.1 = ((bf16[32,160,128]{2,1,0:T(8,128)(2,1)}), bf16[32,160,128]{2,1,0:T(8,128)(2,1)S(1)}, u32[]{:S(2)}, u32[]{:S(2)}) async-start(bf16[32,160,128]{2,1,0:T(8,128)(2,1)} %pack.1), calls=%async_computation.1 | async-start | bytes 2621440 | tf_op jit(solution)/shard_map/all_to_all | solution.py:58
  76.3 14.4 %all-to-all-done.1.packed = bf16[32,160,128]{2,1,0:T(8,128)(2,1)S(1)} async-done(((bf16[32,160,128]{2,1,0:T(8,128)(2,1)}), bf16[32,160,128]{2,1,0:T(8,128)(2,1)S(1)}, u32[]{:S(2)}, u32[]{:S(2)}) %all-to-all-start.1) | async-done | bytes 1310752 | tf_op jit(solution)/shard_map/all_to_all | solution.py:58
  90.7 10.1 %attend.1 = (bf16[32,32,128]{2,1,0:T(8,128)(2,1)}, f32[8,1,256]{2,1,0:T(1,128)S(1)}) custom-call(bf16[32,160,128]{2,1,0:T(8,128)(2,1)S(1)} %all-to-all-done.1.packed, s32[32,128]{1,0:T(8,128)S(1)} %copy.113.seg_key, s32[8,1,128]{2,1,0:T(1,128)S(1)} %bitcast.248), custom_call_target="tpu_custom_call" | custom-call | flops 13200000000 | bytes 65536 | tf_op jit(solution)/shard_map/attend/pallas_call | solution.py:553
  100.8 7.6 %all-to-all-start.2 = ((bf16[32,32,128]{2,1,0:T(8,128)(2,1)}), bf16[32,32,128]{2,1,0:T(8,128)(2,1)S(1)}, u32[]{:S(2)}, u32[]{:S(2)}) async-start(bf16[32,32,128]{2,1,0:T(8,128)(2,1)} %get-tuple-element.72.mixed), calls=%async_computation.2 | async-start | bytes 524288 | tf_op jit(solution)/shard_map/all_to_all | solution.py:58
  112.5 5.4 %all-to-all-done.2.received = bf16[32,32,128]{2,1,0:T(8,128)(2,1)S(1)} async-done(((bf16[32,32,128]{2,1,0:T(8,128)(2,1)}), bf16[32,32,128]{2,1,0:T(8,128)(2,1)S(1)}, u32[]{:S(2)}, u32[]{:S(2)}) %all-to-all-start.2) | async-done | bytes 262176 | tf_op jit(solution)/shard_map/all_to_all | solution.py:58
  118.6 3.6 collective-permute-start.6
  127.8 7.8 %all-to-all-start.3 = ((bf16[32,32,1024]{2,1,0:T(8,128)(2,1)}), bf16[32,32,1024]{2,1,0:T(8,128)(2,1)}, u32[]{:S(2)}, u32[]{:S(2)}) async-start(bf16[32,32,1024]{2,1,0:T(8,128)(2,1)} %bitcast.257), calls=%async_computation.3 | async-start | bytes 4194304 | tf_op jit(solution)/shard_map/all_to_all | solution.py:58
  146.7 16.1 %all-to-all-done.3 = bf16[32,32,1024]{2,1,0:T(8,128)(2,1)} async-done(((bf16[32,32,1024]{2,1,0:T(8,128)(2,1)}), bf16[32,32,1024]{2,1,0:T(8,128)(2,1)}, u32[]{:S(2)}, u32[]{:S(2)}) %all-to-all-start.3) | async-done | bytes 2097184 | tf_op jit(solution)/shard_map/all_to_all | solution.py:58
  162.7 8.8 %all-to-all-start.4 = ((bf16[32,32,1024]{2,1,0:T(8,128)(2,1)}), bf16[32,32,1024]{2,1,0:T(8,128)(2,1)}, u32[]{:S(2)}, u32[]{:S(2)}) async-start(bf16[32,32,1024]{2,1,0:T(8,128)(2,1)} %bitcast.256), calls=%async_computation.4 | async-start | bytes 4194304 | tf_op jit(solution)/shard_map/all_to_all | solution.py:58
  178.3 5.1 %multiply_convert_fusion.3 = (bf16[1024,512]{1,0:T(8,128)(2,1)S(1)}, f32[1024,512]{1,0:T(8,128)}) fusion(f32[1024,512]{1,0:T(8,128)S(1)} %fusion.73, bf16[1024,1024]{1,0:T(8,128)(2,1)} %bitcast.46, bf16[1024,512]{1,0:T(8,128)(2,1)S(1)} %pad_maximum_fusion.4), kind=kOutput, calls=%fused_computation.8 | convolution fusion | flops 1076887552 | bytes 8388608 | tf_op jit(solution)/shard_map/dot_general | solution.py:38
  187.1 11.1 %all-to-all-done.4 = bf16[32,32,1024]{2,1,0:T(8,128)(2,1)} async-done(((bf16[32,32,1024]{2,1,0:T(8,128)(2,1)}), bf16[32,32,1024]{2,1,0:T(8,128)(2,1)}, u32[]{:S(2)}, u32[]{:S(2)}) %all-to-all-start.4) | async-done | bytes 2097184 | tf_op jit(solution)/shard_map/all_to_all | solution.py:58
  198.2 7.9 %all-to-all-start.5 = ((bf16[32,32,1024]{2,1,0:T(8,128)(2,1)}), bf16[32,32,1024]{2,1,0:T(8,128)(2,1)}, u32[]{:S(2)}, u32[]{:S(2)}) async-start(bf16[32,32,1024]{2,1,0:T(8,128)(2,1)} %bitcast.267), calls=%async_computation.5 | async-start | bytes 4194304 | tf_op jit(solution)/shard_map/all_to_all | solution.py:58
  206.2 8.4 %probabilities.1 = (bf16[8,4096,256]{2,1,0:T(8,128)(2,1)S(1)}, bf16[128,4096]{1,0:T(8,128)(2,1)S(1)}) custom-call(bf16[32,160,128]{2,1,0:T(8,128)(2,1)S(1)} %all-to-all-done.1.packed, s32[32,128]{1,0:T(8,128)S(1)} %copy.113.seg_key, s32[8,1,128]{2,1,0:T(1,128)S(1)} %bitcast.249, f32[8,1,256]{2,1,0:T(1,128)S(1)} %get-tuple-element.87.lse), custom_call_target="tpu_custom_call" | custom-call | flops 12099999744 | bytes 65536 | tf_op jit(solution)/shard_map/probabilities/pallas_call | solution.py:575
  215.8 5.2 %multiply_convert_fusion.1 = (bf16[1024,512]{1,0:T(8,128)(2,1)S(1)}, bf16[1024,512]{1,0:T(8,128)(2,1)S(1)}) fusion(f32[1024,512]{1,0:T(8,128)S(1)} %copy-done.49, f32[1024,512]{1,0:T(8,128)S(1)} %copy-done.50, bf16[1024,1024]{1,0:T(8,128)(2,1)} %bitcast.75, bf16[512,1024]{1,0:T(8,128)(2,1)S(1)} %copy-done.27), kind=kOutput, calls=%fused_computation.6 | convolution fusion | flops 1080557568 | bytes 9437184 | tf_op jit(solution)/shard_map/dot_general | solution.py:38
  226.3 6.6 %all-to-all-done.5 = bf16[32,32,1024]{2,1,0:T(8,128)(2,1)} async-done(((bf16[32,32,1024]{2,1,0:T(8,128)(2,1)}), bf16[32,32,1024]{2,1,0:T(8,128)(2,1)}, u32[]{:S(2)}, u32[]{:S(2)}) %all-to-all-start.5) | async-done | bytes 2097184 | tf_op jit(solution)/shard_map/all_to_all | solution.py:58
  232.9 8.0 %all-to-all-start.6 = ((bf16[32,32,1024]{2,1,0:T(8,128)(2,1)}), bf16[32,32,1024]{2,1,0:T(8,128)(2,1)}, u32[]{:S(2)}, u32[]{:S(2)}) async-start(bf16[32,32,1024]{2,1,0:T(8,128)(2,1)} %bitcast.258), calls=%async_computation.6 | async-start | bytes 4194304 | tf_op jit(solution)/shard_map/all_to_all | solution.py:58
  241.3 3.2 fusion.3
  249.0 4.2 %convolution_convert_fusion.4 = bf16[512,1024]{1,0:T(8,128)(2,1)} fusion(bf16[1024,512]{1,0:T(8,128)(2,1)} %copy-done.29, bf16[1024,1024]{1,0:T(8,128)(2,1)} %bitcast.75), kind=kOutput, calls=%fused_computation.16 | convolution fusion | flops 1074266112 | bytes 4194304 | tf_op jit(solution)/shard_map/dot_general | solution.py:38
  258.0 9.8 %all-to-all-done.6 = bf16[32,32,1024]{2,1,0:T(8,128)(2,1)} async-done(((bf16[32,32,1024]{2,1,0:T(8,128)(2,1)}), bf16[32,32,1024]{2,1,0:T(8,128)(2,1)}, u32[]{:S(2)}, u32[]{:S(2)}) %all-to-all-start.6) | async-done | bytes 2097184 | tf_op jit(solution)/shard_map/all_to_all | solution.py:58
  276.2 6.4 %all-to-all-start.7 = ((bf16[32,32,128]{2,1,0:T(8,128)(2,1)}), bf16[32,32,128]{2,1,0:T(8,128)(2,1)S(1)}, u32[]{:S(2)}, u32[]{:S(2)}) async-start(bf16[32,32,128]{2,1,0:T(8,128)(2,1)} %heads_out.1), calls=%async_computation.7 | async-start | bytes 524288 | tf_op jit(solution)/shard_map/all_to_all | solution.py:58
  285.2 9.3 %all-to-all-done.7.upper = bf16[32,32,128]{2,1,0:T(8,128)(2,1)S(1)} async-done(((bf16[32,32,128]{2,1,0:T(8,128)(2,1)}), bf16[32,32,128]{2,1,0:T(8,128)(2,1)S(1)}, u32[]{:S(2)}, u32[]{:S(2)}) %all-to-all-start.7) | async-done | bytes 262176 | tf_op jit(solution)/shard_map/all_to_all | solution.py:58
  294.5 6.7 %all-to-all-start.8 = ((bf16[128,8,640]{2,1,0:T(8,128)(2,1)}), bf16[128,8,640]{2,1,0:T(8,128)(2,1)}, u32[]{:S(2)}, u32[]{:S(2)}) async-start(bf16[128,8,640]{2,1,0:T(8,128)(2,1)} %bitcast.95), calls=%async_computation.8 | async-start | bytes 2621440 | tf_op jit(solution)/shard_map/all_to_all | solution.py:58
  302.4 21.7 %attend_back.1 = bf16[32,160,128]{2,1,0:T(8,128)(2,1)} custom-call(bf16[32,160,128]{2,1,0:T(8,128)(2,1)S(1)} %all-to-all-done.1.packed, bf16[8,4096,256]{2,1,0:T(8,128)(2,1)} %copy-done.6, bf16[128,4096]{1,0:T(8,128)(2,1)S(1)} %copy-done.8, bf16[32,32,128]{2,1,0:T(8,128)(2,1)S(1)} %all-to-all-done.7.upper, bf16[32,32,128]{2,1,0:T(8,128)(2,1)} %get-tuple-element.72.mixed), custom_call_target="tpu_custom_call" | custom-call | flops 23100000256 | bytes 65536 | tf_op jit(solution)/shard_map/attend_back/pallas_call | solution.py:599
  324.1 10.3 %all-to-all-start.9 = ((bf16[32,160,128]{2,1,0:T(8,128)(2,1)}), bf16[32,160,128]{2,1,0:T(8,128)(2,1)S(1)}, u32[]{:S(2)}, u32[]{:S(2)}) async-start(bf16[32,160,128]{2,1,0:T(8,128)(2,1)} %attend_back.1), calls=%async_computation.9 | async-start | bytes 2621440 | tf_op jit(solution)/shard_map/all_to_all | solution.py:58
  335.3 18.4 %all-to-all-done.9.refs_0_ = bf16[32,160,128]{2,1,0:T(8,128)(2,1)S(1)} async-done(((bf16[32,160,128]{2,1,0:T(8,128)(2,1)}), bf16[32,160,128]{2,1,0:T(8,128)(2,1)S(1)}, u32[]{:S(2)}, u32[]{:S(2)}) %all-to-all-start.9) | async-done | bytes 1310752 | tf_op jit(solution)/shard_map/all_to_all | solution.py:58
  354.7 3.6 unpack.1
  362.5 5.8 %finish.1 = (bf16[1024,1152]{1,0:T(8,128)(2,1)}, f32[256,1024]{1,0:T(8,128)}) custom-call(s32[2]{0:T(128)} %pad_add_fusion.refs_0_, f32[256,1024]{1,0:T(8,128)} %get-tuple-element.101.refs_1_, f32[256,1024]{1,0:T(8,128)} %copy-done.5, f32[256,128]{1,0:T(8,128)} %broadcast_select_fusion.refs_2_.refs_3_, f32[256,128]{1,0:T(8,128)} %get-tuple-element.102.refs_4_, ...), custom_call_target="tpu_custom_call" | custom-call | flops 4400000000 | bytes 65536 | tf_op jit(solution)/shard_map/finish/pallas_call | solution.py:179
  368.3 4.9 %all-to-all-start.10 = ((bf16[128,8,1152]{2,1,0:T(8,128)(2,1)}), bf16[128,8,1152]{2,1,0:T(8,128)(2,1)}, u32[]{:S(2)}, u32[]{:S(2)}) async-start(bf16[128,8,1152]{2,1,0:T(8,128)(2,1)} %bitcast.262), calls=%async_computation.10 | async-start | bytes 4718592 | tf_op jit(solution)/shard_map/all_to_all | solution.py:58
  388.0 20.5 %all-to-all-done.10.refs_1_ = bf16[128,8,1152]{2,1,0:T(8,128)(2,1)} async-done(((bf16[128,8,1152]{2,1,0:T(8,128)(2,1)}), bf16[128,8,1152]{2,1,0:T(8,128)(2,1)}, u32[]{:S(2)}, u32[]{:S(2)}) %all-to-all-start.10) | async-done | bytes 2359328 | tf_op jit(solution)/shard_map/all_to_all | solution.py:58
  408.5 3.6 final.1
  (287 shorter events, 105.5 us)
Async XLA Ops:
  7.2 5.9 %collective-permute-start.1 = (bf16[8,1024]{1,0:T(8,128)(2,1)}, bf16[8,1024]{1,0:T(8,128)(2,1)S(1)}, u32[]{:S(2)}, u32[]{:S(2)}) collective-permute-start(bf16[8,1024]{1,0:T(8,128)(2,1)} %param.29), channel_id=1, source_target_pairs={{0,1},{1,0},{2,3},{3,2},{4,5},{5,4},{6,7},{7,6},{8,9},{9,8},{10,11... | collective-permute-start | bytes 49160 | tf_op jit(solution)/shard_map/ppermute | solution.py:42
  8.7 4.4 %collective-permute-start.2 = (bf16[8,1024]{1,0:T(8,128)(2,1)}, bf16[8,1024]{1,0:T(8,128)(2,1)S(1)}, u32[]{:S(2)}, u32[]{:S(2)}) collective-permute-start(bf16[8,1024]{1,0:T(8,128)(2,1)} %param.29), channel_id=1, source_target_pairs={{0,2},{1,3},{2,0},{3,1},{4,6},{5,7},{6,4},{7,5},{8,10},{9,11},{10,... | collective-permute-start | bytes 49160 | tf_op jit(solution)/shard_map/ppermute | solution.py:42
  10.0 3.4 collective-permute-start.3
  13.4 43.6 %all-to-all-start = ((bf16[128,8,1152]{2,1,0:T(8,128)(2,1)}), bf16[128,8,1152]{2,1,0:T(8,128)(2,1)S(1)}, u32[]{:S(2)}, u32[]{:S(2)}) async-start(bf16[128,8,1152]{2,1,0:T(8,128)(2,1)} %weights.1), calls=%async_computation | async-start | bytes 4718592 | tf_op jit(solution)/shard_map/all_to_all | solution.py:58
  23.5 98.8 %all-gather.2.cloned.1.call-start = ((), (), s32[]{:S(2)}) async-start(), calls=%async_computation.13 | async-start | bytes 2162688 | tf_op jit(solution)/shard_map/all_gather | solution.py:680
  23.5 4.2 collective-permute-start
  66.7 24.0 %all-to-all-start.1 = ((bf16[32,160,128]{2,1,0:T(8,128)(2,1)}), bf16[32,160,128]{2,1,0:T(8,128)(2,1)S(1)}, u32[]{:S(2)}, u32[]{:S(2)}) async-start(bf16[32,160,128]{2,1,0:T(8,128)(2,1)} %pack.1), calls=%async_computation.1 | async-start | bytes 2621440 | tf_op jit(solution)/shard_map/all_to_all | solution.py:58
  100.8 17.1 %all-to-all-start.2 = ((bf16[32,32,128]{2,1,0:T(8,128)(2,1)}), bf16[32,32,128]{2,1,0:T(8,128)(2,1)S(1)}, u32[]{:S(2)}, u32[]{:S(2)}) async-start(bf16[32,32,128]{2,1,0:T(8,128)(2,1)} %get-tuple-element.72.mixed), calls=%async_computation.2 | async-start | bytes 524288 | tf_op jit(solution)/shard_map/all_to_all | solution.py:58
  109.0 14.8 %collective-permute-start.14 = (bf16[128,1024]{1,0:T(8,128)(2,1)}, bf16[128,1024]{1,0:T(8,128)(2,1)S(1)}, u32[]{:S(2)}, u32[]{:S(2)}) collective-permute-start(bf16[128,1024]{1,0:T(8,128)(2,1)} %bitcast.20), channel_id=1, source_target_pairs={{0,2},{1,3},{2,0},{3,1},{4,6},{5,7},{6,4},{7,5},{8,10},{9,11},{10,... | collective-permute-start | bytes 786440 | tf_op jit(solution)/shard_map/ppermute | solution.py:42
  109.1 30.5 %collective-permute-start.13 = (bf16[128,1024]{1,0:T(8,128)(2,1)}, bf16[128,1024]{1,0:T(8,128)(2,1)}, u32[]{:S(2)}, u32[]{:S(2)}) collective-permute-start(bf16[128,1024]{1,0:T(8,128)(2,1)} %bitcast.20), channel_id=1, source_target_pairs={{0,1},{1,0},{2,3},{3,2},{4,5},{5,4},{6,7},{7,6},{8,9},{9,8},{10,11... | collective-permute-start | bytes 786440 | tf_op jit(solution)/shard_map/ppermute | solution.py:42
  110.6 29.3 %collective-permute-start.11 = (bf16[256,512]{1,0:T(8,128)(2,1)}, bf16[256,512]{1,0:T(8,128)(2,1)}, u32[]{:S(2)}, u32[]{:S(2)}) collective-permute-start(bf16[256,512]{1,0:T(8,128)(2,1)} %bitcast.19), channel_id=1, source_target_pairs={{0,2},{1,3},{2,0},{3,1},{4,6},{5,7},{6,4},{7,5},{8,10},{9,11},{10,... | collective-permute-start | bytes 786440 | tf_op jit(solution)/shard_map/ppermute | solution.py:42
  112.2 29.5 %collective-permute-start.10 = (bf16[256,512]{1,0:T(8,128)(2,1)}, bf16[256,512]{1,0:T(8,128)(2,1)}, u32[]{:S(2)}, u32[]{:S(2)}) collective-permute-start(bf16[256,512]{1,0:T(8,128)(2,1)} %bitcast.19), channel_id=1, source_target_pairs={{0,1},{1,0},{2,3},{3,2},{4,5},{5,4},{6,7},{7,6},{8,9},{9,8},{10,11... | collective-permute-start | bytes 786440 | tf_op jit(solution)/shard_map/ppermute | solution.py:42
  118.6 5.3 %collective-permute-start.6 = (bf16[128,512]{1,0:T(8,128)(2,1)S(1)}, bf16[128,512]{1,0:T(8,128)(2,1)S(1)}, u32[]{:S(2)}, u32[]{:S(2)}) collective-permute-start(bf16[128,512]{1,0:T(8,128)(2,1)S(1)} %get-tuple-element.153), channel_id=1, source_target_pairs={{0,1},{1,0},{2,3},{3,2},{4,5},{5,4},{6,7},{7,6},{8,9},{9,8},{10,11... | collective-permute-start | bytes 393224 | tf_op jit(solution)/shard_map/ppermute | solution.py:42
  123.8 16.3 %collective-permute-start.8 = (bf16[256,512]{1,0:T(8,128)(2,1)}, bf16[256,512]{1,0:T(8,128)(2,1)}, u32[]{:S(2)}, u32[]{:S(2)}) collective-permute-start(bf16[256,512]{1,0:T(8,128)(2,1)} %bitcast.18), channel_id=1, source_target_pairs={{0,2},{1,3},{2,0},{3,1},{4,6},{5,7},{6,4},{7,5},{8,10},{9,11},{10,... | collective-permute-start | bytes 786440 | tf_op jit(solution)/shard_map/ppermute | solution.py:42
  123.9 16.5 %collective-permute-start.15 = (bf16[128,1024]{1,0:T(8,128)(2,1)S(1)}, bf16[128,1024]{1,0:T(8,128)(2,1)S(1)}, u32[]{:S(2)}, u32[]{:S(2)}) collective-permute-start(bf16[128,1024]{1,0:T(8,128)(2,1)S(1)} %collective-permute-done.14), channel_id=1, source_target_pairs={{0,1},{1,0},{2,3},{3,2},{4,5},{5,4},{6,7},{7,6},{8,9},{9,8},{10,11... | collective-permute-start | bytes 786440 | tf_op jit(solution)/shard_map/ppermute | solution.py:42
  127.8 35.0 %all-to-all-start.3 = ((bf16[32,32,1024]{2,1,0:T(8,128)(2,1)}), bf16[32,32,1024]{2,1,0:T(8,128)(2,1)}, u32[]{:S(2)}, u32[]{:S(2)}) async-start(bf16[32,32,1024]{2,1,0:T(8,128)(2,1)} %bitcast.257), calls=%async_computation.3 | async-start | bytes 4194304 | tf_op jit(solution)/shard_map/all_to_all | solution.py:58
  139.6 3.5 collective-permute-start.7
  140.1 3.0 collective-permute-start.9
  162.7 35.5 %all-to-all-start.4 = ((bf16[32,32,1024]{2,1,0:T(8,128)(2,1)}), bf16[32,32,1024]{2,1,0:T(8,128)(2,1)}, u32[]{:S(2)}, u32[]{:S(2)}) async-start(bf16[32,32,1024]{2,1,0:T(8,128)(2,1)} %bitcast.256), calls=%async_computation.4 | async-start | bytes 4194304 | tf_op jit(solution)/shard_map/all_to_all | solution.py:58
  174.0 40.6 %collective-permute-start.16 = (bf16[128,1024]{1,0:T(8,128)(2,1)}, bf16[128,1024]{1,0:T(8,128)(2,1)}, u32[]{:S(2)}, u32[]{:S(2)}) collective-permute-start(bf16[128,1024]{1,0:T(8,128)(2,1)} %pad_maximum_fusion.9), channel_id=1, source_target_pairs={{0,1},{1,0},{2,3},{3,2},{4,5},{5,4},{6,7},{7,6},{8,9},{9,8},{10,11... | collective-permute-start | bytes 786440 | tf_op jit(solution)/shard_map/ppermute | solution.py:42
  198.2 34.7 %all-to-all-start.5 = ((bf16[32,32,1024]{2,1,0:T(8,128)(2,1)}), bf16[32,32,1024]{2,1,0:T(8,128)(2,1)}, u32[]{:S(2)}, u32[]{:S(2)}) async-start(bf16[32,32,1024]{2,1,0:T(8,128)(2,1)} %bitcast.267), calls=%async_computation.5 | async-start | bytes 4194304 | tf_op jit(solution)/shard_map/all_to_all | solution.py:58
  232.9 34.9 %all-to-all-start.6 = ((bf16[32,32,1024]{2,1,0:T(8,128)(2,1)}), bf16[32,32,1024]{2,1,0:T(8,128)(2,1)}, u32[]{:S(2)}, u32[]{:S(2)}) async-start(bf16[32,32,1024]{2,1,0:T(8,128)(2,1)} %bitcast.258), calls=%async_computation.6 | async-start | bytes 4194304 | tf_op jit(solution)/shard_map/all_to_all | solution.py:58
  240.8 143.2 %reduce-scatter.3.cloned.1.call-start = ((), (), s32[]{:S(2)}) async-start(), calls=%async_computation.14 | async-start | bytes 2621440 | tf_op jit(solution)/shard_map/reduce_scatter | solution.py:828
  271.6 3.8 collective-permute-start.18
  274.8 7.7 %collective-permute-start.17 = (bf16[128,512]{1,0:T(8,128)(2,1)}, bf16[128,512]{1,0:T(8,128)(2,1)}, u32[]{:S(2)}, u32[]{:S(2)}) collective-permute-start(bf16[128,512]{1,0:T(8,128)(2,1)} %get-tuple-element.147), channel_id=1, source_target_pairs={{0,1},{1,0},{2,3},{3,2},{4,5},{5,4},{6,7},{7,6},{8,9},{9,8},{10,11... | collective-permute-start | bytes 393224 | tf_op jit(solution)/shard_map/ppermute | solution.py:42
  276.2 18.4 %all-to-all-start.7 = ((bf16[32,32,128]{2,1,0:T(8,128)(2,1)}), bf16[32,32,128]{2,1,0:T(8,128)(2,1)S(1)}, u32[]{:S(2)}, u32[]{:S(2)}) async-start(bf16[32,32,128]{2,1,0:T(8,128)(2,1)} %heads_out.1), calls=%async_computation.7 | async-start | bytes 524288 | tf_op jit(solution)/shard_map/all_to_all | solution.py:58
  294.5 29.6 %all-to-all-start.8 = ((bf16[128,8,640]{2,1,0:T(8,128)(2,1)}), bf16[128,8,640]{2,1,0:T(8,128)(2,1)}, u32[]{:S(2)}, u32[]{:S(2)}) async-start(bf16[128,8,640]{2,1,0:T(8,128)(2,1)} %bitcast.95), calls=%async_computation.8 | async-start | bytes 2621440 | tf_op jit(solution)/shard_map/all_to_all | solution.py:58
  324.1 29.5 %all-to-all-start.9 = ((bf16[32,160,128]{2,1,0:T(8,128)(2,1)}), bf16[32,160,128]{2,1,0:T(8,128)(2,1)S(1)}, u32[]{:S(2)}, u32[]{:S(2)}) async-start(bf16[32,160,128]{2,1,0:T(8,128)(2,1)} %attend_back.1), calls=%async_computation.9 | async-start | bytes 2621440 | tf_op jit(solution)/shard_map/all_to_all | solution.py:58
  334.4 51.8 %reduce-scatter.5.cloned.1.call-start = ((), (), s32[]{:S(2)}) async-start(), calls=%async_computation.15 | async-start | bytes 1310720 | tf_op jit(solution)/shard_map/reduce_scatter | solution.py:887
  358.3 3.6 collective-permute-start.19
  368.3 40.2 %all-to-all-start.10 = ((bf16[128,8,1152]{2,1,0:T(8,128)(2,1)}), bf16[128,8,1152]{2,1,0:T(8,128)(2,1)}, u32[]{:S(2)}, u32[]{:S(2)}) async-start(bf16[128,8,1152]{2,1,0:T(8,128)(2,1)} %bitcast.262), calls=%async_computation.10 | async-start | bytes 4718592 | tf_op jit(solution)/shard_map/all_to_all | solution.py:58
  380.0 2.8 collective-permute-start.20
  (55 other events, 568.1 us)
Sparse Core Ops, SparseCore 0:
  28.0 90.8 all-gather.1
  275.5 30.7 reduce-scatter.2
  361.9 19.3 reduce-scatter.4

commit v3 on v2

--- a/solution.py
+++ b/solution.py
@@ -325,11 +325,14 @@
         last_small[at, :] = jnp.where(lanes((TOK, TOK)) < HD, block, known).astype(BF)
 
 
-def final_kernel(ids, parts, query, key, value, attn_gain, query_gain, key_gain):
-    def column(t):
-        piece = parts[:, :, t * 128 : t * 128 + 128].astype(F32)
-        return jnp.sum(piece.reshape(4 * N_CTX // PARTS, PARTS, 8, 128), axis=0)
-
+def final_kernel(ids, *refs):
+    pieces, (query, key, value, attn_gain, query_gain, key_gain) = refs[:-6], refs[-6:]
+    sums = [0.0] * (COLS // 128 + 1)
+    for piece in pieces:
+        for t in range(len(sums)):
+            block = piece[:, :, t * 128 : t * 128 + 128].astype(F32)
+            sums[t] = sums[t] + jnp.sum(block.reshape(-1, PARTS, 8, 128), axis=0)
+    column = sums.__getitem__
     low_half = lanes((8, 128)) < HD
     for h in range(0, PART_HEADS, 2):
         first, second = column(2 * h), column(2 * h + 2)
@@ -609,7 +612,7 @@
         out_specs=whole((N_CTX, PACK, 128)),
         out_shape=jax.ShapeDtypeStruct((N_CTX, PACK, 128), BF),
         scratch_shapes=[pltpu.VMEM((KEYS, 128), BF), pltpu.VMEM((KEYS, 128), F32)],
-        compiler_params=pltpu.CompilerParams(vmem_limit_bytes=40 << 20),
+        compiler_params=pltpu.CompilerParams(vmem_limit_bytes=VMEM_LIMIT),
         cost_estimate=estimate(21),
         name="attend_back",
     )(packed, probs, kv_t, upper, mixed)
@@ -945,7 +948,7 @@
     last_sums, ready, final_ids = lax.optimization_barrier((last_sums, ready, final_ids))
     grad_query, grad_key, grad_value, attn_gain, query_gain, key_gain = call(
         final_kernel,
-        (last_sums,),
+        tuple(far(last_sums, cut=(slice(k * 32, k * 32 + 32),)) for k in range(4)),
         [
             ((8, 1024), F32),
             ((8, 512), F32),

time: 426 us -> 425 us (level)
    all_to_all x11, waiting for transfers between devices: 141 us -> 145 us  [exchange(): return lax.all_to_all(array, axis, split_axis=0, concat_axis=0, tiled=True)]
  transfers between devices with their start and end apart: 35 -> 35, of which waited for: 15 -> 15; matrix products, arithmetic and copies ran while one was open for 21% -> 20% of each run, Pallas kernels for 14% -> 14%
where the time goes in v3:
time: 425 us; the launch traced here: 418 us
  waiting for transfers between devices  147 us (35%)
  starting transfers between devices  104 us (24%)
  Pallas kernels  60.8 us (14%)
  matrix products  53.3 us (13%)
  other arithmetic  25.3 us (6%)
  between operations  15.3 us (4%)
  local copies, waits for them, and re-layouts  11.8 us (3%)
    all_to_all x11, waiting for transfers between devices, exchange(): return lax.all_to_all(array, axis, split_axis=0, concat_axis=0, tiled=True)  145 us
    all_to_all x11, starting transfers between devices, exchange(): return lax.all_to_all(array, axis, split_axis=0, concat_axis=0, tiled=True)  82.4 us
    dot_general x22, matrix products, dot(): return lax.dot_general(a, b, (dims, ((), ())), preferred_element_type=F32)  53.3 us
    pallas_call x1, Pallas kernels, attend_back(): pl.pallas_call(backward_kernel, grid=(TILES,), in_specs=[whole((N_CTX, PA...  22.4 us
    ppermute x21, starting transfers between devices, swap(): lax.ppermute(array, 'fsdp', [(i, i ^ j) for i in range(4)])  21.3 us
    pallas_call x4, Pallas kernels, call(): pl.pallas_call(body, in_specs=[pl.BlockSpec(memory_space=pltpu.SMEM)] * l...  15.4 us
    pallas_call x1, Pallas kernels, attend(): pl.pallas_call(forward_kernel, in_specs=[vmem] * 3, out_specs=[pl.BlockSp...  10.1 us
  transfers between devices with their start and end apart: 35, of which 15 were waited for; matrix products, arithmetic and copies ran while one was open for 20% of the time, Pallas kernels for 14%

profile of v3, /device:TPU:1, one launch (start us, length us, event | category | flops | bytes accessed | tf_op | source)
XLA Modules:
  0.0 418.1 jit_solution(6649713001063506223)
XLA Ops:
  13.4 10.1 %all-to-all-start = ((bf16[128,8,1152]{2,1,0:T(8,128)(2,1)}), bf16[128,8,1152]{2,1,0:T(8,128)(2,1)S(1)}, u32[]{:S(2)}, u32[]{:S(2)}) async-start(bf16[128,8,1152]{2,1,0:T(8,128)(2,1)} %weights.1), calls=%async_computation | async-start | bytes 4718592 | tf_op jit(solution)/shard_map/all_to_all | solution.py:58
  27.9 29.1 %all-to-all-done = bf16[128,8,1152]{2,1,0:T(8,128)(2,1)S(1)} async-done(((bf16[128,8,1152]{2,1,0:T(8,128)(2,1)}), bf16[128,8,1152]{2,1,0:T(8,128)(2,1)S(1)}, u32[]{:S(2)}, u32[]{:S(2)}) %all-to-all-start) | async-done | bytes 2359328 | tf_op jit(solution)/shard_map/all_to_all | solution.py:58
  66.7 4.6 %all-to-all-start.1 = ((bf16[32,160,128]{2,1,0:T(8,128)(2,1)}), bf16[32,160,128]{2,1,0:T(8,128)(2,1)S(1)}, u32[]{:S(2)}, u32[]{:S(2)}) async-start(bf16[32,160,128]{2,1,0:T(8,128)(2,1)} %pack.1), calls=%async_computation.1 | async-start | bytes 2621440 | tf_op jit(solution)/shard_map/all_to_all | solution.py:58
  76.3 14.4 %all-to-all-done.1.packed = bf16[32,160,128]{2,1,0:T(8,128)(2,1)S(1)} async-done(((bf16[32,160,128]{2,1,0:T(8,128)(2,1)}), bf16[32,160,128]{2,1,0:T(8,128)(2,1)S(1)}, u32[]{:S(2)}, u32[]{:S(2)}) %all-to-all-start.1) | async-done | bytes 1310752 | tf_op jit(solution)/shard_map/all_to_all | solution.py:58
  90.7 10.1 %attend.1 = (bf16[32,32,128]{2,1,0:T(8,128)(2,1)}, f32[8,1,256]{2,1,0:T(1,128)S(1)}) custom-call(bf16[32,160,128]{2,1,0:T(8,128)(2,1)S(1)} %all-to-all-done.1.packed, s32[32,128]{1,0:T(8,128)S(1)} %copy.113.seg_key, s32[8,1,128]{2,1,0:T(1,128)S(1)} %bitcast.248), custom_call_target="tpu_custom_call" | custom-call | flops 13200000000 | bytes 65536 | tf_op jit(solution)/shard_map/attend/pallas_call | solution.py:556
  100.8 7.6 %all-to-all-start.2 = ((bf16[32,32,128]{2,1,0:T(8,128)(2,1)}), bf16[32,32,128]{2,1,0:T(8,128)(2,1)S(1)}, u32[]{:S(2)}, u32[]{:S(2)}) async-start(bf16[32,32,128]{2,1,0:T(8,128)(2,1)} %get-tuple-element.72.mixed), calls=%async_computation.2 | async-start | bytes 524288 | tf_op jit(solution)/shard_map/all_to_all | solution.py:58
  112.6 5.3 %all-to-all-done.2.received = bf16[32,32,128]{2,1,0:T(8,128)(2,1)S(1)} async-done(((bf16[32,32,128]{2,1,0:T(8,128)(2,1)}), bf16[32,32,128]{2,1,0:T(8,128)(2,1)S(1)}, u32[]{:S(2)}, u32[]{:S(2)}) %all-to-all-start.2) | async-done | bytes 262176 | tf_op jit(solution)/shard_map/all_to_all | solution.py:58
  118.6 3.6 collective-permute-start.6
  127.8 7.8 %all-to-all-start.3 = ((bf16[32,32,1024]{2,1,0:T(8,128)(2,1)}), bf16[32,32,1024]{2,1,0:T(8,128)(2,1)}, u32[]{:S(2)}, u32[]{:S(2)}) async-start(bf16[32,32,1024]{2,1,0:T(8,128)(2,1)} %bitcast.257), calls=%async_computation.3 | async-start | bytes 4194304 | tf_op jit(solution)/shard_map/all_to_all | solution.py:58
  146.6 16.2 %all-to-all-done.3 = bf16[32,32,1024]{2,1,0:T(8,128)(2,1)} async-done(((bf16[32,32,1024]{2,1,0:T(8,128)(2,1)}), bf16[32,32,1024]{2,1,0:T(8,128)(2,1)}, u32[]{:S(2)}, u32[]{:S(2)}) %all-to-all-start.3) | async-done | bytes 2097184 | tf_op jit(solution)/shard_map/all_to_all | solution.py:58
  162.8 8.8 %all-to-all-start.4 = ((bf16[32,32,1024]{2,1,0:T(8,128)(2,1)}), bf16[32,32,1024]{2,1,0:T(8,128)(2,1)}, u32[]{:S(2)}, u32[]{:S(2)}) async-start(bf16[32,32,1024]{2,1,0:T(8,128)(2,1)} %bitcast.256), calls=%async_computation.4 | async-start | bytes 4194304 | tf_op jit(solution)/shard_map/all_to_all | solution.py:58
  178.4 5.1 %multiply_convert_fusion.3 = (bf16[1024,512]{1,0:T(8,128)(2,1)S(1)}, f32[1024,512]{1,0:T(8,128)}) fusion(f32[1024,512]{1,0:T(8,128)S(1)} %fusion.73, bf16[1024,1024]{1,0:T(8,128)(2,1)} %bitcast.46, bf16[1024,512]{1,0:T(8,128)(2,1)S(1)} %pad_maximum_fusion.4), kind=kOutput, calls=%fused_computation.8 | convolution fusion | flops 1076887552 | bytes 8388608 | tf_op jit(solution)/shard_map/dot_general | solution.py:38
  187.2 11.1 %all-to-all-done.4 = bf16[32,32,1024]{2,1,0:T(8,128)(2,1)} async-done(((bf16[32,32,1024]{2,1,0:T(8,128)(2,1)}), bf16[32,32,1024]{2,1,0:T(8,128)(2,1)}, u32[]{:S(2)}, u32[]{:S(2)}) %all-to-all-start.4) | async-done | bytes 2097184 | tf_op jit(solution)/shard_map/all_to_all | solution.py:58
  198.2 7.9 %all-to-all-start.5 = ((bf16[32,32,1024]{2,1,0:T(8,128)(2,1)}), bf16[32,32,1024]{2,1,0:T(8,128)(2,1)}, u32[]{:S(2)}, u32[]{:S(2)}) async-start(bf16[32,32,1024]{2,1,0:T(8,128)(2,1)} %bitcast.268), calls=%async_computation.5 | async-start | bytes 4194304 | tf_op jit(solution)/shard_map/all_to_all | solution.py:58
  206.2 8.4 %probabilities.1 = (bf16[8,4096,256]{2,1,0:T(8,128)(2,1)S(1)}, bf16[128,4096]{1,0:T(8,128)(2,1)S(1)}) custom-call(bf16[32,160,128]{2,1,0:T(8,128)(2,1)S(1)} %all-to-all-done.1.packed, s32[32,128]{1,0:T(8,128)S(1)} %copy.113.seg_key, s32[8,1,128]{2,1,0:T(1,128)S(1)} %bitcast.249, f32[8,1,256]{2,1,0:T(1,128)S(1)} %get-tuple-element.87.lse), custom_call_target="tpu_custom_call" | custom-call | flops 12099999744 | bytes 65536 | tf_op jit(solution)/shard_map/probabilities/pallas_call | solution.py:578
  215.8 5.2 %multiply_convert_fusion.1 = (bf16[1024,512]{1,0:T(8,128)(2,1)S(1)}, bf16[1024,512]{1,0:T(8,128)(2,1)S(1)}) fusion(f32[1024,512]{1,0:T(8,128)S(1)} %copy-done.49, f32[1024,512]{1,0:T(8,128)S(1)} %copy-done.50, bf16[1024,1024]{1,0:T(8,128)(2,1)} %bitcast.75, bf16[512,1024]{1,0:T(8,128)(2,1)S(1)} %copy-done.25), kind=kOutput, calls=%fused_computation.6 | convolution fusion | flops 1080557568 | bytes 9437184 | tf_op jit(solution)/shard_map/dot_general | solution.py:38
  225.6 7.2 %all-to-all-done.5 = bf16[32,32,1024]{2,1,0:T(8,128)(2,1)} async-done(((bf16[32,32,1024]{2,1,0:T(8,128)(2,1)}), bf16[32,32,1024]{2,1,0:T(8,128)(2,1)}, u32[]{:S(2)}, u32[]{:S(2)}) %all-to-all-start.5) | async-done | bytes 2097184 | tf_op jit(solution)/shard_map/all_to_all | solution.py:58
  232.8 8.0 %all-to-all-start.6 = ((bf16[32,32,1024]{2,1,0:T(8,128)(2,1)}), bf16[32,32,1024]{2,1,0:T(8,128)(2,1)}, u32[]{:S(2)}, u32[]{:S(2)}) async-start(bf16[32,32,1024]{2,1,0:T(8,128)(2,1)} %bitcast.258), calls=%async_computation.6 | async-start | bytes 4194304 | tf_op jit(solution)/shard_map/all_to_all | solution.py:58
  241.3 3.2 fusion.3
  249.0 4.2 %convolution_convert_fusion.4 = bf16[512,1024]{1,0:T(8,128)(2,1)} fusion(bf16[1024,512]{1,0:T(8,128)(2,1)} %copy-done.27, bf16[1024,1024]{1,0:T(8,128)(2,1)} %bitcast.75), kind=kOutput, calls=%fused_computation.16 | convolution fusion | flops 1074266112 | bytes 4194304 | tf_op jit(solution)/shard_map/dot_general | solution.py:38
  257.2 10.6 %all-to-all-done.6 = bf16[32,32,1024]{2,1,0:T(8,128)(2,1)} async-done(((bf16[32,32,1024]{2,1,0:T(8,128)(2,1)}), bf16[32,32,1024]{2,1,0:T(8,128)(2,1)}, u32[]{:S(2)}, u32[]{:S(2)}) %all-to-all-start.6) | async-done | bytes 2097184 | tf_op jit(solution)/shard_map/all_to_all | solution.py:58
  275.1 6.4 %all-to-all-start.7 = ((bf16[32,32,128]{2,1,0:T(8,128)(2,1)}), bf16[32,32,128]{2,1,0:T(8,128)(2,1)S(1)}, u32[]{:S(2)}, u32[]{:S(2)}) async-start(bf16[32,32,128]{2,1,0:T(8,128)(2,1)} %heads_out.1), calls=%async_computation.7 | async-start | bytes 524288 | tf_op jit(solution)/shard_map/all_to_all | solution.py:58
  283.3 10.1 %all-to-all-done.7.upper = bf16[32,32,128]{2,1,0:T(8,128)(2,1)S(1)} async-done(((bf16[32,32,128]{2,1,0:T(8,128)(2,1)}), bf16[32,32,128]{2,1,0:T(8,128)(2,1)S(1)}, u32[]{:S(2)}, u32[]{:S(2)}) %all-to-all-start.7) | async-done | bytes 262176 | tf_op jit(solution)/shard_map/all_to_all | solution.py:58
  294.1 6.3 %all-to-all-start.8 = ((bf16[128,8,640]{2,1,0:T(8,128)(2,1)}), bf16[128,8,640]{2,1,0:T(8,128)(2,1)S(1)}, u32[]{:S(2)}, u32[]{:S(2)}) async-start(bf16[128,8,640]{2,1,0:T(8,128)(2,1)} %bitcast.95), calls=%async_computation.8 | async-start | bytes 2621440 | tf_op jit(solution)/shard_map/all_to_all | solution.py:58
  300.4 22.4 %attend_back.1 = bf16[32,160,128]{2,1,0:T(8,128)(2,1)} custom-call(bf16[32,160,128]{2,1,0:T(8,128)(2,1)} %copy-done.2, bf16[8,4096,256]{2,1,0:T(8,128)(2,1)} %copy-done.7, bf16[128,4096]{1,0:T(8,128)(2,1)} %copy-done.8, bf16[32,32,128]{2,1,0:T(8,128)(2,1)} %copy-done.36, bf16[32,32,128]{2,1,0:T(8,128)(2,1)} %get-tuple-element.72.mixed), custom_call_target="tpu_custom_call" | custom-call | flops 23100000256 | bytes 65536 | tf_op jit(solution)/shard_map/attend_back/pallas_call | solution.py:602
  322.8 10.2 %all-to-all-start.9 = ((bf16[32,160,128]{2,1,0:T(8,128)(2,1)}), bf16[32,160,128]{2,1,0:T(8,128)(2,1)}, u32[]{:S(2)}, u32[]{:S(2)}) async-start(bf16[32,160,128]{2,1,0:T(8,128)(2,1)} %attend_back.1), calls=%async_computation.9 | async-start | bytes 2621440 | tf_op jit(solution)/shard_map/all_to_all | solution.py:58
  333.9 18.4 %all-to-all-done.9.refs_0_ = bf16[32,160,128]{2,1,0:T(8,128)(2,1)} async-done(((bf16[32,160,128]{2,1,0:T(8,128)(2,1)}), bf16[32,160,128]{2,1,0:T(8,128)(2,1)}, u32[]{:S(2)}, u32[]{:S(2)}) %all-to-all-start.9) | async-done | bytes 1310752 | tf_op jit(solution)/shard_map/all_to_all | solution.py:58
  352.3 3.7 unpack.1
  361.5 5.8 %finish.1 = (bf16[1024,1152]{1,0:T(8,128)(2,1)}, f32[256,1024]{1,0:T(8,128)}) custom-call(s32[2]{0:T(128)} %pad_add_fusion.refs_0_, f32[256,1024]{1,0:T(8,128)} %get-tuple-element.101.refs_1_, f32[256,1024]{1,0:T(8,128)} %copy-done.6, f32[256,128]{1,0:T(8,128)} %broadcast_select_fusion.refs_2_.refs_3_, f32[256,128]{1,0:T(8,128)} %get-tuple-element.102.refs_4_, ...), custom_call_target="tpu_custom_call" | custom-call | flops 4400000000 | bytes 65536 | tf_op jit(solution)/shard_map/finish/pallas_call | solution.py:179
  367.3 4.8 %all-to-all-start.10 = ((bf16[128,8,1152]{2,1,0:T(8,128)(2,1)}), bf16[128,8,1152]{2,1,0:T(8,128)(2,1)}, u32[]{:S(2)}, u32[]{:S(2)}) async-start(bf16[128,8,1152]{2,1,0:T(8,128)(2,1)} %bitcast.263), calls=%async_computation.10 | async-start | bytes 4718592 | tf_op jit(solution)/shard_map/all_to_all | solution.py:58
  385.5 22.6 %all-to-all-done.10.refs_1_.refs_2_.refs_3_.refs_4_ = bf16[128,8,1152]{2,1,0:T(8,128)(2,1)} async-done(((bf16[128,8,1152]{2,1,0:T(8,128)(2,1)}), bf16[128,8,1152]{2,1,0:T(8,128)(2,1)}, u32[]{:S(2)}, u32[]{:S(2)}) %all-to-all-start.10) | async-done | bytes 2359328 | tf_op jit(solution)/shard_map/all_to_all | solution.py:58
  408.0 3.4 final.1
  (287 shorter events, 100.3 us)
Async XLA Ops:
  7.2 5.9 %collective-permute-start.1 = (bf16[8,1024]{1,0:T(8,128)(2,1)}, bf16[8,1024]{1,0:T(8,128)(2,1)S(1)}, u32[]{:S(2)}, u32[]{:S(2)}) collective-permute-start(bf16[8,1024]{1,0:T(8,128)(2,1)} %param.29), channel_id=1, source_target_pairs={{0,1},{1,0},{2,3},{3,2},{4,5},{5,4},{6,7},{7,6},{8,9},{9,8},{10,11... | collective-permute-start | bytes 49160 | tf_op jit(solution)/shard_map/ppermute | solution.py:42
  8.7 4.4 %collective-permute-start.2 = (bf16[8,1024]{1,0:T(8,128)(2,1)}, bf16[8,1024]{1,0:T(8,128)(2,1)S(1)}, u32[]{:S(2)}, u32[]{:S(2)}) collective-permute-start(bf16[8,1024]{1,0:T(8,128)(2,1)} %param.29), channel_id=1, source_target_pairs={{0,2},{1,3},{2,0},{3,1},{4,6},{5,7},{6,4},{7,5},{8,10},{9,11},{10,... | collective-permute-start | bytes 49160 | tf_op jit(solution)/shard_map/ppermute | solution.py:42
  10.0 3.4 collective-permute-start.3
  13.4 43.6 %all-to-all-start = ((bf16[128,8,1152]{2,1,0:T(8,128)(2,1)}), bf16[128,8,1152]{2,1,0:T(8,128)(2,1)S(1)}, u32[]{:S(2)}, u32[]{:S(2)}) async-start(bf16[128,8,1152]{2,1,0:T(8,128)(2,1)} %weights.1), calls=%async_computation | async-start | bytes 4718592 | tf_op jit(solution)/shard_map/all_to_all | solution.py:58
  23.5 98.8 %all-gather.2.cloned.1.call-start = ((), (), s32[]{:S(2)}) async-start(), calls=%async_computation.13 | async-start | bytes 2162688 | tf_op jit(solution)/shard_map/all_gather | solution.py:683
  23.5 4.2 %collective-permute-start = (bf16[128,1024]{1,0:T(8,128)(2,1)S(1)}, bf16[128,1024]{1,0:T(8,128)(2,1)S(1)}, u32[]{:S(2)}, u32[]{:S(2)}) collective-permute-start(bf16[128,1024]{1,0:T(8,128)(2,1)S(1)} %bitcast.265), channel_id=1, source_target_pairs={{0,1},{1,0},{2,3},{3,2},{4,5},{5,4},{6,7},{7,6},{8,9},{9,8},{10,11... | collective-permute-start | bytes 786440 | tf_op jit(solution)/shard_map/ppermute | solution.py:42
  66.7 24.0 %all-to-all-start.1 = ((bf16[32,160,128]{2,1,0:T(8,128)(2,1)}), bf16[32,160,128]{2,1,0:T(8,128)(2,1)S(1)}, u32[]{:S(2)}, u32[]{:S(2)}) async-start(bf16[32,160,128]{2,1,0:T(8,128)(2,1)} %pack.1), calls=%async_computation.1 | async-start | bytes 2621440 | tf_op jit(solution)/shard_map/all_to_all | solution.py:58
  100.8 17.1 %all-to-all-start.2 = ((bf16[32,32,128]{2,1,0:T(8,128)(2,1)}), bf16[32,32,128]{2,1,0:T(8,128)(2,1)S(1)}, u32[]{:S(2)}, u32[]{:S(2)}) async-start(bf16[32,32,128]{2,1,0:T(8,128)(2,1)} %get-tuple-element.72.mixed), calls=%async_computation.2 | async-start | bytes 524288 | tf_op jit(solution)/shard_map/all_to_all | solution.py:58
  109.0 14.8 %collective-permute-start.14 = (bf16[128,1024]{1,0:T(8,128)(2,1)}, bf16[128,1024]{1,0:T(8,128)(2,1)S(1)}, u32[]{:S(2)}, u32[]{:S(2)}) collective-permute-start(bf16[128,1024]{1,0:T(8,128)(2,1)} %bitcast.20), channel_id=1, source_target_pairs={{0,2},{1,3},{2,0},{3,1},{4,6},{5,7},{6,4},{7,5},{8,10},{9,11},{10,... | collective-permute-start | bytes 786440 | tf_op jit(solution)/shard_map/ppermute | solution.py:42
  109.1 30.5 %collective-permute-start.13 = (bf16[128,1024]{1,0:T(8,128)(2,1)}, bf16[128,1024]{1,0:T(8,128)(2,1)}, u32[]{:S(2)}, u32[]{:S(2)}) collective-permute-start(bf16[128,1024]{1,0:T(8,128)(2,1)} %bitcast.20), channel_id=1, source_target_pairs={{0,1},{1,0},{2,3},{3,2},{4,5},{5,4},{6,7},{7,6},{8,9},{9,8},{10,11... | collective-permute-start | bytes 786440 | tf_op jit(solution)/shard_map/ppermute | solution.py:42
  110.7 29.3 %collective-permute-start.11 = (bf16[256,512]{1,0:T(8,128)(2,1)}, bf16[256,512]{1,0:T(8,128)(2,1)}, u32[]{:S(2)}, u32[]{:S(2)}) collective-permute-start(bf16[256,512]{1,0:T(8,128)(2,1)} %bitcast.19), channel_id=1, source_target_pairs={{0,2},{1,3},{2,0},{3,1},{4,6},{5,7},{6,4},{7,5},{8,10},{9,11},{10,... | collective-permute-start | bytes 786440 | tf_op jit(solution)/shard_map/ppermute | solution.py:42
  112.3 29.4 %collective-permute-start.10 = (bf16[256,512]{1,0:T(8,128)(2,1)}, bf16[256,512]{1,0:T(8,128)(2,1)}, u32[]{:S(2)}, u32[]{:S(2)}) collective-permute-start(bf16[256,512]{1,0:T(8,128)(2,1)} %bitcast.19), channel_id=1, source_target_pairs={{0,1},{1,0},{2,3},{3,2},{4,5},{5,4},{6,7},{7,6},{8,9},{9,8},{10,11... | collective-permute-start | bytes 786440 | tf_op jit(solution)/shard_map/ppermute | solution.py:42
  118.6 5.3 %collective-permute-start.6 = (bf16[128,512]{1,0:T(8,128)(2,1)S(1)}, bf16[128,512]{1,0:T(8,128)(2,1)S(1)}, u32[]{:S(2)}, u32[]{:S(2)}) collective-permute-start(bf16[128,512]{1,0:T(8,128)(2,1)S(1)} %get-tuple-element.153), channel_id=1, source_target_pairs={{0,1},{1,0},{2,3},{3,2},{4,5},{5,4},{6,7},{7,6},{8,9},{9,8},{10,11... | collective-permute-start | bytes 393224 | tf_op jit(solution)/shard_map/ppermute | solution.py:42
  123.8 16.3 %collective-permute-start.8 = (bf16[256,512]{1,0:T(8,128)(2,1)}, bf16[256,512]{1,0:T(8,128)(2,1)}, u32[]{:S(2)}, u32[]{:S(2)}) collective-permute-start(bf16[256,512]{1,0:T(8,128)(2,1)} %bitcast.18), channel_id=1, source_target_pairs={{0,2},{1,3},{2,0},{3,1},{4,6},{5,7},{6,4},{7,5},{8,10},{9,11},{10,... | collective-permute-start | bytes 786440 | tf_op jit(solution)/shard_map/ppermute | solution.py:42
  123.9 16.5 %collective-permute-start.15 = (bf16[128,1024]{1,0:T(8,128)(2,1)S(1)}, bf16[128,1024]{1,0:T(8,128)(2,1)S(1)}, u32[]{:S(2)}, u32[]{:S(2)}) collective-permute-start(bf16[128,1024]{1,0:T(8,128)(2,1)S(1)} %collective-permute-done.14), channel_id=1, source_target_pairs={{0,1},{1,0},{2,3},{3,2},{4,5},{5,4},{6,7},{7,6},{8,9},{9,8},{10,11... | collective-permute-start | bytes 786440 | tf_op jit(solution)/shard_map/ppermute | solution.py:42
  127.8 35.0 %all-to-all-start.3 = ((bf16[32,32,1024]{2,1,0:T(8,128)(2,1)}), bf16[32,32,1024]{2,1,0:T(8,128)(2,1)}, u32[]{:S(2)}, u32[]{:S(2)}) async-start(bf16[32,32,1024]{2,1,0:T(8,128)(2,1)} %bitcast.257), calls=%async_computation.3 | async-start | bytes 4194304 | tf_op jit(solution)/shard_map/all_to_all | solution.py:58
  139.6 3.5 collective-permute-start.7
  140.1 3.0 collective-permute-start.9
  162.8 35.4 %all-to-all-start.4 = ((bf16[32,32,1024]{2,1,0:T(8,128)(2,1)}), bf16[32,32,1024]{2,1,0:T(8,128)(2,1)}, u32[]{:S(2)}, u32[]{:S(2)}) async-start(bf16[32,32,1024]{2,1,0:T(8,128)(2,1)} %bitcast.256), calls=%async_computation.4 | async-start | bytes 4194304 | tf_op jit(solution)/shard_map/all_to_all | solution.py:58
  174.1 40.5 %collective-permute-start.16 = (bf16[128,1024]{1,0:T(8,128)(2,1)}, bf16[128,1024]{1,0:T(8,128)(2,1)}, u32[]{:S(2)}, u32[]{:S(2)}) collective-permute-start(bf16[128,1024]{1,0:T(8,128)(2,1)} %pad_maximum_fusion.9), channel_id=1, source_target_pairs={{0,1},{1,0},{2,3},{3,2},{4,5},{5,4},{6,7},{7,6},{8,9},{9,8},{10,11... | collective-permute-start | bytes 786440 | tf_op jit(solution)/shard_map/ppermute | solution.py:42
  198.2 34.6 %all-to-all-start.5 = ((bf16[32,32,1024]{2,1,0:T(8,128)(2,1)}), bf16[32,32,1024]{2,1,0:T(8,128)(2,1)}, u32[]{:S(2)}, u32[]{:S(2)}) async-start(bf16[32,32,1024]{2,1,0:T(8,128)(2,1)} %bitcast.268), calls=%async_computation.5 | async-start | bytes 4194304 | tf_op jit(solution)/shard_map/all_to_all | solution.py:58
  232.8 34.9 %all-to-all-start.6 = ((bf16[32,32,1024]{2,1,0:T(8,128)(2,1)}), bf16[32,32,1024]{2,1,0:T(8,128)(2,1)}, u32[]{:S(2)}, u32[]{:S(2)}) async-start(bf16[32,32,1024]{2,1,0:T(8,128)(2,1)} %bitcast.258), calls=%async_computation.6 | async-start | bytes 4194304 | tf_op jit(solution)/shard_map/all_to_all | solution.py:58
  240.8 140.7 %reduce-scatter.3.cloned.1.call-start = ((), (), s32[]{:S(2)}) async-start(), calls=%async_computation.14 | async-start | bytes 2621440 | tf_op jit(solution)/shard_map/reduce_scatter | solution.py:831
  270.9 3.4 collective-permute-start.18
  273.5 8.1 %collective-permute-start.17 = (bf16[128,512]{1,0:T(8,128)(2,1)S(1)}, bf16[128,512]{1,0:T(8,128)(2,1)S(1)}, u32[]{:S(2)}, u32[]{:S(2)}) collective-permute-start(bf16[128,512]{1,0:T(8,128)(2,1)S(1)} %get-tuple-element.147), channel_id=1, source_target_pairs={{0,1},{1,0},{2,3},{3,2},{4,5},{5,4},{6,7},{7,6},{8,9},{9,8},{10,11... | collective-permute-start | bytes 393224 | tf_op jit(solution)/shard_map/ppermute | solution.py:42
  275.1 18.3 %all-to-all-start.7 = ((bf16[32,32,128]{2,1,0:T(8,128)(2,1)}), bf16[32,32,128]{2,1,0:T(8,128)(2,1)S(1)}, u32[]{:S(2)}, u32[]{:S(2)}) async-start(bf16[32,32,128]{2,1,0:T(8,128)(2,1)} %heads_out.1), calls=%async_computation.7 | async-start | bytes 524288 | tf_op jit(solution)/shard_map/all_to_all | solution.py:58
  294.1 28.8 %all-to-all-start.8 = ((bf16[128,8,640]{2,1,0:T(8,128)(2,1)}), bf16[128,8,640]{2,1,0:T(8,128)(2,1)S(1)}, u32[]{:S(2)}, u32[]{:S(2)}) async-start(bf16[128,8,640]{2,1,0:T(8,128)(2,1)} %bitcast.95), calls=%async_computation.8 | async-start | bytes 2621440 | tf_op jit(solution)/shard_map/all_to_all | solution.py:58
  322.8 29.5 %all-to-all-start.9 = ((bf16[32,160,128]{2,1,0:T(8,128)(2,1)}), bf16[32,160,128]{2,1,0:T(8,128)(2,1)}, u32[]{:S(2)}, u32[]{:S(2)}) async-start(bf16[32,160,128]{2,1,0:T(8,128)(2,1)} %attend_back.1), calls=%async_computation.9 | async-start | bytes 2621440 | tf_op jit(solution)/shard_map/all_to_all | solution.py:58
  333.1 50.6 %reduce-scatter.5.cloned.1.call-start = ((), (), s32[]{:S(2)}) async-start(), calls=%async_computation.15 | async-start | bytes 1310720 | tf_op jit(solution)/shard_map/reduce_scatter | solution.py:890
  356.0 4.9 %collective-permute-start.19 = (f32[256,128]{1,0:T(8,128)}, f32[256,128]{1,0:T(8,128)S(1)}, u32[]{:S(2)}, u32[]{:S(2)}) collective-permute-start(f32[256,128]{1,0:T(8,128)} %get-tuple-element.102.refs_4_), channel_id=1, source_target_pairs={{0,1},{1,0},{2,3},{3,2},{4,5},{5,4},{6,7},{7,6},{8,9},{9,8},{10,11... | collective-permute-start | bytes 393224 | tf_op jit(solution)/shard_map/ppermute | solution.py:42
  367.3 40.7 %all-to-all-start.10 = ((bf16[128,8,1152]{2,1,0:T(8,128)(2,1)}), bf16[128,8,1152]{2,1,0:T(8,128)(2,1)}, u32[]{:S(2)}, u32[]{:S(2)}) async-start(bf16[128,8,1152]{2,1,0:T(8,128)(2,1)} %bitcast.263), calls=%async_computation.10 | async-start | bytes 4718592 | tf_op jit(solution)/shard_map/all_to_all | solution.py:58
  377.4 2.8 collective-permute-start.20
  (55 other events, 641.0 us)
Sparse Core Ops, SparseCore 0:
  28.0 90.9 all-gather.1
  274.2 30.0 reduce-scatter.2
  361.0 19.3 reduce-scatter.4
